TPU v7x, 32 devices: a whole 2x2x4 slice. The times are simulated.
32 devices in a mesh: ctx: 8 (over z, y), seq: 2 (over x), wsh: 2 (over core).
Axes of the slice: x: 2, y: 2, z: 4, core: 2. Of those that a mesh axis runs over, the one named last changes fastest.
Arguments:
- tokens: bfloat16 [4, 1024, 1024], P(('seq', 'wsh'), 'ctx'), may hold values from -6 to 6
- positions: int32 [4, 1024], P(('seq', 'wsh'), 'ctx'), may hold values from 0 to 895, as said below
- w_qkv: bfloat16 [1024, 3072], P(('seq', 'wsh')), may hold values from -0.1875 to 0.1875
- w_out: bfloat16 [1024, 1024], P(('seq', 'wsh')), may hold values from -3.5 to 3.5
- w_in: bfloat16 [1024, 5248], P(('seq', 'wsh')), may hold values from -0.1875 to 0.1875
- w_down: bfloat16 [2624, 1024], P(('seq', 'wsh')), may hold values from -0.125 to 0.125
- gain_attn: bfloat16 [1024], P(('seq', 'wsh')), may hold values from 0.099609375 to 1.8984375
- gain_mlp: bfloat16 [1024], P(('seq', 'wsh')), may hold values from 0.099609375 to 1.8984375
- cotangent: bfloat16 [4, 1024, 1024], P(('seq', 'wsh'), 'ctx'), may hold values from -6 to 6
Outputs:
- output: bfloat16 [4, 1024, 1024], P(('seq', 'wsh'), 'ctx')
- grad_tokens: bfloat16 [4, 1024, 1024], P(('seq', 'wsh'), 'ctx')
- grad_w_qkv: float32 [1024, 3072], P(('seq', 'wsh'))
- grad_w_out: float32 [1024, 1024], P(('seq', 'wsh'))
- grad_w_in: float32 [1024, 5248], P(('seq', 'wsh'))
- down_weight_gradient: float32 [2624, 1024], P(('seq', 'wsh'))
- grad_gain_attn: float32 [1024], P(('seq', 'wsh'))
- grad_gain_mlp: float32 [1024], P(('seq', 'wsh'))
Inputs may be any that keep to these rules, and one draw needn't show every extreme that they name: Each sequence is a run of packed documents: positions count 0, 1, 2 and so on from the first token of each document. Every sequence holds one document of exactly 1024 - 128 tokens, which begins after the sequence's first token and within its first 128 tokens; the tokens before and after it form one or more shorter documents.
All inputs are finite; a program needn't handle non-finite values.
Results may differ from a plain program's by a relative error of at most 0.02.
Values may be sent and summed in bfloat16 or wider, within the bound.
A program may use at most 192 MiB of HBM per device.

v0:
```python
import math

import jax
import jax.numpy as jnp
from jax import lax
from jax.sharding import PartitionSpec as P

D = 1024
HEADS = 16
HEAD = 64
FF = 2624


layer_eps = 1e-05
rope_base = 160000.0
far_below = -1e30


def from_behind(shard, axis, by):
    size = lax.axis_size(axis)
    return lax.ppermute(shard, axis, [(i, (i + by) % size) for i in range(size)])


def normalize(values, gain_vector):
    middle = jnp.mean(values, -1, keepdims=True)
    centred = values - middle
    spread = jnp.mean(centred * centred, -1, keepdims=True)
    return centred * lax.rsqrt(spread + layer_eps) * gain_vector


def rotary_tables(positions):
    half_size = HEAD // 2
    frequency = jnp.exp(
        jnp.arange(half_size, dtype=jnp.float32) * (-2.0 * math.log(rope_base) / HEAD)
    )
    angles = positions.astype(jnp.float32)[..., None] * frequency
    cosine = jnp.cos(angles)
    sine_table = jnp.sin(angles)
    return (
        jnp.concatenate([cosine, cosine], -1)[..., None, :],
        jnp.concatenate([sine_table, sine_table], -1)[..., None, :],
    )


def rotate(values, cosine, sine_table):
    half_size = values.shape[-1] // 2
    turned = jnp.concatenate([-values[..., half_size:], values[..., :half_size]], -1)
    return values * cosine + turned * sine_table


def rotate_back(grads, cosine, sine_table):
    half_size = grads.shape[-1] // 2
    shifted = grads * sine_table
    return grads * cosine + jnp.concatenate(
        [shifted[..., half_size:], -shifted[..., :half_size]], -1
    )


def geglu(inner_part, gate_part):
    return jax.nn.gelu(inner_part, approximate=False) * gate_part


def same_document(query_starts, key_starts):
    return (query_starts[:, :, None] == key_starts[:, None, :])[:, :, None, :]


def fold_keys(queries, query_starts, scaling, running, piece):
    key_piece, value_piece, start_piece = piece
    seq_count = key_piece.shape[0]
    row_total = key_piece.shape[1]
    block_size = math.gcd(row_total, 512)

    def one_block(block_index, carried):
        best_score, totals, weighted = carried
        key_block = lax.dynamic_slice_in_dim(
            key_piece, block_index * block_size, block_size, 1
        ).reshape(seq_count, block_size, HEADS, HEAD)
        value_block = lax.dynamic_slice_in_dim(
            value_piece, block_index * block_size, block_size, 1
        ).reshape(seq_count, block_size, HEADS, HEAD)
        start_block = lax.dynamic_slice_in_dim(start_piece, block_index * block_size, block_size, 1)
        same_doc = same_document(query_starts, start_block)
        scores = (
            jnp.einsum("sqhd,skhd->sqhk", queries, key_block, preferred_element_type=jnp.float32)
            * scaling
        )
        scores = jnp.where(same_doc, scores, far_below)
        new_best = jnp.maximum(best_score, jnp.max(scores, -1))
        fading = jnp.exp(best_score - new_best)
        raised = jnp.where(same_doc, jnp.exp(scores - new_best[..., None]), 0.0)
        totals = totals * fading + jnp.sum(raised, -1)
        weighted = weighted * fading[..., None] + jnp.einsum(
            "sqhk,skhd->sqhd",
            raised.astype(jnp.bfloat16),
            value_block,
            preferred_element_type=jnp.float32,
        )
        return (new_best, totals, weighted)

    return lax.fori_loop(0, row_total // block_size, one_block, running)


def block_grads(
    queries,
    query_starts,
    key_block,
    value_block,
    key_starts,
    grad_split,
    log_total,
    row_dot,
    scaling,
):
    same_doc = same_document(query_starts, key_starts)
    scores = (
        jnp.einsum("sqhd,skhd->sqhk", queries, key_block, preferred_element_type=jnp.float32)
        * scaling
    )
    weights_f = jnp.where(same_doc, jnp.exp(scores - log_total[..., None]), 0.0)
    grad_weights = jnp.einsum(
        "sqhd,skhd->sqhk", grad_split, value_block, preferred_element_type=jnp.float32
    )
    grad_scores = (weights_f * (grad_weights - row_dot[..., None])).astype(jnp.bfloat16)
    grad_query = (
        jnp.einsum("sqhk,skhd->sqhd", grad_scores, key_block, preferred_element_type=jnp.float32)
        * scaling
    )
    grad_key = (
        jnp.einsum("sqhk,sqhd->skhd", grad_scores, queries, preferred_element_type=jnp.float32)
        * scaling
    )
    grad_value = jnp.einsum(
        "sqhk,sqhd->skhd",
        weights_f.astype(jnp.bfloat16),
        grad_split,
        preferred_element_type=jnp.float32,
    )
    return (grad_query, grad_key, grad_value)


def local(tokens, positions, w_qkv, w_out, w_in, w_down, gain_attn, gain_mlp, cotangent):
    seq_count = tokens.shape[0]
    row_count = tokens.shape[1]
    scaling = HEAD ** (-0.5)
    split_shape = (seq_count, row_count, HEADS, HEAD)
    flat_shape = (seq_count, row_count, D)
    (
        forward_query_weight,
        forward_out_weight,
        forward_in_weight,
        forward_down_weight,
        full_ga,
        full_gm,
    ) = (
        lax.all_gather(w_qkv, ("seq", "wsh"), axis=0, tiled=True),
        lax.all_gather(w_out, ("seq", "wsh"), axis=0, tiled=True),
        lax.all_gather(w_in, ("seq", "wsh"), axis=0, tiled=True),
        lax.all_gather(w_down, ("seq", "wsh"), axis=0, tiled=True),
        lax.all_gather(gain_attn, ("seq", "wsh"), axis=0, tiled=True),
        lax.all_gather(gain_mlp, ("seq", "wsh"), axis=0, tiled=True),
    )
    cosine, sine_table = rotary_tables(positions)
    token_index = lax.axis_index("ctx") * row_count + jnp.arange(row_count, dtype=jnp.int32)
    own_starts = token_index[None, :] - positions
    input_widened = tokens.astype(jnp.float32)
    gain_one = full_ga.astype(jnp.float32)
    gain_two = full_gm.astype(jnp.float32)
    attention_normed = normalize(input_widened, gain_one).astype(jnp.bfloat16)
    projected_output = jnp.einsum(
        "kch,hf->kcf", attention_normed, forward_query_weight, preferred_element_type=jnp.float32
    )
    queries = rotate(projected_output[..., :D].reshape(split_shape), cosine, sine_table).astype(
        jnp.bfloat16
    )
    key_rows = (
        rotate(projected_output[..., D : 2 * D].reshape(split_shape), cosine, sine_table)
        .astype(jnp.bfloat16)
        .reshape(flat_shape)
    )
    value_rows = projected_output[..., 2 * D :].astype(jnp.bfloat16)
    start_state = (
        jnp.full((seq_count, row_count, HEADS), far_below, jnp.float32),
        jnp.zeros((seq_count, row_count, HEADS), jnp.float32),
        jnp.zeros(split_shape, jnp.float32),
    )
    best_score, totals, weighted = fold_keys(
        queries,
        own_starts,
        scaling,
        start_state,
        (
            lax.all_gather(key_rows, "ctx", axis=1, tiled=True),
            lax.all_gather(value_rows, "ctx", axis=1, tiled=True),
            lax.all_gather(own_starts, "ctx", axis=1, tiled=True),
        ),
    )
    attended = weighted / totals[..., None]
    log_total = best_score + jnp.log(totals)
    attended_reduced = attended.reshape(flat_shape).astype(jnp.bfloat16)
    mixed_token_rows = input_widened + jnp.einsum(
        "kch,hf->kcf", attended_reduced, forward_out_weight, preferred_element_type=jnp.float32
    )
    feedforward_normed = normalize(mixed_token_rows, gain_two).astype(jnp.bfloat16)
    hidden_state = jnp.einsum(
        "rnk,kx->rnx", feedforward_normed, forward_in_weight, preferred_element_type=jnp.float32
    )
    inner_part = hidden_state[..., :FF]
    gate_part = hidden_state[..., FF:]
    gated_product = geglu(inner_part, gate_part).astype(jnp.bfloat16)
    output = (
        mixed_token_rows
        + jnp.einsum(
            "ogw,wn->ogn", gated_product, forward_down_weight, preferred_element_type=jnp.float32
        )
    ).astype(jnp.bfloat16)
    backward_query_weight, backward_out_weight, backward_in_weight, backward_down_weight = (
        forward_query_weight,
        forward_out_weight,
        forward_in_weight,
        forward_down_weight,
    )
    down_weight_gradient = jnp.einsum(
        "xvt,xvw->tw", gated_product, cotangent, preferred_element_type=jnp.float32
    )
    grad_product = jnp.einsum(
        "xzi,mi->xzm", cotangent, backward_down_weight, preferred_element_type=jnp.float32
    )
    geglu_pull = jax.vjp(geglu, inner_part, gate_part)[1]
    grad_inner, grad_gate = geglu_pull(grad_product)
    hidden_gradient = jnp.concatenate([grad_inner, grad_gate], -1).astype(jnp.bfloat16)
    grad_w_in = jnp.einsum(
        "hrq,hrw->qw", feedforward_normed, hidden_gradient, preferred_element_type=jnp.float32
    )
    grad_normed_mlp = jnp.einsum(
        "xcu,au->xca", hidden_gradient, backward_in_weight, preferred_element_type=jnp.float32
    )
    mlp_pull = jax.vjp(normalize, mixed_token_rows, gain_two)[1]
    grad_mixed_norm, grad_gain_mlp = mlp_pull(grad_normed_mlp)
    grad_mixed = cotangent.astype(jnp.float32) + grad_mixed_norm
    branch_gradient = grad_mixed.astype(jnp.bfloat16)
    grad_w_out = jnp.einsum(
        "pgj,pgv->jv", attended_reduced, branch_gradient, preferred_element_type=jnp.float32
    )
    grad_attended = jnp.einsum(
        "arq,xq->arx", branch_gradient, backward_out_weight, preferred_element_type=jnp.float32
    ).astype(jnp.bfloat16)
    grad_split = grad_attended.reshape(split_shape)
    row_dot = jnp.sum(grad_split.astype(jnp.float32) * attended, -1)
    cycle_turns = lax.axis_size("ctx") - 1
    zeros_flat = jnp.zeros(flat_shape, jnp.float32)

    def key_turn(turn_index, carried):
        moving_keys, moving_values, moving_starts, grad_keys, grad_values, grad_queries = carried
        grad_query, grad_key, grad_value = block_grads(
            queries,
            own_starts,
            moving_keys.reshape(split_shape),
            moving_values.reshape(split_shape),
            moving_starts,
            grad_split,
            log_total,
            row_dot,
            scaling,
        )
        moving_keys, moving_values, moving_starts = from_behind(
            (moving_keys, moving_values, moving_starts), "ctx", 1
        )
        grad_keys, grad_values = (
            from_behind(
                (grad_keys + grad_key.reshape(flat_shape)).astype(jnp.bfloat16), "ctx", 1
            ).astype(jnp.float32),
            from_behind(
                (grad_values + grad_value.reshape(flat_shape)).astype(jnp.bfloat16), "ctx", 1
            ).astype(jnp.float32),
        )
        return (
            moving_keys,
            moving_values,
            moving_starts,
            grad_keys,
            grad_values,
            grad_queries + grad_query,
        )

    moving_keys, moving_values, moving_starts, grad_keys, grad_values, grad_queries = lax.fori_loop(
        0,
        cycle_turns,
        key_turn,
        (
            key_rows,
            value_rows,
            own_starts,
            zeros_flat,
            zeros_flat,
            jnp.zeros(split_shape, jnp.float32),
        ),
    )
    grad_query, grad_key, grad_value = block_grads(
        queries,
        own_starts,
        moving_keys.reshape(split_shape),
        moving_values.reshape(split_shape),
        moving_starts,
        grad_split,
        log_total,
        row_dot,
        scaling,
    )
    grad_queries = grad_queries + grad_query
    grad_keys, grad_values = (
        from_behind(
            (grad_keys + grad_key.reshape(flat_shape)).astype(jnp.bfloat16), "ctx", 1
        ).astype(jnp.float32),
        from_behind(
            (grad_values + grad_value.reshape(flat_shape)).astype(jnp.bfloat16), "ctx", 1
        ).astype(jnp.float32),
    )
    projected_gradient = jnp.concatenate(
        [
            rotate_back(grad_queries, cosine, sine_table).reshape(flat_shape),
            rotate_back(grad_keys.reshape(split_shape), cosine, sine_table).reshape(flat_shape),
            grad_values,
        ],
        -1,
    ).astype(jnp.bfloat16)
    grad_w_qkv = jnp.einsum(
        "pgj,pgv->jv", attention_normed, projected_gradient, preferred_element_type=jnp.float32
    )
    grad_normed_attn = jnp.einsum(
        "arq,xq->arx", projected_gradient, backward_query_weight, preferred_element_type=jnp.float32
    )
    attn_pull = jax.vjp(normalize, input_widened, gain_one)[1]
    grad_inputs_norm, grad_gain_attn = attn_pull(grad_normed_attn)
    grad_tokens = (grad_mixed + grad_inputs_norm).astype(jnp.bfloat16)
    shares = (
        lax.psum_scatter(
            grad_w_qkv.astype(jnp.bfloat16), ("seq", "wsh"), scatter_dimension=0, tiled=True
        ).astype(jnp.float32),
        lax.psum_scatter(
            grad_w_out.astype(jnp.bfloat16), ("seq", "wsh"), scatter_dimension=0, tiled=True
        ).astype(jnp.float32),
        lax.psum_scatter(
            grad_w_in.astype(jnp.bfloat16), ("seq", "wsh"), scatter_dimension=0, tiled=True
        ).astype(jnp.float32),
        lax.psum_scatter(
            down_weight_gradient.astype(jnp.bfloat16),
            ("seq", "wsh"),
            scatter_dimension=0,
            tiled=True,
        ).astype(jnp.float32),
        lax.psum_scatter(
            grad_gain_attn.astype(jnp.bfloat16), ("seq", "wsh"), scatter_dimension=0, tiled=True
        ).astype(jnp.float32),
        lax.psum_scatter(
            grad_gain_mlp.astype(jnp.bfloat16), ("seq", "wsh"), scatter_dimension=0, tiled=True
        ).astype(jnp.float32),
    )
    summed = lax.psum((shares[0], shares[1], shares[2], shares[3], shares[4], shares[5]), "ctx")
    return (output, grad_tokens, summed[0], summed[1], summed[2], summed[3], summed[4], summed[5])


def solution(mesh):
    placed = (
        P(("seq", "wsh"), "ctx", None),
        P(("seq", "wsh"), "ctx"),
        P(("seq", "wsh"), None),
        P(("seq", "wsh"), None),
        P(("seq", "wsh"), None),
        P(("seq", "wsh"), None),
        P(("seq", "wsh")),
        P(("seq", "wsh")),
        P(("seq", "wsh"), "ctx", None),
    )
    return jax.shard_map(
        local,
        mesh=mesh,
        in_specs=placed,
        out_specs=(
            P(("seq", "wsh"), "ctx", None),
            P(("seq", "wsh"), "ctx", None),
            P(("seq", "wsh"), None),
            P(("seq", "wsh"), None),
            P(("seq", "wsh"), None),
            P(("seq", "wsh"), None),
            P(("seq", "wsh")),
            P(("seq", "wsh")),
        ),
        check_vma=False,
    )
```

profile of v0, /device:TPU:8, one launch (start us, length us, event | category | flops | bytes accessed | tf_op | source)
XLA Modules:
  0.0 1155.2 jit_solution(4309394201670580769)
XLA Ops:
  8.7 5.1 all-gather
  16.2 40.9 %all-gather.9.cloned.1.call-done = bf16[1024,3072]{1,0:T(8,128)(2,1)} async-done(((bf16[256,3072]{1,0:T(8,128)(2,1)}), bf16[1024,3072]{1,0:T(8,128)(2,1)}) %all-gather.9.cloned.1.call-update) | async-done | bytes 6291472 | tf_op jit(solution)/shard_map/all_gather | solution.py:155
  57.2 3.8 convolution_bitcast_fusion.3
  62.4 1.9 fusion.107
  66.4 5.1 all-gather.1
  72.1 18.7 %all_gather.27 = s32[1,1024]{1,0:T(1,128)} all-gather(s32[1,128]{1,0:T(1,128)} %get-tuple-element.649), channel_id=1, replica_groups=mesh['ctx'=8,'seq'=2,'wsh'=2] {'ctx'}, dimensions={1}, use_global_device_ids=true | all-gather | bytes 4608 | tf_op jit(solution)/shard_map/all_gather | solution.py:194
  90.8 9.1 all-gather.19.cloned.1.call-done
  100.0 5.5 convolution_bitcast_fusion.2
  106.7 45.3 %all-gather.11.cloned.1.call-done = bf16[1,1024,1024]{2,1,0:T(8,128)(2,1)} async-done(((bf16[1,128,1024]{2,1,0:T(8,128)(2,1)}), bf16[1,1024,1024]{2,1,0:T(8,128)(2,1)}) %all-gather.11.cloned.1.call-update) | async-done | bytes 2097168 | tf_op jit(solution)/shard_map/all_gather | solution.py:192
  152.0 49.8 %all-gather.13.cloned.1.call-done = bf16[1,1024,1024]{2,1,0:T(8,128)(2,1)} async-done(((bf16[1,128,1024]{2,1,0:T(8,128)(2,1)}), bf16[1,1024,1024]{2,1,0:T(8,128)(2,1)}) %all-gather.13.cloned.1.call-update) | async-done | bytes 2097168 | tf_op jit(solution)/shard_map/all_gather | solution.py:193
  201.8 31.1 %while.39 = (s32[]{:T(128)}, f32[1,128,16]{1,2,0:T(8,128)S(1)}, f32[1,128,16]{1,2,0:T(8,128)S(1)}, f32[1,128,16,64]{1,3,2,0:T(8,128)}, s32[1,128]{1,0:T(1,128)},...) while((s32[]{:T(128)}, f32[1,128,16]{1,2,0:T(8,128)S(1)}, ...), condition=%wide.region_5.6_spmd.clone, body=%wide.region_2.5_spmd.clone.sunk | while | flops 282537984 | bytes 28973820 | solution.py:100
  205.5 3.0 fusion.167
  208.5 3.6 fusion.169
  213.2 3.6 fusion.170
  221.3 3.0 fusion.167
  224.3 3.2 fusion.169
  228.5 3.6 fusion.170
  234.1 2.6 fusion.110
  236.9 60.5 %all-gather.17.cloned.1.call-done = bf16[1024,5248]{1,0:T(8,128)(2,1)} async-done(((bf16[256,5248]{1,0:T(8,128)(2,1)}), bf16[1024,5248]{1,0:T(8,128)(2,1)}) %all-gather.17.cloned.1.call-update) | async-done | bytes 10747920 | tf_op jit(solution)/shard_map/all_gather | solution.py:157
  297.4 5.9 convolution_bitcast_fusion.1
  303.3 3.3 fusion.65
  307.6 3.7 fusion.79
  312.5 2.0 convolution_convert_fusion.3
  317.5 2.5 convolution_convert_fusion.4
  320.3 4.0 convolution_convert_fusion.1
  324.3 178.2 %while.40 = (s32[]{:T(128)}, bf16[1,128,1024]{1,2,0:T(8,128)(2,1)S(1)}, bf16[1,128,1024]{1,2,0:T(8,128)(2,1)}, s32[1,128]{1,0:T(1,128)S(1)}, f32[1,128,1024]{1,2...) while((s32[]{:T(128)}, ...), condition=%wide.region_12.13_spmd.clone, body=%wide.region_11.12_spmd.clone.sunk | while | flops 171196416 | bytes 24433068 | solution.py:285
  336.4 9.4 collective-permute-done.3
  347.6 3.1 collective-permute-done.4
  353.1 2.4 collective-permute-start.1
  358.1 2.0 fusion.183
  360.0 2.4 collective-permute-start.3
  363.9 9.2 collective-permute-done.3
  374.9 2.2 collective-permute-done.4
  379.0 2.9 collective-permute-start.1
  383.9 1.9 fusion.183
  385.8 2.9 collective-permute-start.3
  390.0 9.5 collective-permute-done.3
  404.4 2.9 collective-permute-start.1
  409.8 1.9 fusion.183
  411.7 2.4 collective-permute-start.3
  414.7 2.2 collective-permute-start.4
  417.2 7.7 collective-permute-done.3
  429.5 2.6 collective-permute-start.1
  432.2 2.5 collective-permute-start.2
  439.8 3.4 collective-permute-start.4
  443.5 6.9 collective-permute-done.3
  455.0 3.2 collective-permute-start.1
  458.2 2.5 collective-permute-start.2
  465.3 3.4 collective-permute-start.4
  469.0 6.1 collective-permute-done.3
  479.7 3.7 collective-permute-start.1
  483.4 2.5 collective-permute-start.2
  490.4 3.0 collective-permute-start.4
  493.7 5.3 collective-permute-done.3
  508.0 3.4 collective-permute-start.5
  511.7 4.9 collective-permute-done.5
  517.8 4.6 convolution_convert_fusion.2
  523.9 5.9 convolution_convert_fusion
  531.7 5.2 fusion.57
  536.9 5.7 fusion.71
  543.0 5.7 all-reduce.3
  549.8 35.4 %reduce-scatter.5.cloned.1.call-done = bf16[256,3072]{1,0:T(8,128)(2,1)} async-done(((bf16[1024,3072]{1,0:T(8,128)(2,1)}), bf16[256,3072]{1,0:T(8,128)(2,1)}) %reduce-scatter.5.cloned.1.call-update) | async-done | bytes 1572880 | tf_op jit(solution)/shard_map/reduce_scatter | solution.py:336
  585.2 89.8 %reduce-scatter.9.cloned.1.call-done = bf16[256,5248]{1,0:T(8,128)(2,1)} async-done(((bf16[1024,5248]{1,0:T(8,128)(2,1)}), bf16[256,5248]{1,0:T(8,128)(2,1)}) %reduce-scatter.9.cloned.1.call-update) | async-done | bytes 2686992 | tf_op jit(solution)/shard_map/reduce_scatter | solution.py:342
  675.0 473.3 %all-reduce.5 = (f32[256,3072]{1,0:T(8,128)}, f32[256,1024]{1,0:T(8,128)}, f32[256,5248]{1,0:T(8,128)}, f32[656,1024]{1,0:T(8,128)}, f32[256]{0:T(256)}, /*index=5*/f32[256]{0:T(256)}) all-reduce(bf16[256,3072]{1,0:T(8,128)(2,1)} %reduce-scatter.5.cloned.1.call-done, ...), channel_id=1, replica_groups=mesh['ctx'=8,'seq'=2,'wsh'=2] {'ctx'}, use_global_device_ids=true, to_apply=%region_16.17 | all-reduce | flops 3064320 | bytes 18386944 | tf_op jit(solution)/shard_map/psum | solution.py:358
  (385 shorter events, 105.3 us)
Async XLA Ops:
  7.2 50.0 %all-gather.9.cloned.1.call-start = ((), (), s32[]{:S(2)}) async-start(), calls=%async_computation.4 | async-start | bytes 7864320 | tf_op jit(solution)/shard_map/all_gather | solution.py:155
  7.9 92.0 %all-gather.19.cloned.1.call-start = ((), (), s32[]{:S(2)}) async-start(), calls=%async_computation.9 | async-start | bytes 6717440 | tf_op jit(solution)/shard_map/all_gather | solution.py:158
  8.7 143.3 %all-gather.11.cloned.1.call-start = ((), (), s32[]{:S(2)}) async-start(), calls=%async_computation.5 | async-start | bytes 2359296 | tf_op jit(solution)/shard_map/all_gather | solution.py:192
  13.8 43.3 %copy-start.33 = (f32[4,1,256]{2,1,0:T(1,128)}, f32[4,1,256]{2,1,0:T(1,128)S(1)}, u32[]{:S(2)}) copy-start(f32[4,1,256]{2,1,0:T(1,128)S(1)} %convert_element_type.206) | copy-start | bytes 12292
  16.0 45.1 %copy-start.40 = (f32[128]{0:T(128)}, f32[128]{0:T(128)S(1)}, u32[]{:S(2)}) copy-start(f32[128]{0:T(128)S(1)} %broadcast_multiply_fusion.3) | copy-start | bytes 1540
  16.2 44.8 %copy-start.42 = (f32[128]{0:T(128)}, f32[128]{0:T(128)S(1)}, u32[]{:S(2)}) copy-start(f32[128]{0:T(128)S(1)} %fusion.70) | copy-start | bytes 1540
  16.2 44.8 %copy-start.38 = (f32[128]{0:T(128)}, f32[128]{0:T(128)S(1)}, u32[]{:S(2)}) copy-start(f32[128]{0:T(128)S(1)} %fusion.93) | copy-start | bytes 1540
  64.3 137.4 %all-gather.13.cloned.1.call-start = ((), (), s32[]{:S(2)}) async-start(), calls=%async_computation.6 | async-start | bytes 2359296 | tf_op jit(solution)/shard_map/all_gather | solution.py:193
  65.2 168.9 %all-gather.15.cloned.1.call-start = ((), (), s32[]{:S(2)}) async-start(), calls=%async_computation.7 | async-start | bytes 2621440 | tf_op jit(solution)/shard_map/all_gather | solution.py:156
  65.8 34.2 %copy-start.17 = (bf16[1,128,1024]{2,1,0:T(8,128)(2,1)S(1)}, bf16[1,128,1024]{2,1,0:T(8,128)(2,1)}, u32[]{:S(2)}) copy-start(bf16[1,128,1024]{2,1,0:T(8,128)(2,1)} %param.21) | copy-start | bytes 786436
  65.8 231.7 %all-gather.17.cloned.1.call-start = ((), (), s32[]{:S(2)}) async-start(), calls=%async_computation.8 | async-start | bytes 13434880 | tf_op jit(solution)/shard_map/all_gather | solution.py:157
  66.3 483.4 %reduce-scatter.7.cloned.1.call-start = ((), (), s32[]{:S(2)}) async-start(), calls=%async_computation.11 | async-start | bytes 2621440 | tf_op jit(solution)/shard_map/reduce_scatter | solution.py:339
  234.1 63.3 %copy-start.35 = (f32[4,1,256]{2,1,0:T(1,128)S(1)}, f32[4,1,256]{2,1,0:T(1,128)}, u32[]{:S(2)}) copy-start(f32[4,1,256]{2,1,0:T(1,128)} %convert_element_type.207) | copy-start | bytes 12292
  236.7 74.6 %copy-start = (f32[1,128,1024]{2,1,0:T(8,128)}, f32[1,128,1024]{2,1,0:T(8,128)S(1)}, u32[]{:S(2)}) copy-start(f32[1,128,1024]{2,1,0:T(8,128)S(1)} %get-tuple-element.457) | copy-start | bytes 1572868
  297.4 10.2 slice-start
  297.4 10.2 slice-start.1
  307.2 13.0 %copy-start.11 = (bf16[128,2624]{1,0:T(8,128)(2,1)}, bf16[128,2624]{1,0:T(8,128)(2,1)S(1)}, u32[]{:S(2)}) copy-start(bf16[128,2624]{1,0:T(8,128)(2,1)S(1)} %get-tuple-element.437) | copy-start | bytes 2015236
  314.6 235.2 %reduce-scatter.11.cloned.1.call-start = ((), (), s32[]{:S(2)}) async-start(), calls=%async_computation.13 | async-start | bytes 6717440 | tf_op jit(solution)/shard_map/reduce_scatter | solution.py:345
  324.3 260.9 %reduce-scatter.5.cloned.1.call-start = ((), (), s32[]{:S(2)}) async-start(), calls=%async_computation.10 | async-start | bytes 7864320 | tf_op jit(solution)/shard_map/reduce_scatter | solution.py:336
  324.4 27.1 %collective-permute-start = (bf16[1,128,1024]{1,2,0:T(8,128)(2,1)S(1)}, bf16[1,128,1024]{1,2,0:T(8,128)(2,1)S(1)}, u32[]{:S(2)}, u32[]{:S(2)}) collective-permute-start(bf16[1,128,1024]{1,2,0:T(8,128)(2,1)S(1)} %copy.120), channel_id=1, source_target_pairs={{0,4},{4,8},{8,12},{12,16},{16,20},{20,24},{24,28},{28,0},{1,5},{5... | collective-permute-start | bytes 786440 | tf_op jit(solution)/shard_map/while/body/eval_jaxpr/ppermute | solution.py:21
  326.9 24.7 %collective-permute-start.1 = (bf16[1,128,1024]{1,2,0:T(8,128)(2,1)S(1)}, bf16[1,128,1024]{1,2,0:T(8,128)(2,1)}, u32[]{:S(2)}, u32[]{:S(2)}) collective-permute-start(bf16[1,128,1024]{1,2,0:T(8,128)(2,1)S(1)} %copy.121), channel_id=1, source_target_pairs={{0,4},{4,8},{8,12},{12,16},{16,20},{20,24},{24,28},{28,0},{1,5},{5... | collective-permute-start | bytes 786440 | tf_op jit(solution)/shard_map/while/body/eval_jaxpr/ppermute | solution.py:21
  328.3 23.2 %collective-permute-start.2 = (s32[1,128]{1,0:T(1,128)S(1)}, s32[1,128]{1,0:T(1,128)S(1)}, u32[]{:S(2)}, u32[]{:S(2)}) collective-permute-start(s32[1,128]{1,0:T(1,128)S(1)} %copy.122), channel_id=1, source_target_pairs={{0,4},{4,8},{8,12},{12,16},{16,20},{20,24},{24,28},{28,0},{1,5},{5... | collective-permute-start | bytes 1544 | tf_op jit(solution)/shard_map/while/body/eval_jaxpr/ppermute | solution.py:21
  332.6 13.2 %collective-permute-start.3 = (bf16[1,128,1024]{1,2,0:T(8,128)(2,1)}, bf16[1,128,1024]{1,2,0:T(8,128)(2,1)}, u32[]{:S(2)}, u32[]{:S(2)}) collective-permute-start(bf16[1,128,1024]{1,2,0:T(8,128)(2,1)} %fusion.183), channel_id=1, source_target_pairs={{0,4},{4,8},{8,12},{12,16},{16,20},{20,24},{24,28},{28,0},{1,5},{5... | collective-permute-start | bytes 786440 | tf_op jit(solution)/shard_map/while/body/eval_jaxpr/ppermute | solution.py:21
  334.6 16.1 %collective-permute-start.4 = (bf16[1,128,1024]{1,2,0:T(8,128)(2,1)S(1)}, bf16[1,128,1024]{1,2,0:T(8,128)(2,1)S(1)}, u32[]{:S(2)}, u32[]{:S(2)}) collective-permute-start(bf16[1,128,1024]{1,2,0:T(8,128)(2,1)S(1)} %fusion.185), channel_id=1, source_target_pairs={{0,4},{4,8},{8,12},{12,16},{16,20},{20,24},{24,28},{28,0},{1,5},{5... | collective-permute-start | bytes 786440 | tf_op jit(solution)/shard_map/while/body/eval_jaxpr/ppermute | solution.py:21
  336.4 15.1 %copy-start.6 = (f32[1,128,16,64]{1,3,2,0:T(8,128)}, f32[1,128,16,64]{1,3,2,0:T(8,128)S(1)}, u32[]{:S(2)}) copy-start(f32[1,128,16,64]{1,3,2,0:T(8,128)S(1)} %fusion.186) | copy-start | bytes 1572868 | tf_op jit(solution)/shard_map/while
  351.6 26.3 %collective-permute-start = (bf16[1,128,1024]{1,2,0:T(8,128)(2,1)S(1)}, bf16[1,128,1024]{1,2,0:T(8,128)(2,1)S(1)}, u32[]{:S(2)}, u32[]{:S(2)}) collective-permute-start(bf16[1,128,1024]{1,2,0:T(8,128)(2,1)S(1)} %copy.120), channel_id=1, source_target_pairs={{0,4},{4,8},{8,12},{12,16},{16,20},{20,24},{24,28},{28,0},{1,5},{5... | collective-permute-start | bytes 786440 | tf_op jit(solution)/shard_map/while/body/eval_jaxpr/ppermute | solution.py:21
  353.1 24.7 %collective-permute-start.1 = (bf16[1,128,1024]{1,2,0:T(8,128)(2,1)S(1)}, bf16[1,128,1024]{1,2,0:T(8,128)(2,1)}, u32[]{:S(2)}, u32[]{:S(2)}) collective-permute-start(bf16[1,128,1024]{1,2,0:T(8,128)(2,1)S(1)} %copy.121), channel_id=1, source_target_pairs={{0,4},{4,8},{8,12},{12,16},{16,20},{20,24},{24,28},{28,0},{1,5},{5... | collective-permute-start | bytes 786440 | tf_op jit(solution)/shard_map/while/body/eval_jaxpr/ppermute | solution.py:21
  355.5 22.4 %collective-permute-start.2 = (s32[1,128]{1,0:T(1,128)S(1)}, s32[1,128]{1,0:T(1,128)S(1)}, u32[]{:S(2)}, u32[]{:S(2)}) collective-permute-start(s32[1,128]{1,0:T(1,128)S(1)} %copy.122), channel_id=1, source_target_pairs={{0,4},{4,8},{8,12},{12,16},{16,20},{20,24},{24,28},{28,0},{1,5},{5... | collective-permute-start | bytes 1544 | tf_op jit(solution)/shard_map/while/body/eval_jaxpr/ppermute | solution.py:21
  360.0 13.1 %collective-permute-start.3 = (bf16[1,128,1024]{1,2,0:T(8,128)(2,1)}, bf16[1,128,1024]{1,2,0:T(8,128)(2,1)}, u32[]{:S(2)}, u32[]{:S(2)}) collective-permute-start(bf16[1,128,1024]{1,2,0:T(8,128)(2,1)} %fusion.183), channel_id=1, source_target_pairs={{0,4},{4,8},{8,12},{12,16},{16,20},{20,24},{24,28},{28,0},{1,5},{5... | collective-permute-start | bytes 786440 | tf_op jit(solution)/shard_map/while/body/eval_jaxpr/ppermute | solution.py:21
  362.9 14.1 %collective-permute-start.4 = (bf16[1,128,1024]{1,2,0:T(8,128)(2,1)S(1)}, bf16[1,128,1024]{1,2,0:T(8,128)(2,1)S(1)}, u32[]{:S(2)}, u32[]{:S(2)}) collective-permute-start(bf16[1,128,1024]{1,2,0:T(8,128)(2,1)S(1)} %fusion.185), channel_id=1, source_target_pairs={{0,4},{4,8},{8,12},{12,16},{16,20},{20,24},{24,28},{28,0},{1,5},{5... | collective-permute-start | bytes 786440 | tf_op jit(solution)/shard_map/while/body/eval_jaxpr/ppermute | solution.py:21
  363.9 14.0 %copy-start.6 = (f32[1,128,16,64]{1,3,2,0:T(8,128)}, f32[1,128,16,64]{1,3,2,0:T(8,128)S(1)}, u32[]{:S(2)}) copy-start(f32[1,128,16,64]{1,3,2,0:T(8,128)S(1)} %fusion.186) | copy-start | bytes 1572868 | tf_op jit(solution)/shard_map/while
  377.9 25.4 %collective-permute-start = (bf16[1,128,1024]{1,2,0:T(8,128)(2,1)S(1)}, bf16[1,128,1024]{1,2,0:T(8,128)(2,1)S(1)}, u32[]{:S(2)}, u32[]{:S(2)}) collective-permute-start(bf16[1,128,1024]{1,2,0:T(8,128)(2,1)S(1)} %copy.120), channel_id=1, source_target_pairs={{0,4},{4,8},{8,12},{12,16},{16,20},{20,24},{24,28},{28,0},{1,5},{5... | collective-permute-start | bytes 786440 | tf_op jit(solution)/shard_map/while/body/eval_jaxpr/ppermute | solution.py:21
  379.0 24.4 %collective-permute-start.1 = (bf16[1,128,1024]{1,2,0:T(8,128)(2,1)S(1)}, bf16[1,128,1024]{1,2,0:T(8,128)(2,1)}, u32[]{:S(2)}, u32[]{:S(2)}) collective-permute-start(bf16[1,128,1024]{1,2,0:T(8,128)(2,1)S(1)} %copy.121), channel_id=1, source_target_pairs={{0,4},{4,8},{8,12},{12,16},{16,20},{20,24},{24,28},{28,0},{1,5},{5... | collective-permute-start | bytes 786440 | tf_op jit(solution)/shard_map/while/body/eval_jaxpr/ppermute | solution.py:21
  381.9 21.4 %collective-permute-start.2 = (s32[1,128]{1,0:T(1,128)S(1)}, s32[1,128]{1,0:T(1,128)S(1)}, u32[]{:S(2)}, u32[]{:S(2)}) collective-permute-start(s32[1,128]{1,0:T(1,128)S(1)} %copy.122), channel_id=1, source_target_pairs={{0,4},{4,8},{8,12},{12,16},{16,20},{20,24},{24,28},{28,0},{1,5},{5... | collective-permute-start | bytes 1544 | tf_op jit(solution)/shard_map/while/body/eval_jaxpr/ppermute | solution.py:21
  385.8 13.7 %collective-permute-start.3 = (bf16[1,128,1024]{1,2,0:T(8,128)(2,1)}, bf16[1,128,1024]{1,2,0:T(8,128)(2,1)}, u32[]{:S(2)}, u32[]{:S(2)}) collective-permute-start(bf16[1,128,1024]{1,2,0:T(8,128)(2,1)} %fusion.183), channel_id=1, source_target_pairs={{0,4},{4,8},{8,12},{12,16},{16,20},{20,24},{24,28},{28,0},{1,5},{5... | collective-permute-start | bytes 786440 | tf_op jit(solution)/shard_map/while/body/eval_jaxpr/ppermute | solution.py:21
  389.2 13.3 %collective-permute-start.4 = (bf16[1,128,1024]{1,2,0:T(8,128)(2,1)S(1)}, bf16[1,128,1024]{1,2,0:T(8,128)(2,1)S(1)}, u32[]{:S(2)}, u32[]{:S(2)}) collective-permute-start(bf16[1,128,1024]{1,2,0:T(8,128)(2,1)S(1)} %fusion.185), channel_id=1, source_target_pairs={{0,4},{4,8},{8,12},{12,16},{16,20},{20,24},{24,28},{28,0},{1,5},{5... | collective-permute-start | bytes 786440 | tf_op jit(solution)/shard_map/while/body/eval_jaxpr/ppermute | solution.py:21
  389.9 13.4 %copy-start.6 = (f32[1,128,16,64]{1,3,2,0:T(8,128)}, f32[1,128,16,64]{1,3,2,0:T(8,128)S(1)}, u32[]{:S(2)}) copy-start(f32[1,128,16,64]{1,3,2,0:T(8,128)S(1)} %fusion.186) | copy-start | bytes 1572868 | tf_op jit(solution)/shard_map/while
  403.4 25.0 %collective-permute-start = (bf16[1,128,1024]{1,2,0:T(8,128)(2,1)S(1)}, bf16[1,128,1024]{1,2,0:T(8,128)(2,1)S(1)}, u32[]{:S(2)}, u32[]{:S(2)}) collective-permute-start(bf16[1,128,1024]{1,2,0:T(8,128)(2,1)S(1)} %copy.120), channel_id=1, source_target_pairs={{0,4},{4,8},{8,12},{12,16},{16,20},{20,24},{24,28},{28,0},{1,5},{5... | collective-permute-start | bytes 786440 | tf_op jit(solution)/shard_map/while/body/eval_jaxpr/ppermute | solution.py:21
  404.4 24.0 %collective-permute-start.1 = (bf16[1,128,1024]{1,2,0:T(8,128)(2,1)S(1)}, bf16[1,128,1024]{1,2,0:T(8,128)(2,1)}, u32[]{:S(2)}, u32[]{:S(2)}) collective-permute-start(bf16[1,128,1024]{1,2,0:T(8,128)(2,1)S(1)} %copy.121), channel_id=1, source_target_pairs={{0,4},{4,8},{8,12},{12,16},{16,20},{20,24},{24,28},{28,0},{1,5},{5... | collective-permute-start | bytes 786440 | tf_op jit(solution)/shard_map/while/body/eval_jaxpr/ppermute | solution.py:21
  407.4 21.1 %collective-permute-start.2 = (s32[1,128]{1,0:T(1,128)S(1)}, s32[1,128]{1,0:T(1,128)S(1)}, u32[]{:S(2)}, u32[]{:S(2)}) collective-permute-start(s32[1,128]{1,0:T(1,128)S(1)} %copy.122), channel_id=1, source_target_pairs={{0,4},{4,8},{8,12},{12,16},{16,20},{20,24},{24,28},{28,0},{1,5},{5... | collective-permute-start | bytes 1544 | tf_op jit(solution)/shard_map/while/body/eval_jaxpr/ppermute | solution.py:21
  411.7 13.2 %collective-permute-start.3 = (bf16[1,128,1024]{1,2,0:T(8,128)(2,1)}, bf16[1,128,1024]{1,2,0:T(8,128)(2,1)}, u32[]{:S(2)}, u32[]{:S(2)}) collective-permute-start(bf16[1,128,1024]{1,2,0:T(8,128)(2,1)} %fusion.183), channel_id=1, source_target_pairs={{0,4},{4,8},{8,12},{12,16},{16,20},{20,24},{24,28},{28,0},{1,5},{5... | collective-permute-start | bytes 786440 | tf_op jit(solution)/shard_map/while/body/eval_jaxpr/ppermute | solution.py:21
  414.7 12.9 %collective-permute-start.4 = (bf16[1,128,1024]{1,2,0:T(8,128)(2,1)S(1)}, bf16[1,128,1024]{1,2,0:T(8,128)(2,1)S(1)}, u32[]{:S(2)}, u32[]{:S(2)}) collective-permute-start(bf16[1,128,1024]{1,2,0:T(8,128)(2,1)S(1)} %fusion.185), channel_id=1, source_target_pairs={{0,4},{4,8},{8,12},{12,16},{16,20},{20,24},{24,28},{28,0},{1,5},{5... | collective-permute-start | bytes 786440 | tf_op jit(solution)/shard_map/while/body/eval_jaxpr/ppermute | solution.py:21
  417.2 11.3 copy-start.6
  428.5 25.4 %collective-permute-start = (bf16[1,128,1024]{1,2,0:T(8,128)(2,1)S(1)}, bf16[1,128,1024]{1,2,0:T(8,128)(2,1)S(1)}, u32[]{:S(2)}, u32[]{:S(2)}) collective-permute-start(bf16[1,128,1024]{1,2,0:T(8,128)(2,1)S(1)} %copy.120), channel_id=1, source_target_pairs={{0,4},{4,8},{8,12},{12,16},{16,20},{20,24},{24,28},{28,0},{1,5},{5... | collective-permute-start | bytes 786440 | tf_op jit(solution)/shard_map/while/body/eval_jaxpr/ppermute | solution.py:21
  429.5 24.4 %collective-permute-start.1 = (bf16[1,128,1024]{1,2,0:T(8,128)(2,1)S(1)}, bf16[1,128,1024]{1,2,0:T(8,128)(2,1)}, u32[]{:S(2)}, u32[]{:S(2)}) collective-permute-start(bf16[1,128,1024]{1,2,0:T(8,128)(2,1)S(1)} %copy.121), channel_id=1, source_target_pairs={{0,4},{4,8},{8,12},{12,16},{16,20},{20,24},{24,28},{28,0},{1,5},{5... | collective-permute-start | bytes 786440 | tf_op jit(solution)/shard_map/while/body/eval_jaxpr/ppermute | solution.py:21
  432.2 21.8 %collective-permute-start.2 = (s32[1,128]{1,0:T(1,128)S(1)}, s32[1,128]{1,0:T(1,128)S(1)}, u32[]{:S(2)}, u32[]{:S(2)}) collective-permute-start(s32[1,128]{1,0:T(1,128)S(1)} %copy.122), channel_id=1, source_target_pairs={{0,4},{4,8},{8,12},{12,16},{16,20},{20,24},{24,28},{28,0},{1,5},{5... | collective-permute-start | bytes 1544 | tf_op jit(solution)/shard_map/while/body/eval_jaxpr/ppermute | solution.py:21
  438.5 11.9 %collective-permute-start.3 = (bf16[1,128,1024]{1,2,0:T(8,128)(2,1)}, bf16[1,128,1024]{1,2,0:T(8,128)(2,1)}, u32[]{:S(2)}, u32[]{:S(2)}) collective-permute-start(bf16[1,128,1024]{1,2,0:T(8,128)(2,1)} %fusion.183), channel_id=1, source_target_pairs={{0,4},{4,8},{8,12},{12,16},{16,20},{20,24},{24,28},{28,0},{1,5},{5... | collective-permute-start | bytes 786440 | tf_op jit(solution)/shard_map/while/body/eval_jaxpr/ppermute | solution.py:21
  439.8 13.3 %collective-permute-start.4 = (bf16[1,128,1024]{1,2,0:T(8,128)(2,1)S(1)}, bf16[1,128,1024]{1,2,0:T(8,128)(2,1)S(1)}, u32[]{:S(2)}, u32[]{:S(2)}) collective-permute-start(bf16[1,128,1024]{1,2,0:T(8,128)(2,1)S(1)} %fusion.185), channel_id=1, source_target_pairs={{0,4},{4,8},{8,12},{12,16},{16,20},{20,24},{24,28},{28,0},{1,5},{5... | collective-permute-start | bytes 786440 | tf_op jit(solution)/shard_map/while/body/eval_jaxpr/ppermute | solution.py:21
  443.5 10.4 copy-start.6
  454.0 24.6 %collective-permute-start = (bf16[1,128,1024]{1,2,0:T(8,128)(2,1)S(1)}, bf16[1,128,1024]{1,2,0:T(8,128)(2,1)S(1)}, u32[]{:S(2)}, u32[]{:S(2)}) collective-permute-start(bf16[1,128,1024]{1,2,0:T(8,128)(2,1)S(1)} %copy.120), channel_id=1, source_target_pairs={{0,4},{4,8},{8,12},{12,16},{16,20},{20,24},{24,28},{28,0},{1,5},{5... | collective-permute-start | bytes 786440 | tf_op jit(solution)/shard_map/while/body/eval_jaxpr/ppermute | solution.py:21
  455.0 23.6 %collective-permute-start.1 = (bf16[1,128,1024]{1,2,0:T(8,128)(2,1)S(1)}, bf16[1,128,1024]{1,2,0:T(8,128)(2,1)}, u32[]{:S(2)}, u32[]{:S(2)}) collective-permute-start(bf16[1,128,1024]{1,2,0:T(8,128)(2,1)S(1)} %copy.121), channel_id=1, source_target_pairs={{0,4},{4,8},{8,12},{12,16},{16,20},{20,24},{24,28},{28,0},{1,5},{5... | collective-permute-start | bytes 786440 | tf_op jit(solution)/shard_map/while/body/eval_jaxpr/ppermute | solution.py:21
  458.2 20.4 %collective-permute-start.2 = (s32[1,128]{1,0:T(1,128)S(1)}, s32[1,128]{1,0:T(1,128)S(1)}, u32[]{:S(2)}, u32[]{:S(2)}) collective-permute-start(s32[1,128]{1,0:T(1,128)S(1)} %copy.122), channel_id=1, source_target_pairs={{0,4},{4,8},{8,12},{12,16},{16,20},{20,24},{24,28},{28,0},{1,5},{5... | collective-permute-start | bytes 1544 | tf_op jit(solution)/shard_map/while/body/eval_jaxpr/ppermute | solution.py:21
  464.6 10.6 collective-permute-start.3
  465.3 12.5 %collective-permute-start.4 = (bf16[1,128,1024]{1,2,0:T(8,128)(2,1)S(1)}, bf16[1,128,1024]{1,2,0:T(8,128)(2,1)S(1)}, u32[]{:S(2)}, u32[]{:S(2)}) collective-permute-start(bf16[1,128,1024]{1,2,0:T(8,128)(2,1)S(1)} %fusion.185), channel_id=1, source_target_pairs={{0,4},{4,8},{8,12},{12,16},{16,20},{20,24},{24,28},{28,0},{1,5},{5... | collective-permute-start | bytes 786440 | tf_op jit(solution)/shard_map/while/body/eval_jaxpr/ppermute | solution.py:21
  478.7 23.8 %collective-permute-start = (bf16[1,128,1024]{1,2,0:T(8,128)(2,1)S(1)}, bf16[1,128,1024]{1,2,0:T(8,128)(2,1)S(1)}, u32[]{:S(2)}, u32[]{:S(2)}) collective-permute-start(bf16[1,128,1024]{1,2,0:T(8,128)(2,1)S(1)} %copy.120), channel_id=1, source_target_pairs={{0,4},{4,8},{8,12},{12,16},{16,20},{20,24},{24,28},{28,0},{1,5},{5... | collective-permute-start | bytes 786440 | tf_op jit(solution)/shard_map/while/body/eval_jaxpr/ppermute | solution.py:21
  479.7 22.8 %collective-permute-start.1 = (bf16[1,128,1024]{1,2,0:T(8,128)(2,1)S(1)}, bf16[1,128,1024]{1,2,0:T(8,128)(2,1)}, u32[]{:S(2)}, u32[]{:S(2)}) collective-permute-start(bf16[1,128,1024]{1,2,0:T(8,128)(2,1)S(1)} %copy.121), channel_id=1, source_target_pairs={{0,4},{4,8},{8,12},{12,16},{16,20},{20,24},{24,28},{28,0},{1,5},{5... | collective-permute-start | bytes 786440 | tf_op jit(solution)/shard_map/while/body/eval_jaxpr/ppermute | solution.py:21
  483.4 19.1 %collective-permute-start.2 = (s32[1,128]{1,0:T(1,128)S(1)}, s32[1,128]{1,0:T(1,128)S(1)}, u32[]{:S(2)}, u32[]{:S(2)}) collective-permute-start(s32[1,128]{1,0:T(1,128)S(1)} %copy.122), channel_id=1, source_target_pairs={{0,4},{4,8},{8,12},{12,16},{16,20},{20,24},{24,28},{28,0},{1,5},{5... | collective-permute-start | bytes 1544 | tf_op jit(solution)/shard_map/while/body/eval_jaxpr/ppermute | solution.py:21
  489.7 9.3 collective-permute-start.3
  490.4 11.3 collective-permute-start.4
  505.3 11.8 %collective-permute-start.6 = (bf16[1,128,1024]{1,2,0:T(8,128)(2,1)S(1)}, bf16[1,128,1024]{1,2,0:T(8,128)(2,1)S(1)}, u32[]{:S(2)}, u32[]{:S(2)}) collective-permute-start(bf16[1,128,1024]{1,2,0:T(8,128)(2,1)S(1)} %fusion.77), channel_id=1, source_target_pairs={{0,4},{4,8},{8,12},{12,16},{16,20},{20,24},{24,28},{28,0},{1,5},{5... | collective-permute-start | bytes 786440 | tf_op jit(solution)/shard_map/ppermute | solution.py:21
  508.0 8.6 collective-permute-start.5
  522.4 152.6 %reduce-scatter.9.cloned.1.call-start = ((), (), s32[]{:S(2)}) async-start(), calls=%async_computation.12 | async-start | bytes 13434880 | tf_op jit(solution)/shard_map/reduce_scatter | solution.py:342
  536.9 11.9 %copy-start.16 = (f32[1,128,1024]{2,1,0:T(8,128)S(1)}, f32[1,128,1024]{2,1,0:T(8,128)}, u32[]{:S(2)}) copy-start(f32[1,128,1024]{2,1,0:T(8,128)} %copy-done.15) | copy-start | bytes 1572868
  536.9 11.9 %copy-start.19 = (bf16[1,128,1024]{2,1,0:T(8,128)(2,1)S(1)}, bf16[1,128,1024]{2,1,0:T(8,128)(2,1)}, u32[]{:S(2)}) copy-start(bf16[1,128,1024]{2,1,0:T(8,128)(2,1)} %param.21) | copy-start | bytes 786436
  (54 other events, 149.1 us)
Sparse Core Ops, SparseCore 0:
  9.6 47.5 all-gather.8
  58.7 41.1 all-gather.18
  102.7 49.2 all-gather.10
  154.0 47.7 all-gather.12
  203.2 21.0 all-gather.14
  225.7 71.6 all-gather.16
  314.7 31.4 reduce-scatter.6
  349.5 52.2 reduce-scatter.10
  522.6 62.5 reduce-scatter.4
  587.8 87.1 reduce-scatter.8
where the time goes:
time: 1160 us
  blocking collectives  508 us (44%)
  waiting for transfers between devices  403 us (35%)
  matrix products  81.9 us (7%)
  starting transfers between devices  61.8 us (5%)
  other arithmetic  58.4 us (5%)
  local copies, waits for them, and re-layouts  26.2 us (2%)
  between operations  15.5 us (1%)
    psum x1, blocking collectives, local(): lax.psum((shares[0], shares[1], shares[2], shares[3], shares[4], shares[5...  473 us
    reduce_scatter x1, waiting for transfers between devices, local(): lax.psum_scatter(grad_w_in.astype(jnp.bfloat16), ('seq', 'wsh'), scatter_...  89.8 us
    ppermute x37, waiting for transfers between devices, from_behind(): lax.ppermute(shard, axis, [(i, (i + by) % size) for i in range(size)])  69.2 us
    ppermute x37, starting transfers between devices, from_behind(): lax.ppermute(shard, axis, [(i, (i + by) % size) for i in range(size)])  60.9 us
    all_gather x1, waiting for transfers between devices, local(): lax.all_gather(w_in, ('seq', 'wsh'), axis=0, tiled=True)  60.5 us
    all_gather x1, waiting for transfers between devices, local(): lax.all_gather(value_rows, 'ctx', axis=1, tiled=True)  49.8 us
    all_gather x1, waiting for transfers between devices, local(): lax.all_gather(key_rows, 'ctx', axis=1, tiled=True)  45.3 us
    all_gather x1, waiting for transfers between devices, local(): lax.all_gather(w_qkv, ('seq', 'wsh'), axis=0, tiled=True)  40.9 us
  transfers between devices with their start and end apart: 47, of which 22 were waited for; matrix products, arithmetic and copies ran while one was open for 12% of the time, Pallas kernels for 0%

commit v1 on v0

--- a/solution.py
+++ b/solution.py
@@ -1,8 +1,11 @@
+import functools
 import math
 
 import jax
 import jax.numpy as jnp
 from jax import lax
+from jax.experimental import pallas as pl
+from jax.experimental.pallas import tpu as pltpu
 from jax.sharding import PartitionSpec as P
 
 D = 1024
@@ -359,6 +362,455 @@
     return (output, grad_tokens, summed[0], summed[1], summed[2], summed[3], summed[4], summed[5])
 
 
+GROUP = ("seq", "wsh")
+MESH = pl.DeviceIdType.MESH
+
+
+def group_peer(index):
+    return {"seq": index // 2, "wsh": lax.rem(index, 2)}
+
+
+def ctx_peer(index):
+    return {"ctx": index}
+
+
+def exchange_kernel(size, group, spread, src, dst, send_sems, recv_sems, own_sem):
+    if group:
+        me = lax.axis_index("seq") * 2 + lax.axis_index("wsh")
+        peer_of = group_peer
+    else:
+        me = lax.axis_index("ctx")
+        peer_of = ctx_peer
+    barrier = pltpu.get_barrier_semaphore()
+    for step in range(1, size):
+        pl.semaphore_signal(
+            barrier, inc=1, device_id=peer_of(lax.rem(me + step, size)), device_id_type=MESH
+        )
+    pl.semaphore_wait(barrier, size - 1)
+    copies = []
+    for step in range(1, size):
+        peer = lax.rem(me + step, size)
+        copy = pltpu.make_async_remote_copy(
+            src_ref=src.at[peer] if spread else src,
+            dst_ref=dst.at[me],
+            send_sem=send_sems.at[step - 1],
+            recv_sem=recv_sems.at[step - 1],
+            device_id=peer_of(peer),
+            device_id_type=MESH,
+        )
+        copy.start()
+        copies.append(copy)
+    own = pltpu.make_async_copy(src.at[me] if spread else src, dst.at[me], own_sem)
+    own.start()
+    own.wait()
+    for copy in copies:
+        copy.wait()
+
+
+def exchange(shard, size, group, spread, number):
+    shape = shard.shape if spread else (size,) + shard.shape
+    return pl.pallas_call(
+        functools.partial(exchange_kernel, size, group, spread),
+        out_shape=jax.ShapeDtypeStruct(shape, shard.dtype),
+        in_specs=[pl.BlockSpec(memory_space=pl.ANY)],
+        out_specs=pl.BlockSpec(memory_space=pl.ANY),
+        scratch_shapes=[
+            pltpu.SemaphoreType.DMA((size - 1,)),
+            pltpu.SemaphoreType.DMA((size - 1,)),
+            pltpu.SemaphoreType.DMA,
+        ],
+        compiler_params=pltpu.CompilerParams(collective_id=number, has_side_effects=True),
+    )(shard)
+
+
+def reduce_kernel(turns, size, count, *refs):
+    low, wide = jnp.bfloat16, jnp.float32
+    grads, outs = refs[:count], refs[count : 2 * count]
+    from_y, from_z, total = (refs[(2 + i) * count : (3 + i) * count] for i in range(3))
+    sends, recvs = refs[5 * count : 5 * count + 2]
+    depth = size // 2
+    parts = 4
+    me = lax.axis_index("ctx")
+    place, side = me // 2, lax.rem(me, 2)
+    across = me + 1 - 2 * side
+    group_me = lax.axis_index("seq") * 2 + lax.axis_index("wsh")
+    z_peers = [lax.rem(place + step, depth) for step in range(1, depth)]
+    x_peers = [lax.rem(group_me + step, parts) for step in range(1, parts)]
+
+    barrier = pltpu.get_barrier_semaphore()
+    pl.semaphore_signal(barrier, inc=1, device_id=ctx_peer(across), device_id_type=MESH)
+    for peer in z_peers:
+        pl.semaphore_signal(
+            barrier, inc=1, device_id=ctx_peer(peer * 2 + side), device_id_type=MESH
+        )
+    for peer in x_peers:
+        pl.semaphore_signal(barrier, inc=1, device_id=group_peer(peer), device_id_type=MESH)
+    pl.semaphore_wait(barrier, 1 + len(z_peers) + len(x_peers))
+
+    def remote(chunk, slot, source, target, device):
+        copy = pltpu.make_async_remote_copy(
+            src_ref=source,
+            dst_ref=target,
+            send_sem=sends.at[chunk, slot],
+            recv_sem=recvs.at[chunk, slot],
+            device_id=device,
+            device_id_type=MESH,
+        )
+        copy.start()
+        return copy
+
+    def by_rows(rows, step_body):
+        block = 32 if rows % 32 == 0 else 16
+
+        def body(index, carry):
+            step_body(pl.ds(pl.multiple_of(index * block, block), block))
+            return carry
+
+        lax.fori_loop(0, rows // block, body, 0)
+
+    z_slot = depth
+    x_slot = z_slot + depth - 1
+    zg_slot = x_slot + parts - 1
+    yg_slot = zg_slot + depth - 1
+    ys, zs, xs, zgs, ygs = ({} for _ in range(5))
+
+    def start_y(c):
+        ys[c] = [
+            remote(c, z, grads[c].at[2 * z + 1 - side], from_y[c].at[z], ctx_peer(across))
+            for z in range(depth)
+        ]
+
+    def start_z(c):
+        rows = total[c].shape[0]
+        for copy in ys[c]:
+            copy.wait()
+
+        def add(at):
+            for z in range(depth):
+                from_y[c][z, at, :] = (
+                    grads[c][2 * z + side, at, :].astype(wide) + from_y[c][z, at, :].astype(wide)
+                ).astype(low)
+
+        by_rows(rows, add)
+        zs[c] = [
+            remote(
+                c, z_slot + i, from_y[c].at[peer], from_z[c].at[place], ctx_peer(peer * 2 + side)
+            )
+            for i, peer in enumerate(z_peers)
+        ]
+
+    def start_x(c):
+        rows = total[c].shape[0]
+        for copy in zs[c]:
+            copy.wait()
+
+        def add(at):
+            summed = from_y[c][place, at, :].astype(wide)
+            for peer in z_peers:
+                summed = summed + from_z[c][peer, at, :].astype(wide)
+            if turns[c]:
+                total[c][at, :] = summed.astype(low)
+            else:
+                outs[c][me, at, :] = summed.astype(low)
+
+        by_rows(rows, add)
+        if turns[c]:
+            piece = rows // parts
+            xs[c] = [
+                remote(
+                    c,
+                    x_slot + i,
+                    total[c].at[pl.ds(pl.multiple_of(peer * piece, piece), piece)],
+                    outs[c].at[me, pl.ds(pl.multiple_of(group_me * piece, piece), piece)],
+                    group_peer(peer),
+                )
+                for i, peer in enumerate(x_peers)
+            ]
+            mine = pl.ds(pl.multiple_of(group_me * piece, piece), piece)
+            outs[c][me, mine, :] = total[c][mine, :]
+
+    def start_zg(c):
+        if turns[c]:
+            for copy in xs[c]:
+                copy.wait()
+        zgs[c] = [
+            remote(c, zg_slot + i, outs[c].at[me], outs[c].at[me], ctx_peer(peer * 2 + side))
+            for i, peer in enumerate(z_peers)
+        ]
+        ygs[c] = [remote(c, yg_slot, outs[c].at[me], outs[c].at[me], ctx_peer(across))]
+
+    def start_yg(c):
+        for i, (copy, step) in enumerate(zip(zgs[c], range(1, depth))):
+            copy.wait()
+            came = lax.rem(place + depth - step, depth) * 2 + side
+            ygs[c].append(
+                remote(c, yg_slot + step, outs[c].at[came], outs[c].at[came], ctx_peer(across))
+            )
+
+    for c in range(count):
+        start_y(c)
+    for turn in range(count + 3):
+        for stage, back in ((start_z, 0), (start_x, 1), (start_zg, 2), (start_yg, 3)):
+            if 0 <= turn - back < count:
+                stage(turn - back)
+    for c in range(count):
+        for copy in ygs[c]:
+            copy.wait()
+
+
+def reduce_over_ctx(grads, turns, size, number):
+    count = len(grads)
+    depth = size // 2
+    slots = depth + 2 * (depth - 1) + 3 + depth
+    whole = pl.BlockSpec(memory_space=pltpu.VMEM)
+    pairs = [pltpu.VMEM((depth,) + g.shape[1:], g.dtype) for g in grads]
+    totals = [pltpu.VMEM(g.shape[1:], g.dtype) for g in grads]
+    return pl.pallas_call(
+        functools.partial(reduce_kernel, turns, size, count),
+        out_shape=[jax.ShapeDtypeStruct(g.shape, g.dtype) for g in grads],
+        in_specs=[whole] * count,
+        out_specs=[whole] * count,
+        scratch_shapes=pairs
+        + pairs
+        + totals
+        + [pltpu.SemaphoreType.DMA((count, slots)), pltpu.SemaphoreType.DMA((count, slots))],
+        compiler_params=pltpu.CompilerParams(
+            collective_id=number, has_side_effects=True, vmem_limit_bytes=48 * 1024 * 1024
+        ),
+    )(*grads)
+
+
+def permute_group(chunk_for, parts):
+    me = lax.axis_index(GROUP)
+    came = [chunk_for(me)]
+    for step in range(1, parts):
+        pairs = [(i, i ^ step) for i in range(parts)]
+        came.append(lax.ppermute(chunk_for(me ^ step), GROUP, pairs))
+    order = jnp.arange(parts) ^ me
+    return jnp.stack(came)[order]
+
+
+def layer_norm_parts(values):
+    middle = jnp.mean(values, -1, keepdims=True)
+    centred = values - middle
+    factor = lax.rsqrt(jnp.mean(centred * centred, -1, keepdims=True) + layer_eps)
+    return centred * factor, factor
+
+
+def norm_back(grad, gain, normed, factor):
+    scaled = grad * gain
+    return factor * (
+        scaled
+        - jnp.mean(scaled, -1, keepdims=True)
+        - normed * jnp.mean(scaled * normed, -1, keepdims=True)
+    )
+
+
+def dot(equation, left, right):
+    return jnp.einsum(equation, left, right, preferred_element_type=jnp.float32)
+
+
+def parallel(parts, ctx_size, tokens, positions, w_qkv, w_out, w_in, w_down, gain_attn, gain_mlp,
+             cotangent):
+    low = jnp.bfloat16
+    wide = jnp.float32
+    row_count = tokens.shape[1]
+    length = row_count * ctx_size
+    part_heads = HEADS // parts
+    part_ff = FF // parts
+    part_d = D // parts
+    pairs = parts * part_heads // ctx_size
+    seq_split = part_heads // pairs
+    half = HEAD // 2
+    scaling = HEAD ** (-0.5)
+    ctx_index = lax.axis_index("ctx")
+
+    def gather(shard, number):
+        return exchange(shard, parts, True, False, number)
+
+    def swap(shard, number):
+        return exchange(shard, parts, True, True, number)
+
+    def swap_ctx(shard, number):
+        return exchange(shard, ctx_size, False, True, number)
+
+    def gather_ctx(shard, number):
+        return exchange(shard, ctx_size, False, False, number)
+
+    inputs = tokens[0].astype(wide)
+    cot = cotangent[0]
+    small = jnp.concatenate(
+        [positions[0].astype(wide), gain_attn.astype(wide), gain_mlp.astype(wide)]
+    )
+    small = gather(small.reshape(-1, 128), 25).reshape(parts, -1)
+    gain_one = small[:, row_count : row_count + part_d].reshape(D)
+    gain_two = small[:, row_count + part_d :].reshape(D)
+    all_positions = (
+        gather_ctx(small[:, :row_count].astype(jnp.int32), 26).transpose(1, 0, 2).reshape(parts, length)
+    )
+    starts = jnp.arange(length, dtype=jnp.int32)[None, :] - all_positions
+    group_positions = lax.dynamic_slice_in_dim(all_positions, ctx_index * row_count, row_count, 1)
+    my_seq = ctx_index // seq_split
+    seq_positions = lax.dynamic_index_in_dim(all_positions, my_seq, 0, False)
+    seq_starts = lax.dynamic_index_in_dim(starts, my_seq, 0, False)
+
+    in_split = w_in.reshape(part_d, 2, parts, part_ff)
+    in_cols = permute_group(
+        lambda peer: lax.dynamic_index_in_dim(in_split, peer, 2, False), parts
+    ).reshape(D, 2 * part_ff)
+    all_cot = permute_group(lambda peer: cot, parts)
+    qkv_cols = swap(
+        w_qkv.reshape(part_d, 3, parts, part_d).transpose(2, 0, 1, 3).reshape(parts, part_d, 3 * part_d),
+        1,
+    ).reshape(D, 3 * part_d)
+    norm_one, factor_one = layer_norm_parts(inputs)
+    normed_attn = gather((norm_one * gain_one).astype(low), 2)
+    projected = dot("stc,cf->stf", normed_attn, qkv_cols)
+    cosine, sine = rotary_tables(group_positions)
+    turned = [
+        rotate(
+            projected[..., i * part_d : (i + 1) * part_d].reshape(
+                parts, row_count, part_heads, HEAD
+            ),
+            cosine,
+            sine,
+        )
+        for i in range(2)
+    ]
+    turned.append(projected[..., 2 * part_d :].reshape(parts, row_count, part_heads, HEAD))
+    heads_out = jnp.stack([t.astype(low) for t in turned])
+    heads_out = (
+        heads_out.reshape(3, parts, row_count, seq_split, pairs * HEAD)
+        .transpose(1, 3, 2, 0, 4)
+        .reshape(ctx_size, row_count, 3 * pairs * HEAD)
+    )
+    heads_in = swap_ctx(heads_out, 3).reshape(length, 3, pairs, HEAD).transpose(1, 2, 0, 3)
+    queries, keys, values = heads_in
+    same = (seq_starts[:, None] == seq_starts[None, :])[None]
+    scores = jnp.where(same, dot("hqd,hkd->hqk", queries, keys) * scaling, far_below)
+    best = jnp.max(scores, -1, keepdims=True)
+    raised = jnp.where(same, jnp.exp(scores - best), 0.0)
+    totals = jnp.sum(raised, -1, keepdims=True)
+    log_total = best + jnp.log(totals)
+    attended = dot("hqk,hkd->hqd", raised.astype(low), values) / totals
+
+    def to_tokens(shard, width):
+        return (
+            shard.transpose(1, 0, 2).reshape(ctx_size, row_count, pairs * width)
+        )
+
+    def from_ctx(shard):
+        return (
+            shard.reshape(parts, seq_split, row_count, -1)
+            .transpose(0, 2, 1, 3)
+            .reshape(parts, row_count, -1)
+        )
+
+    attended_low = from_ctx(swap_ctx(to_tokens(attended.astype(low), HEAD), 4))
+    branch = swap(dot("stc,cf->stf", attended_low, w_out).astype(low), 5)
+    mixed = inputs + jnp.sum(branch.astype(wide), 0)
+    norm_two, factor_two = layer_norm_parts(mixed)
+    normed_mlp = gather((norm_two * gain_two).astype(low), 6)
+    hidden = dot("stc,cf->stf", normed_mlp, in_cols)
+    inner, gate = hidden[..., :part_ff], hidden[..., part_ff:]
+    product, pull = jax.vjp(geglu, inner, gate)
+    product = product.astype(low)
+    grad_product = dot("stn,fn->stf", all_cot, w_down)
+    grad_inner, grad_gate = pull(grad_product)
+    grad_hidden = jnp.concatenate([grad_inner, grad_gate], -1).astype(low)
+    normed_back = swap(dot("stf,cf->stc", grad_hidden, in_cols).astype(low), 9)
+    grad_normed_mlp = jnp.sum(normed_back.astype(wide), 0)
+    grad_gain_mlp = jnp.sum(grad_normed_mlp * norm_two, 0)
+    grad_mixed = cot.astype(wide) + norm_back(grad_normed_mlp, gain_two, norm_two, factor_two)
+    grad_branch = gather(grad_mixed.astype(low), 10)
+    grad_attended = dot("stf,cf->stc", grad_branch, w_out).astype(low)
+    grad_out = (
+        grad_attended.reshape(parts, row_count, seq_split, pairs * HEAD)
+        .transpose(0, 2, 1, 3)
+        .reshape(ctx_size, row_count, pairs * HEAD)
+    )
+    grad_heads = swap_ctx(grad_out, 11).reshape(length, pairs, HEAD).transpose(1, 0, 2)
+
+    output_parts = swap(dot("stf,fn->stn", product, w_down).astype(low), 12)
+    output = (mixed + jnp.sum(output_parts.astype(wide), 0)).astype(low)
+
+    def rows_of(grad, width):
+        return (
+            grad.reshape(parts, ctx_size, part_d // ctx_size, width)
+            .transpose(1, 0, 2, 3)
+            .reshape(ctx_size, -1, width)
+            .astype(low)
+        )
+
+    def columns_of(grad):
+        rows = grad.shape[0]
+        return grad.reshape(rows, ctx_size, D // ctx_size).transpose(1, 0, 2).astype(low)
+
+    def back_to_rows(grad, pieces):
+        width = grad.shape[-1] // pieces
+        return (
+            grad.reshape(ctx_size, parts, part_d // ctx_size, pieces, width)
+            .transpose(0, 2, 3, 1, 4)
+            .reshape(part_d, -1)
+            .astype(wide)
+        )
+
+    def back_to_columns(grad):
+        return grad.transpose(1, 0, 2).reshape(grad.shape[1], D).astype(wide)
+
+    down_grad = columns_of(dot("stf,stn->fn", product, all_cot))
+    in_grad = rows_of(dot("stc,stf->cf", normed_mlp, grad_hidden), 2 * part_ff)
+
+    row_dot = jnp.sum(grad_heads.astype(wide) * attended, -1, keepdims=True)
+    weights_f = jnp.where(same, jnp.exp(scores - log_total), 0.0)
+    grad_weights = dot("hqd,hkd->hqk", grad_heads, values)
+    grad_scores = (weights_f * (grad_weights - row_dot)).astype(low)
+    grad_queries = dot("hqk,hkd->hqd", grad_scores, keys) * scaling
+    grad_keys = dot("hqk,hqd->hkd", grad_scores, queries) * scaling
+    grad_values = dot("hqk,hqd->hkd", weights_f.astype(low), grad_heads)
+    seq_cos, seq_sin = rotary_tables(seq_positions)
+    seq_cos, seq_sin = seq_cos[:, 0][None], seq_sin[:, 0][None]
+    grads = jnp.stack(
+        [
+            rotate_back(grad_queries, seq_cos, seq_sin),
+            rotate_back(grad_keys, seq_cos, seq_sin),
+            grad_values,
+        ]
+    ).astype(low)
+    grads = grads.transpose(2, 0, 1, 3).reshape(ctx_size, row_count, 3 * pairs * HEAD)
+    grads = swap_ctx(grads, 15)
+    grad_projected = (
+        grads.reshape(parts, seq_split, row_count, 3, pairs * HEAD)
+        .transpose(0, 2, 3, 1, 4)
+        .reshape(parts, row_count, 3 * part_d)
+    )
+    attn_back = swap(dot("stf,cf->stc", grad_projected, qkv_cols).astype(low), 16)
+    grad_normed_attn = jnp.sum(attn_back.astype(wide), 0)
+    grad_gain_attn = jnp.sum(grad_normed_attn * norm_one, 0)
+    grad_tokens = (
+        grad_mixed + norm_back(grad_normed_attn, gain_one, norm_one, factor_one)
+    ).astype(low)
+
+    out_grad = columns_of(dot("stc,stf->cf", attended_low, grad_branch))
+    qkv_grad = rows_of(dot("stc,stf->cf", normed_attn, grad_projected), 3 * part_d)
+    out_grad, down_grad, qkv_grad, in_grad = reduce_over_ctx(
+        [out_grad, down_grad, qkv_grad, in_grad], (False, False, True, True), ctx_size, 13
+    )
+    gain_sums = jnp.stack([grad_gain_attn, grad_gain_mlp]).reshape(2, parts, part_d)
+    gain_sums = jnp.sum(swap(gain_sums.transpose(1, 0, 2), 27), 0)
+    gain_sums = jnp.sum(gather_ctx(gain_sums, 28), 0)
+    return (
+        output[None],
+        grad_tokens[None],
+        back_to_rows(qkv_grad, 3),
+        back_to_columns(out_grad),
+        back_to_rows(in_grad, 2),
+        back_to_columns(down_grad),
+        gain_sums[0],
+        gain_sums[1],
+    )
+
+
 def solution(mesh):
     placed = (
         P(("seq", "wsh"), "ctx", None),
@@ -371,8 +823,12 @@
         P(("seq", "wsh")),
         P(("seq", "wsh"), "ctx", None),
     )
+    parts = mesh.shape["seq"] * mesh.shape["wsh"]
+    ctx_size = mesh.shape["ctx"]
+    whole_pairs = HEADS % ctx_size == 0 and ctx_size % 2 == 0 and parts == 4
+    body = functools.partial(parallel, parts, ctx_size) if whole_pairs else local
     return jax.shard_map(
-        local,
+        body,
         mesh=mesh,
         in_specs=placed,
         out_specs=(

time: 1160 us -> 637 us (0.55)
  blocking collectives: 508 us -> 0 us
  Pallas kernels: 0 us -> 422 us
  waiting for transfers between devices: 403 us -> 0.02 us
  local copies, waits for them, and re-layouts: 26.2 us -> 109 us
  starting transfers between devices: 61.8 us -> 5.4 us
  matrix products: 81.9 us -> 51.2 us
  other arithmetic: 58.4 us -> 34.8 us
  between operations: 15.5 us -> 1.92 us
    psum x1 -> x0, blocking collectives: 473 us -> none  [local(): lax.psum((shares[0], shares[1], shares[2], shares[3], shares[4], shares[5...]
    pallas_call x0 -> x17, Pallas kernels: none -> 422 us  [the longest x16 230 us: exchange(): pl.pallas_call(functools.partial(exchange_kernel, size, group, spread), o...]
    all_gather x6 -> x0, waiting for transfers between devices: 206 us -> none  [the longest x1 60.5 us: local(): lax.all_gather(w_in, ('seq', 'wsh'), axis=0, tiled=True)]
    reduce_scatter x4 -> x0, waiting for transfers between devices: 125 us -> none  [the longest x1 89.8 us: local(): lax.psum_scatter(grad_w_in.astype(jnp.bfloat16), ('seq', 'wsh'), scatter_...]
    ppermute x37 -> x6, waiting for transfers between devices: 69.2 us -> 0.02 us  [permute_group(): came.append(lax.ppermute(chunk_for(me ^ step), GROUP, pairs))]
    ppermute x37 -> x6, starting transfers between devices: 60.9 us -> 5.4 us  [permute_group(): came.append(lax.ppermute(chunk_for(me ^ step), GROUP, pairs))]
    convert_element_type x1 -> x11, local copies, waits for them, and re-layouts: 0.17 us -> 51.1 us  [the longest x6 41.1 us: back_to_rows(): return grad.reshape(ctx_size, parts, part_d // ctx_size, pieces, width).t...]
    dot_general x56 -> x18, matrix products: 81.9 us -> 51.2 us  [dot(): return jnp.einsum(equation, left, right, preferred_element_type=jnp.float32)]
  transfers between devices with their start and end apart: 47 -> 6, of which waited for: 22 -> 0; matrix products, arithmetic and copies ran while one was open for 12% -> 9% of each run, Pallas kernels for 0% -> 21%
where the time goes in v1:
time: 637 us; the launch traced here: 624 us
  Pallas kernels  422 us (66%)
  local copies, waits for them, and re-layouts  109 us (17%)
  matrix products  51.2 us (8%)
  other arithmetic  34.8 us (5%)
    pallas_call x16, Pallas kernels, exchange(): pl.pallas_call(functools.partial(exchange_kernel, size, group, spread), o...  230 us
    pallas_call x1, Pallas kernels, reduce_over_ctx(): pl.pallas_call(functools.partial(reduce_kernel, turns, size, count), out_...  191 us
    dot_general x18, matrix products, dot(): return jnp.einsum(equation, left, right, preferred_element_type=jnp.float32)  51.2 us
    convert_element_type x6, local copies, waits for them, and re-layouts, back_to_rows(): return grad.reshape(ctx_size, parts, part_d // ctx_size, pieces, width).t...  41.1 us
    unnamed x67, local copies, waits for them, and re-layouts  16.6 us
  transfers between devices with their start and end apart: 6, of which 0 were waited for; matrix products, arithmetic and copies ran while one was open for 9% of the time, Pallas kernels for 21%

profile of v1, /device:TPU:8, one launch (start us, length us, event | category | flops | bytes accessed | tf_op | source)
XLA Modules:
  0.0 624.4 jit_solution(11764519771988861394)
XLA Ops:
  0.7 1.6 collective-permute-start.4
  2.3 4.5 copy.85
  6.8 3.3 dynamic-slice_bitcast_fusion.3
  12.6 29.9 %shard_map.152 = f32[4,5,128]{2,1,0:T(8,128)} custom-call(f32[5,128]{1,0:T(8,128)} %maximum_bitcast_fusion.2.src), custom_call_target="tpu_custom_call" | custom-call | tf_op jit(solution)/shard_map/pallas_call | solution.py:412
  45.1 12.7 %shard_map.154 = bf16[4,128,1024]{2,1,0:T(8,128)(2,1)} custom-call(bf16[128,1024]{1,0:T(8,128)(2,1)} %fusion.38.src), custom_call_target="tpu_custom_call" | custom-call | tf_op jit(solution)/shard_map/pallas_call | solution.py:412
  57.8 2.6 copy.70
  60.3 2.7 copy.71
  63.0 2.6 copy.72.src
  65.6 19.7 %shard_map.155 = bf16[4,256,768]{2,1,0:T(8,128)(2,1)} custom-call(bf16[4,256,768]{2,1,0:T(8,128)(2,1)} %copy.72.src), custom_call_target="tpu_custom_call" | custom-call | tf_op jit(solution)/shard_map/pallas_call | solution.py:412
  85.3 2.4 fusion.89
  89.9 7.1 %shard_map.153 = s32[8,4,128]{2,1,0:T(4,128)} custom-call(s32[4,128]{1,0:T(4,128)} %slice_convert_fusion.1.src), custom_call_target="tpu_custom_call" | custom-call | tf_op jit(solution)/shard_map/pallas_call | solution.py:412
  101.1 21.5 %shard_map.156 = bf16[8,128,384]{2,1,0:T(8,128)(2,1)} custom-call(bf16[8,128,384]{2,1,0:T(8,128)(2,1)} %copy.79.src), custom_call_target="tpu_custom_call" | custom-call | tf_op jit(solution)/shard_map/pallas_call | solution.py:412
  122.5 1.6 copy.80
  126.8 2.9 fusion.3
  129.7 2.3 fusion
  132.9 5.0 fusion.58
  138.9 11.0 %shard_map.157 = bf16[8,128,128]{2,1,0:T(8,128)(2,1)} custom-call(bf16[8,128,128]{2,1,0:T(8,128)(2,1)} %copy.82.src), custom_call_target="tpu_custom_call" | custom-call | tf_op jit(solution)/shard_map/pallas_call | solution.py:412
  151.0 2.6 convolution_convert_fusion.3.src
  153.6 12.5 %shard_map.158 = bf16[4,128,1024]{2,1,0:T(8,128)(2,1)} custom-call(bf16[4,128,1024]{2,1,0:T(8,128)(2,1)} %convolution_convert_fusion.3.src), custom_call_target="tpu_custom_call" | custom-call | tf_op jit(solution)/shard_map/pallas_call | solution.py:412
  166.1 1.5 convert_reduce_fusion.3
  170.1 1.9 collective-permute-start.5
  172.0 17.7 %shard_map.159 = bf16[4,128,1024]{2,1,0:T(8,128)(2,1)} custom-call(bf16[128,1024]{1,0:T(8,128)(2,1)} %multiply_convert_fusion.3.src), custom_call_target="tpu_custom_call" | custom-call | tf_op jit(solution)/shard_map/pallas_call | solution.py:412
  189.7 2.2 copy.98
  192.0 2.3 pad_maximum_fusion.2
  194.3 2.8 gather_fusion.1
  197.1 3.0 pad_maximum_fusion
  200.0 4.0 gather_fusion
  204.0 5.3 copy.86
  209.4 5.9 reshape.562
  215.2 3.8 fusion.90
  219.0 4.5 add_convert_fusion
  225.3 2.8 convolution_convert_fusion.1.src
  228.1 3.9 bitcast_convert_fusion
  232.0 1.9 fusion.10
  233.9 2.0 convolution_convert_fusion.2.src
  235.9 14.1 %shard_map.161 = bf16[4,128,1024]{2,1,0:T(8,128)(2,1)} custom-call(bf16[4,128,1024]{2,1,0:T(8,128)(2,1)} %convolution_convert_fusion.1.src), custom_call_target="tpu_custom_call" | custom-call | tf_op jit(solution)/shard_map/pallas_call | solution.py:412
  250.0 1.5 convert_reduce_fusion.1
  251.8 2.0 add_convert_fusion.1.src
  253.7 14.1 %shard_map.162 = bf16[4,128,1024]{2,1,0:T(8,128)(2,1)} custom-call(bf16[128,1024]{1,0:T(8,128)(2,1)} %add_convert_fusion.1.src), custom_call_target="tpu_custom_call" | custom-call | tf_op jit(solution)/shard_map/pallas_call | solution.py:412
  267.8 1.7 convolution_convert_fusion.4
  270.3 10.8 %shard_map.163 = bf16[8,128,128]{2,1,0:T(8,128)(2,1)} custom-call(bf16[8,128,128]{2,1,0:T(8,128)(2,1)} %bitcast.324), custom_call_target="tpu_custom_call" | custom-call | tf_op jit(solution)/shard_map/pallas_call | solution.py:412
  282.5 6.2 fusion.26
  288.7 5.8 multiply_convert_fusion
  299.7 21.1 %shard_map.164 = bf16[8,128,384]{2,1,0:T(8,128)(2,1)} custom-call(bf16[8,128,384]{2,1,0:T(8,128)(2,1)} %copy.92.src), custom_call_target="tpu_custom_call" | custom-call | tf_op jit(solution)/shard_map/pallas_call | solution.py:412
  320.8 1.5 copy.93
  323.7 2.0 convolution_convert_fusion.src
  325.7 12.5 %shard_map.165 = bf16[4,128,1024]{2,1,0:T(8,128)(2,1)} custom-call(bf16[4,128,1024]{2,1,0:T(8,128)(2,1)} %convolution_convert_fusion.src), custom_call_target="tpu_custom_call" | custom-call | tf_op jit(solution)/shard_map/pallas_call | solution.py:412
  338.3 1.5 convert_reduce_fusion
  340.6 5.5 shard_map.167
  347.4 7.8 %shard_map.168 = f32[8,2,256]{2,1,0:T(2,128)} custom-call(f32[2,256]{1,0:T(2,128)} %reduce_sum.190.src), custom_call_target="tpu_custom_call" | custom-call | tf_op jit(solution)/shard_map/pallas_call | solution.py:412
  356.5 4.5 copy.101
  361.0 3.8 copy.102
  369.2 191.4 %shard_map.166 = (bf16[8,256,128]{2,1,0:T(8,128)(2,1)S(1)}, bf16[8,656,128]{2,1,0:T(8,128)(2,1)S(1)}, bf16[8,128,768]{2,1,0:T(8,128)(2,1)S(1)}, bf16[8,128,1312]{2,1,0:T(8,128)(2,1)}) custom-call(bf16[8,256,128]{2,1,0:T(8,128)(2,1)S(1)} %fusion.21.refs_0_, bf16[8,656,128]{2,1,0:T(8,128)(2,1)S(1)} %bitcast.291, bf16[8,128,768]{2,1,0:T(8,128)(2,1)} %bitcast.299, ...), custom_call_target="tpu_custom_call" | custom-call | tf_op jit(solution)/shard_map/pallas_call | solution.py:568
  560.7 9.3 %reshape.543 = f32[8,4,32,2,656]{4,3,2,1,0:T(2,128)} reshape(bf16[8,128,1312]{2,1,0:T(8,128)(2,1)} %get-tuple-element.14) | data formatting | bytes 8060928 | tf_op jit(solution)/shard_map/convert_element_type | solution.py:755
  570.0 9.5 %copy.105 = f32[8,32,2,4,656]{4,3,2,1,0:T(4,128)} copy(f32[8,32,2,4,656]{4,2,1,3,0:T(2,128)} %bitcast.292) | data formatting | bytes 10747904 | tf_op jit(solution)/shard_map/convert_element_type | solution.py:755
  579.5 8.1 %reshape.540 = f32[256,5248]{1,0:T(8,128)} reshape(f32[8,32,2,4,656]{4,3,2,1,0:T(4,128)} %copy.105) | data formatting | bytes 10747904 | tf_op jit(solution)/shard_map/convert_element_type | solution.py:755
  587.5 3.3 reshape.542
  590.8 5.9 copy.103
  596.7 5.1 reshape.538
  603.2 2.5 copy.107
  605.7 1.9 copy_bitcast_fusion
  607.6 12.5 %shard_map.160 = bf16[4,128,1024]{2,1,0:T(8,128)(2,1)} custom-call(bf16[4,128,1024]{2,1,0:T(8,128)(2,1)} %convolution_convert_fusion.2.src), custom_call_target="tpu_custom_call" | custom-call | tf_op jit(solution)/shard_map/pallas_call | solution.py:412
  620.2 1.6 convert_reduce_fusion.2
  621.8 2.1 fusion.47
  (147 shorter events, 39.5 us)
Async XLA Ops:
  0.6 218.4 %copy-start = (bf16[656,1024]{1,0:T(8,128)(2,1)S(1)}, bf16[656,1024]{1,0:T(8,128)(2,1)}, u32[]{:S(2)}) copy-start(bf16[656,1024]{1,0:T(8,128)(2,1)} %param.14) | copy-start | bytes 4030468
  0.6 169.5 %collective-permute-start.3 = (bf16[128,1024]{1,0:T(8,128)(2,1)}, bf16[128,1024]{1,0:T(8,128)(2,1)}, u32[]{:S(2)}, u32[]{:S(2)}) collective-permute-start(bf16[128,1024]{1,0:T(8,128)(2,1)} %bitcast.49), channel_id=1, source_target_pairs={{0,1},{1,0},{2,3},{3,2},{4,5},{5,4},{6,7},{7,6},{8,9},{9,8},{10,11... | collective-permute-start | bytes 786440 | tf_op jit(solution)/shard_map/ppermute | solution.py:588
  0.7 191.2 %collective-permute-start.4 = (bf16[128,1024]{1,0:T(8,128)(2,1)}, bf16[128,1024]{1,0:T(8,128)(2,1)}, u32[]{:S(2)}, u32[]{:S(2)}) collective-permute-start(bf16[128,1024]{1,0:T(8,128)(2,1)} %bitcast.49), channel_id=1, source_target_pairs={{0,2},{1,3},{2,0},{3,1},{4,6},{5,7},{6,4},{7,5},{8,10},{9,11},{10,... | collective-permute-start | bytes 786440 | tf_op jit(solution)/shard_map/ppermute | solution.py:588
  6.8 5.2 copy-start.26
  6.8 5.2 copy-start.27
  6.8 5.2 copy-start.28
  6.8 37.0 %copy-start.2 = (bf16[1,128,1024]{2,1,0:T(8,128)(2,1)S(1)}, bf16[1,128,1024]{2,1,0:T(8,128)(2,1)}, u32[]{:S(2)}) copy-start(bf16[1,128,1024]{2,1,0:T(8,128)(2,1)} %param.9) | copy-start | bytes 786436
  10.1 187.0 %collective-permute-start = (bf16[256,2,656]{0,2,1:T(8,128)(2,1)}, bf16[256,2,656]{0,2,1:T(8,128)(2,1)}, u32[]{:S(2)}, u32[]{:S(2)}) collective-permute-start(bf16[256,2,656]{0,2,1:T(8,128)(2,1)} %get-tuple-element.47), channel_id=1, source_target_pairs={{0,1},{1,0},{2,3},{3,2},{4,5},{5,4},{6,7},{7,6},{8,9},{9,8},{10,11... | collective-permute-start | bytes 2015240 | tf_op jit(solution)/shard_map/ppermute | solution.py:588
  10.2 186.8 %collective-permute-start.1 = (bf16[256,2,656]{0,2,1:T(8,128)(2,1)}, bf16[256,2,656]{0,2,1:T(8,128)(2,1)}, u32[]{:S(2)}, u32[]{:S(2)}) collective-permute-start(bf16[256,2,656]{0,2,1:T(8,128)(2,1)} %get-tuple-element.46), channel_id=1, source_target_pairs={{0,2},{1,3},{2,0},{3,1},{4,6},{5,7},{6,4},{7,5},{8,10},{9,11},{10,... | collective-permute-start | bytes 2015240 | tf_op jit(solution)/shard_map/ppermute | solution.py:588
  10.8 186.3 %collective-permute-start.2 = (bf16[256,2,656]{0,2,1:T(8,128)(2,1)}, bf16[256,2,656]{0,2,1:T(8,128)(2,1)}, u32[]{:S(2)}, u32[]{:S(2)}) collective-permute-start(bf16[256,2,656]{0,2,1:T(8,128)(2,1)} %get-tuple-element.45), channel_id=1, source_target_pairs={{0,3},{1,2},{2,1},{3,0},{4,7},{5,6},{6,5},{7,4},{8,11},{9,10},{10,... | collective-permute-start | bytes 2015240 | tf_op jit(solution)/shard_map/ppermute | solution.py:588
  65.6 19.7 %copy-start.11 = (bf16[4,128,1024]{2,1,0:T(8,128)(2,1)S(1)}, bf16[4,128,1024]{2,1,0:T(8,128)(2,1)}, u32[]{:S(2)}) copy-start(bf16[4,128,1024]{2,1,0:T(8,128)(2,1)} %shard_map.154) | copy-start | bytes 3145732
  89.0 9.1 %copy-start.23 = (f32[1,4,128,4,32]{2,4,3,1,0:T(8,128)S(1)}, f32[1,4,128,4,32]{2,4,3,1,0:T(8,128)}, u32[]{:S(2)}) copy-start(f32[1,4,128,4,32]{2,4,3,1,0:T(8,128)} %get-tuple-element.58) | copy-start | bytes 786436
  129.7 3.2 copy-start.4
  151.0 15.1 %copy-start.19 = (bf16[4,128,2,128]{1,3,2,0:T(8,128)(2,1)}, bf16[4,128,2,128]{1,3,2,0:T(8,128)(2,1)S(1)}, u32[]{:S(2)}) copy-start(bf16[4,128,2,128]{1,3,2,0:T(8,128)(2,1)S(1)} %copy.83) | copy-start | bytes 786436
  167.6 2.5 copy-start.7
  170.1 21.9 %collective-permute-start.5 = (bf16[128,1024]{1,0:T(8,128)(2,1)}, bf16[128,1024]{1,0:T(8,128)(2,1)}, u32[]{:S(2)}, u32[]{:S(2)}) collective-permute-start(bf16[128,1024]{1,0:T(8,128)(2,1)} %bitcast.49), channel_id=1, source_target_pairs={{0,3},{1,2},{2,1},{3,0},{4,7},{5,6},{6,5},{7,4},{8,11},{9,10},{10,... | collective-permute-start | bytes 786440 | tf_op jit(solution)/shard_map/ppermute | solution.py:588
  215.2 3.8 copy-start.18
  223.5 1.8 copy-start.12
  225.3 2.8 copy-start.17
  251.5 16.3 %copy-start.5 = (f32[128,1024]{1,0:T(8,128)}, f32[128,1024]{1,0:T(8,128)S(1)}, u32[]{:S(2)}) copy-start(f32[128,1024]{1,0:T(8,128)S(1)} %convert_reduce_fusion.1) | copy-start | bytes 1572868
  251.7 16.1 %copy-start.24 = (bf16[256,1024]{1,0:T(8,128)(2,1)S(1)}, bf16[256,1024]{1,0:T(8,128)(2,1)}, u32[]{:S(2)}) copy-start(bf16[256,1024]{1,0:T(8,128)(2,1)} %param.12) | copy-start | bytes 1572868
  269.5 12.8 %copy-start.25 = (f32[2,1024,64]{1,2,0:T(8,128)S(1)}, f32[2,1024,64]{1,2,0:T(8,128)}, u32[]{:S(2)}) copy-start(f32[2,1024,64]{1,2,0:T(8,128)} %get-tuple-element.81) | copy-start | bytes 1572868
  282.5 6.2 copy-start.13
  296.8 1.0 copy-start.22
  322.3 1.4 copy-start.14
  339.7 21.3 %copy-start.9 = (f32[128,1024]{1,0:T(8,128)}, f32[128,1024]{1,0:T(8,128)S(1)}, u32[]{:S(2)}) copy-start(f32[128,1024]{1,0:T(8,128)S(1)} %convert_reduce_fusion) | copy-start | bytes 1572868
  361.0 3.8 copy-start.16
  361.0 3.8 copy-start.20
  364.9 1.2 copy-start.21
  367.1 1.9 copy-start.15
  607.6 14.2 %copy-start.3 = (bf16[1,128,1024]{2,1,0:T(8,128)(2,1)S(1)}, bf16[1,128,1024]{2,1,0:T(8,128)(2,1)}, u32[]{:S(2)}) copy-start(bf16[1,128,1024]{2,1,0:T(8,128)(2,1)} %param.9) | copy-start | bytes 786436
  607.6 14.2 %copy-start.6 = (f32[128,1024]{1,0:T(8,128)S(1)}, f32[128,1024]{1,0:T(8,128)}, u32[]{:S(2)}) copy-start(f32[128,1024]{1,0:T(8,128)} %copy-done.5) | copy-start | bytes 1572868
  607.6 14.2 %copy-start.8 = (f32[128,1024]{1,0:T(8,128)S(1)}, f32[128,1024]{1,0:T(8,128)}, u32[]{:S(2)}) copy-start(f32[128,1024]{1,0:T(8,128)} %copy-done.7) | copy-start | bytes 1572868
  607.6 14.2 %copy-start.10 = (f32[128,1024]{1,0:T(8,128)S(1)}, f32[128,1024]{1,0:T(8,128)}, u32[]{:S(2)}) copy-start(f32[128,1024]{1,0:T(8,128)} %copy-done.9) | copy-start | bytes 1572868
  620.2 3.8 copy-start.1

commit v2 on v1

--- a/solution.py
+++ b/solution.py
@@ -374,7 +374,10 @@
     return {"ctx": index}
 
 
-def exchange_kernel(size, group, spread, src, dst, send_sems, recv_sems, own_sem):
+def exchange_kernel(size, group, spreads, *refs):
+    count = len(spreads)
+    sources, targets = refs[:count], refs[count : 2 * count]
+    send_sems, recv_sems, own_sems = refs[2 * count :]
     if group:
         me = lax.axis_index("seq") * 2 + lax.axis_index("wsh")
         peer_of = group_peer
@@ -388,46 +391,181 @@
         )
     pl.semaphore_wait(barrier, size - 1)
     copies = []
-    for step in range(1, size):
-        peer = lax.rem(me + step, size)
-        copy = pltpu.make_async_remote_copy(
-            src_ref=src.at[peer] if spread else src,
-            dst_ref=dst.at[me],
-            send_sem=send_sems.at[step - 1],
-            recv_sem=recv_sems.at[step - 1],
-            device_id=peer_of(peer),
-            device_id_type=MESH,
-        )
-        copy.start()
-        copies.append(copy)
-    own = pltpu.make_async_copy(src.at[me] if spread else src, dst.at[me], own_sem)
-    own.start()
-    own.wait()
+    for index, spread in enumerate(spreads):
+        src, dst = sources[index], targets[index]
+        for step in range(1, size):
+            peer = lax.rem(me + step, size)
+            copy = pltpu.make_async_remote_copy(
+                src_ref=src.at[peer] if spread else src,
+                dst_ref=dst.at[me],
+                send_sem=send_sems.at[index, step - 1],
+                recv_sem=recv_sems.at[index, step - 1],
+                device_id=peer_of(peer),
+                device_id_type=MESH,
+            )
+            copy.start()
+            copies.append(copy)
+        own = pltpu.make_async_copy(src.at[me] if spread else src, dst.at[me], own_sems.at[index])
+        own.start()
+        copies.append(own)
     for copy in copies:
         copy.wait()
 
 
-def exchange(shard, size, group, spread, number):
-    shape = shard.shape if spread else (size,) + shard.shape
+def exchange(shards, size, group, spreads, number):
+    count = len(shards)
     return pl.pallas_call(
-        functools.partial(exchange_kernel, size, group, spread),
-        out_shape=jax.ShapeDtypeStruct(shape, shard.dtype),
-        in_specs=[pl.BlockSpec(memory_space=pl.ANY)],
-        out_specs=pl.BlockSpec(memory_space=pl.ANY),
+        functools.partial(exchange_kernel, size, group, spreads),
+        out_shape=[
+            jax.ShapeDtypeStruct(x.shape if spread else (size,) + x.shape, x.dtype)
+            for x, spread in zip(shards, spreads)
+        ],
+        in_specs=[pl.BlockSpec(memory_space=pl.ANY)] * count,
+        out_specs=[pl.BlockSpec(memory_space=pl.ANY)] * count,
         scratch_shapes=[
-            pltpu.SemaphoreType.DMA((size - 1,)),
-            pltpu.SemaphoreType.DMA((size - 1,)),
+            pltpu.SemaphoreType.DMA((count, size - 1)),
+            pltpu.SemaphoreType.DMA((count, size - 1)),
+            pltpu.SemaphoreType.DMA((count,)),
+        ],
+        compiler_params=pltpu.CompilerParams(collective_id=number, has_side_effects=True),
+    )(*shards)
+
+
+def square_places():
+    seq, wsh = lax.axis_index("seq"), lax.axis_index("wsh")
+    me = seq * 2 + wsh
+    sibling = seq * 2 + 1 - wsh
+    across = (1 - seq) * 2 + wsh
+    corner = (1 - seq) * 2 + 1 - wsh
+    return me, sibling, across, corner
+
+
+def greet(peers, peer_of):
+    barrier = pltpu.get_barrier_semaphore()
+    for peer in peers:
+        pl.semaphore_signal(barrier, inc=1, device_id=peer_of(peer), device_id_type=MESH)
+    pl.semaphore_wait(barrier, len(peers))
+
+
+def square_copy(source, target, sends, recvs, slot, peer):
+    copy = pltpu.make_async_remote_copy(
+        src_ref=source,
+        dst_ref=target,
+        send_sem=sends.at[slot],
+        recv_sem=recvs.at[slot],
+        device_id=group_peer(peer),
+        device_id_type=MESH,
+    )
+    copy.start()
+    return copy
+
+
+def square_gather_kernel(src, dst, sends, recvs, own_sem):
+    me, sibling, across, corner = square_places()
+    greet([sibling, across], group_peer)
+    far = square_copy(src, dst.at[me], sends, recvs, 0, across)
+    near = square_copy(src, dst.at[me], sends, recvs, 1, sibling)
+    own = pltpu.make_async_copy(src, dst.at[me], own_sem)
+    own.start()
+    far.wait()
+    onward = square_copy(dst.at[across], dst.at[across], sends, recvs, 2, sibling)
+    near.wait()
+    own.wait()
+    onward.wait()
+
+
+def square_gather(shard, number):
+    whole = pl.BlockSpec(memory_space=pltpu.VMEM)
+    return pl.pallas_call(
+        square_gather_kernel,
+        out_shape=jax.ShapeDtypeStruct((4,) + shard.shape, shard.dtype),
+        in_specs=[whole],
+        out_specs=whole,
+        scratch_shapes=[
+            pltpu.SemaphoreType.DMA((3,)),
+            pltpu.SemaphoreType.DMA((3,)),
             pltpu.SemaphoreType.DMA,
         ],
-        compiler_params=pltpu.CompilerParams(collective_id=number, has_side_effects=True),
+        compiler_params=pltpu.CompilerParams(
+            collective_id=number, has_side_effects=True, vmem_limit_bytes=32 * 1024 * 1024
+        ),
     )(shard)
+
+
+def square_sum_kernel(src, out, held, sends, recvs):
+    wide = jnp.float32
+    rows = src.shape[1]
+    block = 32 if rows % 32 == 0 else 16
+    me, sibling, across, corner = square_places()
+    greet([sibling, across], group_peer)
+    first = square_copy(src.at[corner], held.at[0], sends, recvs, 0, sibling)
+    near = square_copy(src.at[sibling], held.at[1], sends, recvs, 1, sibling)
+    first.wait()
+
+    def join(index, carry):
+        at = pl.ds(pl.multiple_of(index * block, block), block)
+        held[2, at, :] = (src[across, at, :].astype(wide) + held[0, at, :].astype(wide)).astype(
+            held.dtype
+        )
+        return carry
+
+    lax.fori_loop(0, rows // block, join, 0)
+    far = square_copy(held.at[2], held.at[3], sends, recvs, 2, across)
+    near.wait()
+    far.wait()
+
+    def finish(index, carry):
+        at = pl.ds(pl.multiple_of(index * block, block), block)
+        out[at, :] = (
+            src[me, at, :].astype(wide) + held[1, at, :].astype(wide) + held[3, at, :].astype(wide)
+        )
+        return carry
+
+    lax.fori_loop(0, rows // block, finish, 0)
+
+
+def square_sum(terms, number):
+    whole = pl.BlockSpec(memory_space=pltpu.VMEM)
+    return pl.pallas_call(
+        square_sum_kernel,
+        out_shape=jax.ShapeDtypeStruct(terms.shape[1:], jnp.float32),
+        in_specs=[whole],
+        out_specs=whole,
+        scratch_shapes=[
+            pltpu.VMEM(terms.shape, terms.dtype),
+            pltpu.SemaphoreType.DMA((3,)),
+            pltpu.SemaphoreType.DMA((3,)),
+        ],
+        compiler_params=pltpu.CompilerParams(
+            collective_id=number, has_side_effects=True, vmem_limit_bytes=32 * 1024 * 1024
+        ),
+    )(terms)
+
+
+def rows_kernel(parts, pieces, grad, out):
+    rows = out.shape[0]
+    width = grad.shape[-1] // pieces
+    for piece in range(pieces):
+        for part in range(parts):
+            start = (piece * parts + part) * width
+            out[:, start : start + width] = grad[
+                0, part * rows : (part + 1) * rows, piece * width : (piece + 1) * width
+            ].astype(out.dtype)
+
+
+def columns_kernel(grad, out):
+    out[...] = grad[0].astype(out.dtype)
 
 
 def reduce_kernel(turns, size, count, *refs):
     low, wide = jnp.bfloat16, jnp.float32
+    refs = list(refs)
+    gains = refs.pop(count)
+    gain_out = refs.pop(2 * count)
     grads, outs = refs[:count], refs[count : 2 * count]
     from_y, from_z, total = (refs[(2 + i) * count : (3 + i) * count] for i in range(3))
     sends, recvs = refs[5 * count : 5 * count + 2]
+    gain_in, gain_all, gain_sends, gain_recvs = refs[5 * count + 2 :]
     depth = size // 2
     parts = 4
     me = lax.axis_index("ctx")
@@ -437,15 +575,13 @@
     z_peers = [lax.rem(place + step, depth) for step in range(1, depth)]
     x_peers = [lax.rem(group_me + step, parts) for step in range(1, parts)]
 
+    ctx_peers = [lax.rem(me + step, size) for step in range(1, size)]
     barrier = pltpu.get_barrier_semaphore()
-    pl.semaphore_signal(barrier, inc=1, device_id=ctx_peer(across), device_id_type=MESH)
-    for peer in z_peers:
-        pl.semaphore_signal(
-            barrier, inc=1, device_id=ctx_peer(peer * 2 + side), device_id_type=MESH
-        )
+    for peer in ctx_peers:
+        pl.semaphore_signal(barrier, inc=1, device_id=ctx_peer(peer), device_id_type=MESH)
     for peer in x_peers:
         pl.semaphore_signal(barrier, inc=1, device_id=group_peer(peer), device_id_type=MESH)
-    pl.semaphore_wait(barrier, 1 + len(z_peers) + len(x_peers))
+    pl.semaphore_wait(barrier, len(ctx_peers) + len(x_peers))
 
     def remote(chunk, slot, source, target, device):
         copy = pltpu.make_async_remote_copy(
@@ -547,18 +683,56 @@
                 remote(c, yg_slot + step, outs[c].at[came], outs[c].at[came], ctx_peer(across))
             )
 
+    gain_copies = []
+    for i, peer in enumerate(x_peers):
+        gain_copies.append(
+            pltpu.make_async_remote_copy(
+                src_ref=gains.at[peer],
+                dst_ref=gain_in.at[group_me],
+                send_sem=gain_sends.at[i],
+                recv_sem=gain_recvs.at[i],
+                device_id=group_peer(peer),
+                device_id_type=MESH,
+            )
+        )
+        gain_copies[-1].start()
     for c in range(count):
         start_y(c)
+    for copy in gain_copies:
+        copy.wait()
+    summed = gains[group_me]
+    for peer in x_peers:
+        summed = summed + gain_in[peer]
+    gain_all[me] = summed
+    gain_copies = []
+    for i, peer in enumerate(ctx_peers):
+        gain_copies.append(
+            pltpu.make_async_remote_copy(
+                src_ref=gain_all.at[me],
+                dst_ref=gain_all.at[me],
+                send_sem=gain_sends.at[parts - 1 + i],
+                recv_sem=gain_recvs.at[parts - 1 + i],
+                device_id=ctx_peer(peer),
+                device_id_type=MESH,
+            )
+        )
+        gain_copies[-1].start()
     for turn in range(count + 3):
         for stage, back in ((start_z, 0), (start_x, 1), (start_zg, 2), (start_yg, 3)):
             if 0 <= turn - back < count:
                 stage(turn - back)
+    for copy in gain_copies:
+        copy.wait()
+    summed = gain_all[0]
+    for peer in range(1, size):
+        summed = summed + gain_all[peer]
+    gain_out[...] = summed
     for c in range(count):
         for copy in ygs[c]:
             copy.wait()
 
 
-def reduce_over_ctx(grads, turns, size, number):
+def reduce_over_ctx(grads, gains, turns, size, number):
     count = len(grads)
     depth = size // 2
     slots = depth + 2 * (depth - 1) + 3 + depth
@@ -567,17 +741,25 @@
     totals = [pltpu.VMEM(g.shape[1:], g.dtype) for g in grads]
     return pl.pallas_call(
         functools.partial(reduce_kernel, turns, size, count),
-        out_shape=[jax.ShapeDtypeStruct(g.shape, g.dtype) for g in grads],
-        in_specs=[whole] * count,
-        out_specs=[whole] * count,
+        out_shape=[jax.ShapeDtypeStruct(g.shape, g.dtype) for g in grads]
+        + [jax.ShapeDtypeStruct(gains.shape[1:], gains.dtype)],
+        in_specs=[whole] * (count + 1),
+        out_specs=[whole] * (count + 1),
         scratch_shapes=pairs
         + pairs
         + totals
-        + [pltpu.SemaphoreType.DMA((count, slots)), pltpu.SemaphoreType.DMA((count, slots))],
+        + [
+            pltpu.SemaphoreType.DMA((count, slots)),
+            pltpu.SemaphoreType.DMA((count, slots)),
+            pltpu.VMEM(gains.shape, gains.dtype),
+            pltpu.VMEM((size,) + gains.shape[1:], gains.dtype),
+            pltpu.SemaphoreType.DMA((size + 2,)),
+            pltpu.SemaphoreType.DMA((size + 2,)),
+        ],
         compiler_params=pltpu.CompilerParams(
             collective_id=number, has_side_effects=True, vmem_limit_bytes=48 * 1024 * 1024
         ),
-    )(*grads)
+    )(*grads, gains)
 
 
 def permute_group(chunk_for, parts):
@@ -586,8 +768,7 @@
     for step in range(1, parts):
         pairs = [(i, i ^ step) for i in range(parts)]
         came.append(lax.ppermute(chunk_for(me ^ step), GROUP, pairs))
-    order = jnp.arange(parts) ^ me
-    return jnp.stack(came)[order]
+    return came
 
 
 def layer_norm_parts(values):
@@ -625,28 +806,33 @@
     scaling = HEAD ** (-0.5)
     ctx_index = lax.axis_index("ctx")
 
-    def gather(shard, number):
-        return exchange(shard, parts, True, False, number)
-
-    def swap(shard, number):
-        return exchange(shard, parts, True, True, number)
+    gather = square_gather
 
     def swap_ctx(shard, number):
-        return exchange(shard, ctx_size, False, True, number)
-
-    def gather_ctx(shard, number):
-        return exchange(shard, ctx_size, False, False, number)
+        return exchange([shard], ctx_size, False, (True,), number)[0]
 
     inputs = tokens[0].astype(wide)
     cot = cotangent[0]
     small = jnp.concatenate(
         [positions[0].astype(wide), gain_attn.astype(wide), gain_mlp.astype(wide)]
     )
-    small = gather(small.reshape(-1, 128), 25).reshape(parts, -1)
+    qkv_split = w_qkv.reshape(part_d, 3, parts, part_d).transpose(2, 0, 1, 3)
+    small, all_tokens, qkv_cols = exchange(
+        [small.reshape(-1, 128), tokens[0], qkv_split.reshape(parts, part_d, 3 * part_d)],
+        parts,
+        True,
+        (False, False, True),
+        1,
+    )
+    small = small.reshape(parts, -1)
+    qkv_cols = qkv_cols.reshape(D, 3 * part_d)
+    w_in, cot_sent, small = lax.optimization_barrier((w_in, cot, small))
     gain_one = small[:, row_count : row_count + part_d].reshape(D)
     gain_two = small[:, row_count + part_d :].reshape(D)
     all_positions = (
-        gather_ctx(small[:, :row_count].astype(jnp.int32), 26).transpose(1, 0, 2).reshape(parts, length)
+        exchange([small[:, :row_count].astype(jnp.int32)], ctx_size, False, (False,), 26)[0]
+        .transpose(1, 0, 2)
+        .reshape(parts, length)
     )
     starts = jnp.arange(length, dtype=jnp.int32)[None, :] - all_positions
     group_positions = lax.dynamic_slice_in_dim(all_positions, ctx_index * row_count, row_count, 1)
@@ -654,17 +840,21 @@
     seq_positions = lax.dynamic_index_in_dim(all_positions, my_seq, 0, False)
     seq_starts = lax.dynamic_index_in_dim(starts, my_seq, 0, False)
 
-    in_split = w_in.reshape(part_d, 2, parts, part_ff)
-    in_cols = permute_group(
-        lambda peer: lax.dynamic_index_in_dim(in_split, peer, 2, False), parts
-    ).reshape(D, 2 * part_ff)
-    all_cot = permute_group(lambda peer: cot, parts)
-    qkv_cols = swap(
-        w_qkv.reshape(part_d, 3, parts, part_d).transpose(2, 0, 1, 3).reshape(parts, part_d, 3 * part_d),
-        1,
-    ).reshape(D, 3 * part_d)
+    relative = jnp.arange(parts) ^ lax.axis_index(GROUP)
+
+    def in_chunk(peer):
+        return jnp.concatenate(
+            [
+                lax.dynamic_slice_in_dim(w_in, half_at + peer * part_ff, part_ff, 1)
+                for half_at in (0, FF)
+            ],
+            1,
+        )
+
+    in_cols = jnp.concatenate(permute_group(in_chunk, parts))
+    all_cot = jnp.stack(permute_group(lambda peer: cot_sent, parts))[relative]
     norm_one, factor_one = layer_norm_parts(inputs)
-    normed_attn = gather((norm_one * gain_one).astype(low), 2)
+    normed_attn = (layer_norm_parts(all_tokens.astype(wide))[0] * gain_one).astype(low)
     projected = dot("stc,cf->stf", normed_attn, qkv_cols)
     cosine, sine = rotary_tables(group_positions)
     turned = [
@@ -707,19 +897,20 @@
         )
 
     attended_low = from_ctx(swap_ctx(to_tokens(attended.astype(low), HEAD), 4))
-    branch = swap(dot("stc,cf->stf", attended_low, w_out).astype(low), 5)
-    mixed = inputs + jnp.sum(branch.astype(wide), 0)
+    mixed = inputs + square_sum(dot("stc,cf->stf", attended_low, w_out).astype(low), 5)
     norm_two, factor_two = layer_norm_parts(mixed)
     normed_mlp = gather((norm_two * gain_two).astype(low), 6)
-    hidden = dot("stc,cf->stf", normed_mlp, in_cols)
+    turned_mlp = normed_mlp.reshape(parts, row_count, parts, part_d)[:, :, relative]
+    hidden = dot("stc,cf->stf", turned_mlp.reshape(normed_mlp.shape), in_cols)
     inner, gate = hidden[..., :part_ff], hidden[..., part_ff:]
     product, pull = jax.vjp(geglu, inner, gate)
     product = product.astype(low)
     grad_product = dot("stn,fn->stf", all_cot, w_down)
     grad_inner, grad_gate = pull(grad_product)
     grad_hidden = jnp.concatenate([grad_inner, grad_gate], -1).astype(low)
-    normed_back = swap(dot("stf,cf->stc", grad_hidden, in_cols).astype(low), 9)
-    grad_normed_mlp = jnp.sum(normed_back.astype(wide), 0)
+    normed_back = dot("stf,cf->stc", grad_hidden, in_cols).astype(low)
+    normed_back = normed_back.reshape(parts, row_count, parts, part_d)[:, :, relative]
+    grad_normed_mlp = square_sum(normed_back.reshape(normed_mlp.shape), 9)
     grad_gain_mlp = jnp.sum(grad_normed_mlp * norm_two, 0)
     grad_mixed = cot.astype(wide) + norm_back(grad_normed_mlp, gain_two, norm_two, factor_two)
     grad_branch = gather(grad_mixed.astype(low), 10)
@@ -731,8 +922,12 @@
     )
     grad_heads = swap_ctx(grad_out, 11).reshape(length, pairs, HEAD).transpose(1, 0, 2)
 
-    output_parts = swap(dot("stf,fn->stn", product, w_down).astype(low), 12)
-    output = (mixed + jnp.sum(output_parts.astype(wide), 0)).astype(low)
+    output_parts = dot("stf,fn->stn", product, w_down).astype(low)
+    output_parts, grad_branch = lax.optimization_barrier((output_parts, grad_branch))
+    output_parts = permute_group(
+        lambda peer: lax.dynamic_index_in_dim(output_parts, peer, 0, False), parts
+    )
+    output = (mixed + sum(part.astype(wide) for part in output_parts)).astype(low)
 
     def rows_of(grad, width):
         return (
@@ -747,16 +942,25 @@
         return grad.reshape(rows, ctx_size, D // ctx_size).transpose(1, 0, 2).astype(low)
 
     def back_to_rows(grad, pieces):
-        width = grad.shape[-1] // pieces
-        return (
-            grad.reshape(ctx_size, parts, part_d // ctx_size, pieces, width)
-            .transpose(0, 2, 3, 1, 4)
-            .reshape(part_d, -1)
-            .astype(wide)
-        )
+        rows = part_d // ctx_size
+        width = parts * grad.shape[-1]
+        return pl.pallas_call(
+            functools.partial(rows_kernel, parts, pieces),
+            grid=(ctx_size,),
+            out_shape=jax.ShapeDtypeStruct((part_d, width), wide),
+            in_specs=[pl.BlockSpec((1,) + grad.shape[1:], lambda i: (i, 0, 0))],
+            out_specs=pl.BlockSpec((rows, width), lambda i: (i, 0)),
+        )(grad)
 
     def back_to_columns(grad):
-        return grad.transpose(1, 0, 2).reshape(grad.shape[1], D).astype(wide)
+        rows, width = grad.shape[1:]
+        return pl.pallas_call(
+            columns_kernel,
+            grid=(ctx_size,),
+            out_shape=jax.ShapeDtypeStruct((rows, D), wide),
+            in_specs=[pl.BlockSpec((1, rows, width), lambda i: (i, 0, 0))],
+            out_specs=pl.BlockSpec((rows, width), lambda i: (0, i)),
+        )(grad)
 
     down_grad = columns_of(dot("stf,stn->fn", product, all_cot))
     in_grad = rows_of(dot("stc,stf->cf", normed_mlp, grad_hidden), 2 * part_ff)
@@ -784,8 +988,7 @@
         .transpose(0, 2, 3, 1, 4)
         .reshape(parts, row_count, 3 * part_d)
     )
-    attn_back = swap(dot("stf,cf->stc", grad_projected, qkv_cols).astype(low), 16)
-    grad_normed_attn = jnp.sum(attn_back.astype(wide), 0)
+    grad_normed_attn = square_sum(dot("stf,cf->stc", grad_projected, qkv_cols).astype(low), 16)
     grad_gain_attn = jnp.sum(grad_normed_attn * norm_one, 0)
     grad_tokens = (
         grad_mixed + norm_back(grad_normed_attn, gain_one, norm_one, factor_one)
@@ -793,12 +996,14 @@
 
     out_grad = columns_of(dot("stc,stf->cf", attended_low, grad_branch))
     qkv_grad = rows_of(dot("stc,stf->cf", normed_attn, grad_projected), 3 * part_d)
-    out_grad, down_grad, qkv_grad, in_grad = reduce_over_ctx(
-        [out_grad, down_grad, qkv_grad, in_grad], (False, False, True, True), ctx_size, 13
-    )
     gain_sums = jnp.stack([grad_gain_attn, grad_gain_mlp]).reshape(2, parts, part_d)
-    gain_sums = jnp.sum(swap(gain_sums.transpose(1, 0, 2), 27), 0)
-    gain_sums = jnp.sum(gather_ctx(gain_sums, 28), 0)
+    out_grad, down_grad, qkv_grad, in_grad, gain_sums = reduce_over_ctx(
+        [out_grad, down_grad, qkv_grad, in_grad],
+        gain_sums.transpose(1, 0, 2),
+        (False, False, True, True),
+        ctx_size,
+        13,
+    )
     return (
         output[None],
         grad_tokens[None],

time: 637 us -> 515 us (0.81)
  the two profiles are of different devices: /device:TPU:8 before, /device:TPU:24 now
where the time goes in v2:
time: 515 us; the launch traced here: 505 us
  Pallas kernels  367 us (71%)
  local copies, waits for them, and re-layouts  58.5 us (11%)
  matrix products  45.9 us (9%)
  other arithmetic  25.7 us (5%)
  starting transfers between devices  6.38 us (1%)
    pallas_call x1, Pallas kernels, reduce_over_ctx(): pl.pallas_call(functools.partial(reduce_kernel, turns, size, count), out_...  195 us
    pallas_call x6, Pallas kernels, exchange(): pl.pallas_call(functools.partial(exchange_kernel, size, group, spreads),...  98.6 us
    dot_general x18, matrix products, dot(): return jnp.einsum(equation, left, right, preferred_element_type=jnp.float32)  45.9 us
    pallas_call x3, Pallas kernels, square_sum(): pl.pallas_call(square_sum_kernel, out_shape=jax.ShapeDtypeStruct(terms.sh...  30.9 us
    pallas_call x2, Pallas kernels, square_gather(): pl.pallas_call(square_gather_kernel, out_shape=jax.ShapeDtypeStruct((4,)...  19.5 us
    pallas_call x2, Pallas kernels, back_to_rows(): pl.pallas_call(functools.partial(rows_kernel, parts, pieces), grid=(ctx_s...  12.6 us
    unnamed x71, local copies, waits for them, and re-layouts  11.3 us
    pallas_call x2, Pallas kernels, back_to_columns(): pl.pallas_call(columns_kernel, grid=(ctx_size,), out_shape=jax.ShapeDtype...  10.5 us
  transfers between devices with their start and end apart: 9, of which 0 were waited for; matrix products, arithmetic and copies ran while one was open for 17% of the time, Pallas kernels for 63%

profile of v2, /device:TPU:24, one launch (start us, length us, event | category | flops | bytes accessed | tf_op | source)
XLA Modules:
  0.0 505.4 jit_solution(5004046517559578064)
XLA Ops:
  2.7 2.6 copy.83
  5.3 1.5 copy.84
  6.8 1.6 copy.85.refs_2_
  9.0 30.7 %shard_map.152 = (f32[4,5,128]{2,1,0:T(8,128)}, bf16[4,128,1024]{2,1,0:T(8,128)(2,1)}, bf16[4,256,768]{2,1,0:T(8,128)(2,1)}) custom-call(f32[5,128]{1,0:T(8,128)} %maximum_bitcast_fusion.5.refs_0_, bf16[128,1024]{1,0:T(8,128)(2,1)} %bitcast.256, bf16[4,256,768]{2,1,0:T(8,128)(2,1)} %copy.85.refs_2_), custom_call_target="tpu_custom_call" | custom-call | tf_op jit(solution)/shard_map/pallas_call | solution.py:417
  40.5 1.9 collective-permute-start.5
  42.9 4.5 copy.100
  47.4 2.7 constant_dynamic-slice_fusion.7
  51.9 1.5 collective-permute-start.1
  56.1 1.1 fusion.38
  58.2 1.4 fusion.37
  59.5 6.9 %shard_map.153 = s32[8,4,128]{2,1,0:T(4,128)} custom-call(s32[4,128]{1,0:T(4,128)} %slice_convert_fusion.1.refs_0_), custom_call_target="tpu_custom_call" | custom-call | tf_op jit(solution)/shard_map/pallas_call | solution.py:417
  67.2 1.6 broadcast_compare_fusion
  72.5 1.2 copy.92.refs_0_
  73.7 19.8 %shard_map.154 = bf16[8,128,384]{2,1,0:T(8,128)(2,1)} custom-call(bf16[8,128,384]{2,1,0:T(8,128)(2,1)} %copy.92.refs_0_), custom_call_target="tpu_custom_call" | custom-call | tf_op jit(solution)/shard_map/pallas_call | solution.py:417
  93.6 1.7 copy.93
  95.3 1.2 reshape.363
  96.5 2.9 fusion.3
  99.5 2.3 fusion
  101.7 1.0 copy-done.6
  102.7 4.7 fusion.60
  108.4 9.4 %shard_map.155 = bf16[8,128,128]{2,1,0:T(8,128)(2,1)} custom-call(bf16[8,128,128]{2,1,0:T(8,128)(2,1)} %copy.95.refs_0_), custom_call_target="tpu_custom_call" | custom-call | tf_op jit(solution)/shard_map/pallas_call | solution.py:417
  117.8 1.1 copy.96
  119.4 10.3 %shard_map.156 = f32[128,1024]{1,0:T(8,128)S(1)} custom-call(bf16[4,128,1024]{2,1,0:T(8,128)(2,1)S(1)} %convolution_convert_fusion.3.src), custom_call_target="tpu_custom_call" | custom-call | tf_op jit(solution)/shard_map/pallas_call | solution.py:529
  131.8 9.9 %shard_map.157 = bf16[4,128,1024]{2,1,0:T(8,128)(2,1)S(1)} custom-call(bf16[128,1024]{1,0:T(8,128)(2,1)S(1)} %multiply_convert_fusion.3.src), custom_call_target="tpu_custom_call" | custom-call | tf_op jit(solution)/shard_map/pallas_call | solution.py:479
  141.8 1.1 copy.166
  142.8 2.8 gather_fusion
  145.6 2.3 copy.99
  147.9 2.2 copy.122
  150.2 2.2 pad_maximum_fusion.1
  152.4 2.9 gather_fusion.1
  155.3 4.3 fusion.36
  159.6 4.5 add_convert_fusion
  164.4 2.0 convolution_convert_fusion.2
  166.3 1.9 fusion.15
  168.3 3.8 bitcast_convert_fusion
  172.0 3.3 convolution_convert_fusion.1
  176.2 10.3 %shard_map.158 = f32[128,1024]{1,0:T(8,128)S(1)} custom-call(bf16[4,128,1024]{2,1,0:T(8,128)(2,1)S(1)} %bitcast.253), custom_call_target="tpu_custom_call" | custom-call | tf_op jit(solution)/shard_map/pallas_call | solution.py:529
  186.8 2.1 fusion.88
  188.9 9.6 %shard_map.159 = bf16[4,128,1024]{2,1,0:T(8,128)(2,1)S(1)} custom-call(bf16[128,1024]{1,0:T(8,128)(2,1)S(1)} %get-tuple-element.40.src), custom_call_target="tpu_custom_call" | custom-call | tf_op jit(solution)/shard_map/pallas_call | solution.py:479
  199.9 1.0 collective-permute-start.8
  200.9 1.0 collective-permute-start.7
  202.6 11.0 %shard_map.160 = bf16[8,128,128]{2,1,0:T(8,128)(2,1)} custom-call(bf16[8,128,128]{2,1,0:T(8,128)(2,1)} %bitcast.286), custom_call_target="tpu_custom_call" | custom-call | tf_op jit(solution)/shard_map/pallas_call | solution.py:417
  213.6 1.1 copy.111
  215.6 6.3 %fusion.31 = bf16[1,2,1024,64]{2,3,1,0:T(8,128)(2,1)S(1)} fusion(f32[2,1024,1024]{1,2,0:T(8,128)} %copy-done.6, f32[2,1024]{1,0:T(2,128)S(1)} %log_add_fusion, pred[1024,1024]{0,1:T(8,128)(4,1)S(1)} %copy-done.11, bf16[1024,2,64]{0,2,1:T(8,128)(2,1)} %reshape.372), kind=kOutput, calls=%fused_computation.62 | convolution fusion | flops 279052288 | bytes 9969664 | tf_op jit(solution)/shard_map/hqk,hqd->hkd/dot_general | solution.py:791
  222.0 5.6 %multiply_convert_fusion = bf16[2,1024,1024]{1,2,0:T(8,128)(2,1)S(1)} fusion(f32[2,1024,1024]{1,2,0:T(8,128)} %copy-done.6, f32[2,1024]{1,0:T(2,128)S(1)} %multiply_reduce_fusion.1, f32[2,1024]{1,0:T(2,128)S(1)} %log_add_fusion, pred[1024,1024]{0,1:T(8,128)(4,1)S(1)} %copy-done.11, bf16[1024,2,64]{0,2,1:T(8,128)(2,1)S(1)} %copy-done.21, ...), kind=kOutput, calls=%fused_computation.3 | convolution fusion | flops 283115520 | bytes 14172160 | tf_op jit(solution)/shard_map/hqd,hkd->hqk/dot_general | solution.py:791
  227.6 1.4 fusion.73
  231.4 1.4 copy.116.refs_0_
  232.7 20.7 %shard_map.161 = bf16[8,128,384]{2,1,0:T(8,128)(2,1)} custom-call(bf16[8,128,384]{2,1,0:T(8,128)(2,1)} %copy.116.refs_0_), custom_call_target="tpu_custom_call" | custom-call | tf_op jit(solution)/shard_map/pallas_call | solution.py:417
  253.4 1.5 copy.117
  255.0 1.3 copy-done.31
  256.4 1.0 convolution_convert_fusion.src
  257.4 10.3 %shard_map.162 = f32[128,1024]{1,0:T(8,128)S(1)} custom-call(bf16[4,128,1024]{2,1,0:T(8,128)(2,1)S(1)} %convolution_convert_fusion.src), custom_call_target="tpu_custom_call" | custom-call | tf_op jit(solution)/shard_map/pallas_call | solution.py:529
  269.0 1.0 fusion.96
  270.0 1.3 copy.163
  271.3 4.7 copy.125
  276.0 3.8 copy.126
  280.2 194.9 %shard_map.163 = (bf16[8,256,128]{2,1,0:T(8,128)(2,1)S(1)}, bf16[8,656,128]{2,1,0:T(8,128)(2,1)S(1)}, bf16[8,128,768]{2,1,0:T(8,128)(2,1)S(1)}, bf16[8,128,1312]{2,1,0:T(8,128)(2,1)}, f32[2,256]{1,0:T(2,128)S(1)}) custom-call(bf16[8,256,128]{2,1,0:T(8,128)(2,1)S(1)} %fusion.26.refs_0_, bf16[8,656,128]{2,1,0:T(8,128)(2,1)S(1)} %bitcast.251, ...), custom_call_target="tpu_custom_call" | custom-call | tf_op jit(solution)/shard_map/pallas_call | solution.py:742
  475.2 1.1 copy-done.2
  476.3 1.1 copy-done.3
  478.2 5.7 %shard_map.164 = f32[256,3072]{1,0:T(8,128)} custom-call(bf16[8,128,768]{2,1,0:T(8,128)(2,1)} %copy-done.2), custom_call_target="tpu_custom_call" | custom-call | tf_op jit(solution)/shard_map/pallas_call | solution.py:947
  483.9 4.9 shard_map.165
  488.8 6.8 %shard_map.166 = f32[256,5248]{1,0:T(8,128)} custom-call(bf16[8,128,1312]{2,1,0:T(8,128)(2,1)} %get-tuple-element.31.grad), custom_call_target="tpu_custom_call" | custom-call | tf_op jit(solution)/shard_map/pallas_call | solution.py:947
  495.6 5.7 %shard_map.167 = f32[656,1024]{1,0:T(8,128)} custom-call(bf16[8,656,128]{2,1,0:T(8,128)(2,1)} %copy-done.3), custom_call_target="tpu_custom_call" | custom-call | tf_op jit(solution)/shard_map/pallas_call | solution.py:957
  502.9 2.1 fusion.65
  (152 shorter events, 28.2 us)
Async XLA Ops:
  0.6 158.9 %copy-start = (bf16[656,1024]{1,0:T(8,128)(2,1)S(1)}, bf16[656,1024]{1,0:T(8,128)(2,1)}, u32[]{:S(2)}) copy-start(bf16[656,1024]{1,0:T(8,128)(2,1)} %param.14) | copy-start | bytes 4030468
  40.5 91.3 %collective-permute-start.5 = (bf16[128,1024]{1,0:T(8,128)(2,1)}, bf16[128,1024]{1,0:T(8,128)(2,1)}, u32[]{:S(2)}, u32[]{:S(2)}) collective-permute-start(bf16[128,1024]{1,0:T(8,128)(2,1)} %bitcast.1), channel_id=1, source_target_pairs={{0,3},{1,2},{2,1},{3,0},{4,7},{5,6},{6,5},{7,4},{8,11},{9,10},{10,... | collective-permute-start | bytes 786440 | tf_op jit(solution)/shard_map/ppermute | solution.py:770
  42.4 107.8 %collective-permute-start.4 = (bf16[128,1024]{1,0:T(8,128)(2,1)}, bf16[128,1024]{1,0:T(8,128)(2,1)}, u32[]{:S(2)}, u32[]{:S(2)}) collective-permute-start(bf16[128,1024]{1,0:T(8,128)(2,1)} %bitcast.1), channel_id=1, source_target_pairs={{0,2},{1,3},{2,0},{3,1},{4,6},{5,7},{6,4},{7,5},{8,10},{9,11},{10,... | collective-permute-start | bytes 786440 | tf_op jit(solution)/shard_map/ppermute | solution.py:770
  51.0 4.3 copy-start.5
  51.0 104.3 %collective-permute-start.2 = (bf16[256,1312]{0,1:T(8,128)(2,1)}, bf16[256,1312]{0,1:T(8,128)(2,1)}, u32[]{:S(2)}, u32[]{:S(2)}) collective-permute-start(bf16[256,1312]{0,1:T(8,128)(2,1)} %pad_maximum_fusion.7), channel_id=1, source_target_pairs={{0,3},{1,2},{2,1},{3,0},{4,7},{5,6},{6,5},{7,4},{8,11},{9,10},{10,... | collective-permute-start | bytes 2015240 | tf_op jit(solution)/shard_map/ppermute | solution.py:770
  51.9 103.4 %collective-permute-start.1 = (bf16[256,1312]{0,1:T(8,128)(2,1)}, bf16[256,1312]{0,1:T(8,128)(2,1)}, u32[]{:S(2)}, u32[]{:S(2)}) collective-permute-start(bf16[256,1312]{0,1:T(8,128)(2,1)} %pad_maximum_fusion.6), channel_id=1, source_target_pairs={{0,2},{1,3},{2,0},{3,1},{4,6},{5,7},{6,4},{7,5},{8,10},{9,11},{10,... | collective-permute-start | bytes 2015240 | tf_op jit(solution)/shard_map/ppermute | solution.py:770
  54.3 101.0 %collective-permute-start = (bf16[256,1312]{0,1:T(8,128)(2,1)}, bf16[256,1312]{0,1:T(8,128)(2,1)}, u32[]{:S(2)}, u32[]{:S(2)}) collective-permute-start(bf16[256,1312]{0,1:T(8,128)(2,1)} %pad_maximum_fusion.5), channel_id=1, source_target_pairs={{0,1},{1,0},{2,3},{3,2},{4,5},{5,4},{6,7},{7,6},{8,9},{9,8},{10,11... | collective-permute-start | bytes 2015240 | tf_op jit(solution)/shard_map/ppermute | solution.py:770
  54.6 1.4 copy-start.30
  57.1 1.0 copy-start.7
  59.5 10.8 %copy-start.16 = (f32[4,128,256]{2,1,0:T(8,128)S(1)}, f32[4,128,256]{2,1,0:T(8,128)}, u32[]{:S(2)}) copy-start(f32[4,128,256]{2,1,0:T(8,128)} %get-tuple-element.56) | copy-start | bytes 1572868
  71.4 1.0 copy-start.23
  93.6 3.0 copy-start.10
  99.5 3.3 copy-start.6
  107.4 11.5 %copy-start.25 = (bf16[256,1024]{1,0:T(8,128)(2,1)S(1)}, bf16[256,1024]{1,0:T(8,128)(2,1)}, u32[]{:S(2)}) copy-start(bf16[256,1024]{1,0:T(8,128)(2,1)} %param.12) | copy-start | bytes 1572868
  118.9 10.8 %copy-start.19 = (bf16[4,128,2,128]{1,3,2,0:T(8,128)(2,1)}, bf16[4,128,2,128]{1,3,2,0:T(8,128)(2,1)S(1)}, u32[]{:S(2)}) copy-start(bf16[4,128,2,128]{1,3,2,0:T(8,128)(2,1)S(1)} %copy.96) | copy-start | bytes 786436
  131.7 18.5 %collective-permute-start.3 = (bf16[128,1024]{1,0:T(8,128)(2,1)}, bf16[128,1024]{1,0:T(8,128)(2,1)S(1)}, u32[]{:S(2)}, u32[]{:S(2)}) collective-permute-start(bf16[128,1024]{1,0:T(8,128)(2,1)} %bitcast.1), channel_id=1, source_target_pairs={{0,1},{1,0},{2,3},{3,2},{4,5},{5,4},{6,7},{7,6},{8,9},{9,8},{10,11... | collective-permute-start | bytes 786440 | tf_op jit(solution)/shard_map/ppermute | solution.py:770
  152.4 2.9 copy-start.28
  155.3 4.3 copy-start.18
  168.3 3.8 copy-start.29
  186.8 11.7 %copy-start.26 = (bf16[256,1024]{1,0:T(8,128)(2,1)S(1)}, bf16[256,1024]{1,0:T(8,128)(2,1)}, u32[]{:S(2)}) copy-start(bf16[256,1024]{1,0:T(8,128)(2,1)} %param.12) | copy-start | bytes 1572868
  188.9 10.1 %copy-start.12 = (bf16[4,128,1024]{2,1,0:T(8,128)(2,1)S(1)}, bf16[4,128,1024]{2,1,0:T(8,128)(2,1)}, u32[]{:S(2)}) copy-start(bf16[4,128,1024]{2,1,0:T(8,128)(2,1)} %convolution_convert_fusion.2) | copy-start | bytes 3145732
  199.9 15.7 %copy-start.11 = (pred[1024,1024]{0,1:T(8,128)(4,1)S(1)}, pred[1024,1024]{0,1:T(8,128)(4,1)}, u32[]{:S(2)}) copy-start(pred[1024,1024]{0,1:T(8,128)(4,1)} %broadcast_compare_fusion) | copy-start | bytes 3145732
  199.9 303.0 %collective-permute-start.8 = (bf16[128,1024]{1,0:T(8,128)(2,1)}, bf16[128,1024]{1,0:T(8,128)(2,1)}, u32[]{:S(2)}, u32[]{:S(2)}) collective-permute-start(bf16[128,1024]{1,0:T(8,128)(2,1)} %get-tuple-element.59), channel_id=1, source_target_pairs={{0,3},{1,2},{2,1},{3,0},{4,7},{5,6},{6,5},{7,4},{8,11},{9,10},{10,... | collective-permute-start | bytes 786440 | tf_op jit(solution)/shard_map/ppermute | solution.py:770
  200.9 302.0 %collective-permute-start.7 = (bf16[128,1024]{1,0:T(8,128)(2,1)}, bf16[128,1024]{1,0:T(8,128)(2,1)}, u32[]{:S(2)}, u32[]{:S(2)}) collective-permute-start(bf16[128,1024]{1,0:T(8,128)(2,1)} %get-tuple-element.60), channel_id=1, source_target_pairs={{0,2},{1,3},{2,0},{3,1},{4,6},{5,7},{6,4},{7,5},{8,10},{9,11},{10,... | collective-permute-start | bytes 786440 | tf_op jit(solution)/shard_map/ppermute | solution.py:770
  201.9 301.0 %collective-permute-start.6 = (bf16[128,1024]{1,0:T(8,128)(2,1)}, bf16[128,1024]{1,0:T(8,128)(2,1)}, u32[]{:S(2)}, u32[]{:S(2)}) collective-permute-start(bf16[128,1024]{1,0:T(8,128)(2,1)} %get-tuple-element.58), channel_id=1, source_target_pairs={{0,1},{1,0},{2,3},{3,2},{4,5},{5,4},{6,7},{7,6},{8,9},{9,8},{10,11... | collective-permute-start | bytes 786440 | tf_op jit(solution)/shard_map/ppermute | solution.py:770
  215.6 6.3 %copy-start.21 = (bf16[1024,2,64]{0,2,1:T(8,128)(2,1)S(1)}, bf16[1024,2,64]{0,2,1:T(8,128)(2,1)}, u32[]{:S(2)}) copy-start(bf16[1024,2,64]{0,2,1:T(8,128)(2,1)} %reshape.372) | copy-start | bytes 786436
  215.6 6.3 %copy-start.27 = (f32[2,1024,64]{1,2,0:T(8,128)S(1)}, f32[2,1024,64]{1,2,0:T(8,128)}, u32[]{:S(2)}) copy-start(f32[2,1024,64]{1,2,0:T(8,128)} %get-tuple-element.91) | copy-start | bytes 1572868
  215.6 6.4 %copy-start.14 = (bf16[1024,3,2,64]{0,3,2,1:T(8,128)(2,1)S(1)}, bf16[1024,3,2,64]{0,3,2,1:T(8,128)(2,1)}, u32[]{:S(2)}) copy-start(bf16[1024,3,2,64]{0,3,2,1:T(8,128)(2,1)} %reshape.363) | copy-start | bytes 2359300
  227.6 1.4 copy-start.13
  229.9 1.0 copy-start.24
  255.0 1.4 copy-start.31
  257.4 10.3 %copy-start.8 = (bf16[1,128,1024]{2,1,0:T(8,128)(2,1)S(1)}, bf16[1,128,1024]{2,1,0:T(8,128)(2,1)}, u32[]{:S(2)}) copy-start(bf16[1,128,1024]{2,1,0:T(8,128)(2,1)} %param.9) | copy-start | bytes 786436
  257.4 10.6 %copy-start.17 = (bf16[82,8,8,128]{3,2,1,0:T(8,128)(2,1)S(1)}, bf16[82,8,8,128]{3,2,1,0:T(8,128)(2,1)}, u32[]{:S(2)}) copy-start(bf16[82,8,8,128]{3,2,1,0:T(8,128)(2,1)} %fusion.15) | copy-start | bytes 4030468
  267.7 1.2 copy-start.22
  276.0 3.8 copy-start.20
  475.2 1.1 copy-start.2
  476.3 1.1 copy-start.3
  477.4 0.8 copy-start.4
  495.6 6.2 %copy-start.9 = (bf16[1,128,1024]{2,1,0:T(8,128)(2,1)S(1)}, bf16[1,128,1024]{2,1,0:T(8,128)(2,1)}, u32[]{:S(2)}) copy-start(bf16[1,128,1024]{2,1,0:T(8,128)(2,1)} %param.9) | copy-start | bytes 786436
  495.6 6.2 %copy-start.15 = (f32[128,1024]{1,0:T(8,128)S(1)}, f32[128,1024]{1,0:T(8,128)}, u32[]{:S(2)}) copy-start(f32[128,1024]{1,0:T(8,128)} %get-tuple-element.41) | copy-start | bytes 1572868
  501.9 3.1 copy-start.1

commit v3 on v2

--- a/solution.py
+++ b/solution.py
@@ -542,22 +542,23 @@
     )(terms)
 
 
-def rows_kernel(parts, pieces, grad, out):
-    rows = out.shape[0]
-    width = grad.shape[-1] // pieces
-    for piece in range(pieces):
-        for part in range(parts):
-            start = (piece * parts + part) * width
-            out[:, start : start + width] = grad[
-                0, part * rows : (part + 1) * rows, piece * width : (piece + 1) * width
-            ].astype(out.dtype)
-
-
-def columns_kernel(grad, out):
-    out[...] = grad[0].astype(out.dtype)
-
-
-def reduce_kernel(turns, size, count, *refs):
+def place_kernel(parts, pieces, *refs):
+    count = len(pieces)
+    for count_of, grad, out in zip(pieces, refs[:count], refs[count:]):
+        if not count_of:
+            out[...] = grad[0].astype(out.dtype)
+            continue
+        rows = out.shape[0]
+        width = grad.shape[-1] // count_of
+        for piece in range(count_of):
+            for part in range(parts):
+                start = (piece * parts + part) * width
+                out[:, start : start + width] = grad[
+                    0, part * rows : (part + 1) * rows, piece * width : (piece + 1) * width
+                ].astype(out.dtype)
+
+
+def reduce_kernel(turns, ready, size, count, *refs):
     low, wide = jnp.bfloat16, jnp.float32
     refs = list(refs)
     gains = refs.pop(count)
@@ -636,11 +637,16 @@
         ]
 
     def start_x(c):
-        rows = total[c].shape[0]
-        for copy in zs[c]:
+        rows = outs[c].shape[1]
+        source = grads[c] if ready[c] else total[c]
+        for copy in zs.get(c, ()):
             copy.wait()
 
         def add(at):
+            if ready[c]:
+                if not turns[c]:
+                    outs[c][me, at, :] = grads[c][at, :]
+                return
             summed = from_y[c][place, at, :].astype(wide)
             for peer in z_peers:
                 summed = summed + from_z[c][peer, at, :].astype(wide)
@@ -649,21 +655,22 @@
             else:
                 outs[c][me, at, :] = summed.astype(low)
 
-        by_rows(rows, add)
+        if not (ready[c] and turns[c]):
+            by_rows(rows, add)
         if turns[c]:
             piece = rows // parts
             xs[c] = [
                 remote(
                     c,
                     x_slot + i,
-                    total[c].at[pl.ds(pl.multiple_of(peer * piece, piece), piece)],
+                    source.at[pl.ds(pl.multiple_of(peer * piece, piece), piece)],
                     outs[c].at[me, pl.ds(pl.multiple_of(group_me * piece, piece), piece)],
                     group_peer(peer),
                 )
                 for i, peer in enumerate(x_peers)
             ]
             mine = pl.ds(pl.multiple_of(group_me * piece, piece), piece)
-            outs[c][me, mine, :] = total[c][mine, :]
+            outs[c][me, mine, :] = source[mine, :]
 
     def start_zg(c):
         if turns[c]:
@@ -696,8 +703,13 @@
             )
         )
         gain_copies[-1].start()
-    for c in range(count):
+    late = [c for c in range(count) if not ready[c]]
+    early = [c for c in range(count) if ready[c]]
+    for c in late:
         start_y(c)
+    for c in early:
+        start_x(c)
+    start_zg(early[0])
     for copy in gain_copies:
         copy.wait()
     summed = gains[group_me]
@@ -717,10 +729,17 @@
             )
         )
         gain_copies[-1].start()
-    for turn in range(count + 3):
-        for stage, back in ((start_z, 0), (start_x, 1), (start_zg, 2), (start_yg, 3)):
-            if 0 <= turn - back < count:
-                stage(turn - back)
+    for c in late:
+        start_z(c)
+    for c in early[1:]:
+        start_zg(c)
+    for c in late:
+        start_x(c)
+    start_yg(early[0])
+    for c in late:
+        start_zg(c)
+    for c in early[1:] + late:
+        start_yg(c)
     for copy in gain_copies:
         copy.wait()
     summed = gain_all[0]
@@ -734,14 +753,17 @@
 
 def reduce_over_ctx(grads, gains, turns, size, number):
     count = len(grads)
+    ready = tuple(g.ndim == 2 for g in grads)
     depth = size // 2
     slots = depth + 2 * (depth - 1) + 3 + depth
     whole = pl.BlockSpec(memory_space=pltpu.VMEM)
-    pairs = [pltpu.VMEM((depth,) + g.shape[1:], g.dtype) for g in grads]
-    totals = [pltpu.VMEM(g.shape[1:], g.dtype) for g in grads]
+    pairs = [
+        pltpu.VMEM((1, 16, 128) if g.ndim == 2 else (depth,) + g.shape[1:], g.dtype) for g in grads
+    ]
+    totals = [pltpu.VMEM((16, 128) if g.ndim == 2 else g.shape[1:], g.dtype) for g in grads]
     return pl.pallas_call(
-        functools.partial(reduce_kernel, turns, size, count),
-        out_shape=[jax.ShapeDtypeStruct(g.shape, g.dtype) for g in grads]
+        functools.partial(reduce_kernel, turns, ready, size, count),
+        out_shape=[jax.ShapeDtypeStruct((size,) + g.shape[-2:], g.dtype) for g in grads]
         + [jax.ShapeDtypeStruct(gains.shape[1:], gains.dtype)],
         in_specs=[whole] * (count + 1),
         out_specs=[whole] * (count + 1),
@@ -941,29 +963,53 @@
         rows = grad.shape[0]
         return grad.reshape(rows, ctx_size, D // ctx_size).transpose(1, 0, 2).astype(low)
 
-    def back_to_rows(grad, pieces):
-        rows = part_d // ctx_size
-        width = parts * grad.shape[-1]
+    def place(grads, pieces):
+        specs, shapes = [], []
+        for grad, count_of in zip(grads, pieces):
+            rows, width = grad.shape[1:]
+            if count_of:
+                rows, width = part_d // ctx_size, parts * width
+                shapes.append((part_d, width))
+                specs.append(pl.BlockSpec((rows, width), lambda i: (i, 0)))
+            else:
+                shapes.append((rows, D))
+                specs.append(pl.BlockSpec((rows, width), lambda i: (0, i)))
         return pl.pallas_call(
-            functools.partial(rows_kernel, parts, pieces),
+            functools.partial(place_kernel, parts, pieces),
             grid=(ctx_size,),
-            out_shape=jax.ShapeDtypeStruct((part_d, width), wide),
-            in_specs=[pl.BlockSpec((1,) + grad.shape[1:], lambda i: (i, 0, 0))],
-            out_specs=pl.BlockSpec((rows, width), lambda i: (i, 0)),
-        )(grad)
-
-    def back_to_columns(grad):
-        rows, width = grad.shape[1:]
-        return pl.pallas_call(
-            columns_kernel,
-            grid=(ctx_size,),
-            out_shape=jax.ShapeDtypeStruct((rows, D), wide),
-            in_specs=[pl.BlockSpec((1, rows, width), lambda i: (i, 0, 0))],
-            out_specs=pl.BlockSpec((rows, width), lambda i: (0, i)),
-        )(grad)
-
-    down_grad = columns_of(dot("stf,stn->fn", product, all_cot))
-    in_grad = rows_of(dot("stc,stf->cf", normed_mlp, grad_hidden), 2 * part_ff)
+            out_shape=[jax.ShapeDtypeStruct(shape, wide) for shape in shapes],
+            in_specs=[pl.BlockSpec((1,) + g.shape[1:], lambda i: (i, 0, 0)) for g in grads],
+            out_specs=specs,
+            compiler_params=pltpu.CompilerParams(vmem_limit_bytes=32 * 1024 * 1024),
+        )(*grads)
+
+    depth = ctx_size // 2
+    place_z, side = ctx_index // 2, ctx_index % 2
+
+    def sum_sides(grad):
+        split = grad.reshape((depth, 2) + grad.shape[1:])
+        came = lax.ppermute(
+            lax.dynamic_index_in_dim(split, 1 - side, 1, False),
+            "ctx",
+            [(i, i ^ 1) for i in range(ctx_size)],
+        )
+        kept = lax.dynamic_index_in_dim(split, side, 1, False)
+        return (kept.astype(wide) + came.astype(wide)).astype(low)
+
+    def sum_depth(grad):
+        summed = lax.dynamic_index_in_dim(grad, place_z, 0, False).astype(wide)
+        for step in range(1, depth):
+            summed = summed + lax.ppermute(
+                lax.dynamic_index_in_dim(grad, place_z ^ step, 0, False),
+                "ctx",
+                [(i, i ^ (2 * step)) for i in range(ctx_size)],
+            ).astype(wide)
+        return summed.astype(low)
+
+    down_grad = sum_sides(columns_of(dot("stf,stn->fn", product, all_cot)))
+    in_grad = sum_sides(rows_of(dot("stc,stf->cf", normed_mlp, grad_hidden), 2 * part_ff))
+    down_grad = sum_depth(down_grad)
+    in_grad = sum_depth(in_grad)
 
     row_dot = jnp.sum(grad_heads.astype(wide) * attended, -1, keepdims=True)
     weights_f = jnp.where(same, jnp.exp(scores - log_total), 0.0)
@@ -982,6 +1028,7 @@
         ]
     ).astype(low)
     grads = grads.transpose(2, 0, 1, 3).reshape(ctx_size, row_count, 3 * pairs * HEAD)
+    down_grad, in_grad, grads = lax.optimization_barrier((down_grad, in_grad, grads))
     grads = swap_ctx(grads, 15)
     grad_projected = (
         grads.reshape(parts, seq_split, row_count, 3, pairs * HEAD)
@@ -997,20 +1044,23 @@
     out_grad = columns_of(dot("stc,stf->cf", attended_low, grad_branch))
     qkv_grad = rows_of(dot("stc,stf->cf", normed_attn, grad_projected), 3 * part_d)
     gain_sums = jnp.stack([grad_gain_attn, grad_gain_mlp]).reshape(2, parts, part_d)
-    out_grad, down_grad, qkv_grad, in_grad, gain_sums = reduce_over_ctx(
-        [out_grad, down_grad, qkv_grad, in_grad],
+    down_grad, in_grad, out_grad, qkv_grad, gain_sums = reduce_over_ctx(
+        [down_grad, in_grad, out_grad, qkv_grad],
         gain_sums.transpose(1, 0, 2),
-        (False, False, True, True),
+        (False, True, False, True),
         ctx_size,
         13,
+    )
+    qkv_grad, out_grad, in_grad, down_grad = place(
+        [qkv_grad, out_grad, in_grad, down_grad], (3, 0, 2, 0)
     )
     return (
         output[None],
         grad_tokens[None],
-        back_to_rows(qkv_grad, 3),
-        back_to_columns(out_grad),
-        back_to_rows(in_grad, 2),
-        back_to_columns(down_grad),
+        qkv_grad,
+        out_grad,
+        in_grad,
+        down_grad,
         gain_sums[0],
         gain_sums[1],
     )
@@ -1030,7 +1080,7 @@
     )
     parts = mesh.shape["seq"] * mesh.shape["wsh"]
     ctx_size = mesh.shape["ctx"]
-    whole_pairs = HEADS % ctx_size == 0 and ctx_size % 2 == 0 and parts == 4
+    whole_pairs = HEADS % ctx_size == 0 and ctx_size in (2, 4, 8, 16) and parts == 4
     body = functools.partial(parallel, parts, ctx_size) if whole_pairs else local
     return jax.shard_map(
         body,

time: 515 us -> 502 us (0.975)
  the two profiles are of different devices: /device:TPU:24 before, /device:TPU:8 now
where the time goes in v3:
time: 502 us; the launch traced here: 492 us
  Pallas kernels  302 us (60%)
  local copies, waits for them, and re-layouts  65.1 us (13%)
  matrix products  45.9 us (9%)
  other arithmetic  30.4 us (6%)
  waiting for transfers between devices  30.3 us (6%)
  starting transfers between devices  16.1 us (3%)
    pallas_call x6, Pallas kernels, exchange(): pl.pallas_call(functools.partial(exchange_kernel, size, group, spreads),...  123 us
    pallas_call x1, Pallas kernels, reduce_over_ctx(): pl.pallas_call(functools.partial(reduce_kernel, turns, ready, size, count...  123 us
    dot_general x18, matrix products, dot(): return jnp.einsum(equation, left, right, preferred_element_type=jnp.float32)  45.9 us
    pallas_call x3, Pallas kernels, square_sum(): pl.pallas_call(square_sum_kernel, out_shape=jax.ShapeDtypeStruct(terms.sh...  31.1 us
    ppermute x6, waiting for transfers between devices, sum_depth(): lax.ppermute(lax.dynamic_index_in_dim(grad, place_z ^ step, 0, False), 'c...  30.3 us
    pallas_call x2, Pallas kernels, square_gather(): pl.pallas_call(square_gather_kernel, out_shape=jax.ShapeDtypeStruct((4,)...  19.5 us
    unnamed x73, local copies, waits for them, and re-layouts  12.1 us
  transfers between devices with their start and end apart: 17, of which 4 were waited for; matrix products, arithmetic and copies ran while one was open for 19% of the time, Pallas kernels for 19%

profile of v3, /device:TPU:8, one launch (start us, length us, event | category | flops | bytes accessed | tf_op | source)
XLA Modules:
  0.0 491.9 jit_solution(7449277230229800448)
XLA Ops:
  2.7 2.6 copy.177
  5.3 1.5 copy.178
  6.8 1.6 copy.179.refs_2_
  9.0 30.7 %shard_map.152 = (f32[4,5,128]{2,1,0:T(8,128)}, bf16[4,128,1024]{2,1,0:T(8,128)(2,1)}, bf16[4,256,768]{2,1,0:T(8,128)(2,1)}) custom-call(f32[5,128]{1,0:T(8,128)} %maximum_bitcast_fusion.5.refs_0_, bf16[128,1024]{1,0:T(8,128)(2,1)} %bitcast.288, bf16[4,256,768]{2,1,0:T(8,128)(2,1)} %copy.179.refs_2_), custom_call_target="tpu_custom_call" | custom-call | tf_op jit(solution)/shard_map/pallas_call | solution.py:417
  40.5 1.9 collective-permute-start.5
  42.9 4.5 copy.194
  47.4 2.7 constant_dynamic-slice_fusion.8
  51.9 1.5 collective-permute-start.1
  58.4 1.4 fusion.42
  59.8 7.1 %shard_map.153 = s32[8,4,128]{2,1,0:T(4,128)} custom-call(s32[4,128]{1,0:T(4,128)} %slice_convert_fusion.1.refs_0_), custom_call_target="tpu_custom_call" | custom-call | tf_op jit(solution)/shard_map/pallas_call | solution.py:417
  67.6 1.6 broadcast_compare_fusion
  74.0 19.6 %shard_map.154 = bf16[8,128,384]{2,1,0:T(8,128)(2,1)} custom-call(bf16[8,128,384]{2,1,0:T(8,128)(2,1)} %copy.186.refs_0_), custom_call_target="tpu_custom_call" | custom-call | tf_op jit(solution)/shard_map/pallas_call | solution.py:417
  93.7 2.5 copy.187
  96.2 2.2 reshape.376
  98.4 2.9 fusion.3
  101.3 2.3 fusion
  104.6 4.7 fusion.65
  110.3 9.7 %shard_map.155 = bf16[8,128,128]{2,1,0:T(8,128)(2,1)} custom-call(bf16[8,128,128]{2,1,0:T(8,128)(2,1)} %copy.189.refs_0_), custom_call_target="tpu_custom_call" | custom-call | tf_op jit(solution)/shard_map/pallas_call | solution.py:417
  121.6 10.3 %shard_map.156 = f32[128,1024]{1,0:T(8,128)S(1)} custom-call(bf16[4,128,1024]{2,1,0:T(8,128)(2,1)S(1)} %convolution_convert_fusion.3.src), custom_call_target="tpu_custom_call" | custom-call | tf_op jit(solution)/shard_map/pallas_call | solution.py:529
  134.1 9.9 %shard_map.157 = bf16[4,128,1024]{2,1,0:T(8,128)(2,1)S(1)} custom-call(bf16[128,1024]{1,0:T(8,128)(2,1)S(1)} %multiply_convert_fusion.3.src), custom_call_target="tpu_custom_call" | custom-call | tf_op jit(solution)/shard_map/pallas_call | solution.py:479
  145.1 2.8 gather_fusion
  147.9 2.3 copy.193
  150.1 2.3 copy.222
  152.4 2.3 pad_maximum_fusion.1
  154.7 2.8 gather_fusion.1
  157.6 3.6 fusion.38
  161.1 4.5 add_convert_fusion
  165.9 2.0 convolution_convert_fusion.2
  167.9 1.9 fusion.16
  169.9 3.7 bitcast_convert_fusion
  173.6 3.3 convolution_convert_fusion.1
  177.8 10.3 %shard_map.158 = f32[128,1024]{1,0:T(8,128)S(1)} custom-call(bf16[4,128,1024]{2,1,0:T(8,128)(2,1)S(1)} %bitcast.284), custom_call_target="tpu_custom_call" | custom-call | tf_op jit(solution)/shard_map/pallas_call | solution.py:529
  188.4 2.0 fusion.96
  190.4 9.6 %shard_map.159 = bf16[4,128,1024]{2,1,0:T(8,128)(2,1)S(1)} custom-call(bf16[128,1024]{1,0:T(8,128)(2,1)S(1)} %get-tuple-element.54.src), custom_call_target="tpu_custom_call" | custom-call | tf_op jit(solution)/shard_map/pallas_call | solution.py:479
  200.0 1.2 convolution_convert_fusion.4
  205.4 1.8 collective-permute-start.9
  207.2 4.5 copy.207
  211.7 2.1 copy.208
  213.8 1.6 copy-done.3
  215.4 1.2 constant_dynamic-slice_fusion
  216.6 2.8 copy.210
  220.4 34.5 %shard_map.160 = bf16[8,128,128]{2,1,0:T(8,128)(2,1)} custom-call(bf16[8,128,128]{2,1,0:T(8,128)(2,1)} %bitcast.320), custom_call_target="tpu_custom_call" | custom-call | tf_op jit(solution)/shard_map/pallas_call | solution.py:417
  256.3 6.3 %fusion.33 = bf16[1,2,1024,64]{2,3,1,0:T(8,128)(2,1)S(1)} fusion(f32[2,1024,1024]{1,2,0:T(8,128)} %copy-done.5, f32[2,1024]{1,0:T(2,128)S(1)} %log_add_fusion, pred[1024,1024]{0,1:T(8,128)(4,1)S(1)} %copy-done.10, bf16[1024,2,64]{0,2,1:T(8,128)(2,1)S(1)} %reshape.386), kind=kOutput, calls=%fused_computation.66 | convolution fusion | flops 279052288 | bytes 9969664 | tf_op jit(solution)/shard_map/hqk,hqd->hkd/dot_general | solution.py:813
  262.6 5.6 %multiply_convert_fusion = bf16[2,1024,1024]{1,2,0:T(8,128)(2,1)S(1)} fusion(f32[2,1024,1024]{1,2,0:T(8,128)} %copy-done.5, f32[2,1024]{1,0:T(2,128)S(1)} %multiply_reduce_fusion.1, f32[2,1024]{1,0:T(2,128)S(1)} %log_add_fusion, pred[1024,1024]{0,1:T(8,128)(4,1)S(1)} %copy-done.10, bf16[1024,2,64]{0,2,1:T(8,128)(2,1)S(1)} %reshape.386, ...), kind=kOutput, calls=%fused_computation.3 | convolution fusion | flops 283115520 | bytes 14172160 | tf_op jit(solution)/shard_map/hqd,hkd->hqk/dot_general | solution.py:813
  268.2 1.4 fusion.81
  273.5 1.3 fusion.18
  275.4 2.6 collective-permute-start.11
  278.0 2.5 copy.211
  280.5 2.1 fusion.10
  283.3 1.5 collective-permute-start.16
  284.9 2.4 collective-permute-start.15
  287.2 3.5 collective-permute-done.12
  290.7 2.1 fusion.73
  292.8 13.6 %collective-permute-done.11 = bf16[656,128]{1,0:T(8,128)(2,1)} collective-permute-done((bf16[656,128]{1,0:T(8,128)(2,1)S(1)}, bf16[656,128]{1,0:T(8,128)(2,1)}, u32[]{:S(2)}, u32[]{:S(2)}) %collective-permute-start.11) | collective-permute-done | bytes 167968 | tf_op jit(solution)/shard_map/ppermute | solution.py:1002
  307.5 8.5 %collective-permute-done.16 = bf16[128,1312]{1,0:T(8,128)(2,1)S(1)} collective-permute-done((bf16[128,1312]{1,0:T(8,128)(2,1)S(1)}, bf16[128,1312]{1,0:T(8,128)(2,1)S(1)}, u32[]{:S(2)}, u32[]{:S(2)}) %collective-permute-start.16) | collective-permute-done | bytes 335904 | tf_op jit(solution)/shard_map/ppermute | solution.py:1002
  316.0 4.7 collective-permute-done.15
  320.9 1.4 copy.217.refs_0_
  322.3 21.7 %shard_map.161 = bf16[8,128,384]{2,1,0:T(8,128)(2,1)} custom-call(bf16[8,128,384]{2,1,0:T(8,128)(2,1)} %copy.217.refs_0_), custom_call_target="tpu_custom_call" | custom-call | tf_op jit(solution)/shard_map/pallas_call | solution.py:417
  344.0 1.6 copy.218
  345.7 1.3 copy-done.32
  348.0 10.5 %shard_map.162 = f32[128,1024]{1,0:T(8,128)S(1)} custom-call(bf16[4,128,1024]{2,1,0:T(8,128)(2,1)S(1)} %convolution_convert_fusion.src), custom_call_target="tpu_custom_call" | custom-call | tf_op jit(solution)/shard_map/pallas_call | solution.py:529
  360.1 122.7 %shard_map.163 = (bf16[8,656,128]{2,1,0:T(8,128)(2,1)S(1)}, bf16[8,128,1312]{2,1,0:T(8,128)(2,1)}, bf16[8,256,128]{2,1,0:T(8,128)(2,1)S(1)}, bf16[8,128,768]{2,1,0:T(8,128)(2,1)S(1)}, f32[2,256]{1,0:T(2,128)S(1)}) custom-call(bf16[656,128]{1,0:T(8,128)(2,1)S(1)} %fusion.72.refs_0_, bf16[128,1312]{1,0:T(8,128)(2,1)S(1)} %fusion.41.refs_1_, ...), custom_call_target="tpu_custom_call" | custom-call | tf_op jit(solution)/shard_map/pallas_call | solution.py:764
  484.3 1.8 copy-done.2
  486.2 5.3 %shard_map.164 = (f32[256,3072]{1,0:T(8,128)}, f32[256,1024]{1,0:T(8,128)}, f32[256,5248]{1,0:T(8,128)}, f32[656,1024]{1,0:T(8,128)}) custom-call(bf16[8,128,768]{2,1,0:T(8,128)(2,1)S(1)} %get-tuple-element.39.refs_0_, bf16[8,256,128]{2,1,0:T(8,128)(2,1)S(1)} %get-tuple-element.40.refs_1_, bf16[8,128,1312]{2,1,0:T(8,128)(2,1)S(1)} %copy-done.2, ...), custom_call_target="tpu_custom_call" | custom-call | tf_op jit(solution)/shard_map/pallas_call | solution.py:977
  (177 shorter events, 41.4 us)
Async XLA Ops:
  0.6 160.5 %copy-start = (bf16[656,1024]{1,0:T(8,128)(2,1)S(1)}, bf16[656,1024]{1,0:T(8,128)(2,1)}, u32[]{:S(2)}) copy-start(bf16[656,1024]{1,0:T(8,128)(2,1)} %param.14) | copy-start | bytes 4030468
  40.5 93.5 %collective-permute-start.5 = (bf16[128,1024]{1,0:T(8,128)(2,1)}, bf16[128,1024]{1,0:T(8,128)(2,1)}, u32[]{:S(2)}, u32[]{:S(2)}) collective-permute-start(bf16[128,1024]{1,0:T(8,128)(2,1)} %bitcast.1), channel_id=1, source_target_pairs={{0,3},{1,2},{2,1},{3,0},{4,7},{5,6},{6,5},{7,4},{8,11},{9,10},{10,... | collective-permute-start | bytes 786440 | tf_op jit(solution)/shard_map/ppermute | solution.py:792
  42.4 110.0 %collective-permute-start.4 = (bf16[128,1024]{1,0:T(8,128)(2,1)}, bf16[128,1024]{1,0:T(8,128)(2,1)}, u32[]{:S(2)}, u32[]{:S(2)}) collective-permute-start(bf16[128,1024]{1,0:T(8,128)(2,1)} %bitcast.1), channel_id=1, source_target_pairs={{0,2},{1,3},{2,0},{3,1},{4,6},{5,7},{6,4},{7,5},{8,10},{9,11},{10,... | collective-permute-start | bytes 786440 | tf_op jit(solution)/shard_map/ppermute | solution.py:792
  51.0 4.3 copy-start.4
  51.0 106.5 %collective-permute-start.2 = (bf16[256,1312]{0,1:T(8,128)(2,1)}, bf16[256,1312]{0,1:T(8,128)(2,1)}, u32[]{:S(2)}, u32[]{:S(2)}) collective-permute-start(bf16[256,1312]{0,1:T(8,128)(2,1)} %pad_maximum_fusion.7), channel_id=1, source_target_pairs={{0,3},{1,2},{2,1},{3,0},{4,7},{5,6},{6,5},{7,4},{8,11},{9,10},{10,... | collective-permute-start | bytes 2015240 | tf_op jit(solution)/shard_map/ppermute | solution.py:792
  51.9 105.6 %collective-permute-start.1 = (bf16[256,1312]{0,1:T(8,128)(2,1)}, bf16[256,1312]{0,1:T(8,128)(2,1)}, u32[]{:S(2)}, u32[]{:S(2)}) collective-permute-start(bf16[256,1312]{0,1:T(8,128)(2,1)} %pad_maximum_fusion.6), channel_id=1, source_target_pairs={{0,2},{1,3},{2,0},{3,1},{4,6},{5,7},{6,4},{7,5},{8,10},{9,11},{10,... | collective-permute-start | bytes 2015240 | tf_op jit(solution)/shard_map/ppermute | solution.py:792
  54.3 103.2 %collective-permute-start = (bf16[256,1312]{0,1:T(8,128)(2,1)}, bf16[256,1312]{0,1:T(8,128)(2,1)}, u32[]{:S(2)}, u32[]{:S(2)}) collective-permute-start(bf16[256,1312]{0,1:T(8,128)(2,1)} %pad_maximum_fusion.5), channel_id=1, source_target_pairs={{0,1},{1,0},{2,3},{3,2},{4,5},{5,4},{6,7},{7,6},{8,9},{9,8},{10,11... | collective-permute-start | bytes 2015240 | tf_op jit(solution)/shard_map/ppermute | solution.py:792
  54.7 1.4 copy-start.31
  57.1 1.1 copy-start.6
  59.8 11.0 %copy-start.17 = (f32[4,128,256]{2,1,0:T(8,128)S(1)}, f32[4,128,256]{2,1,0:T(8,128)}, u32[]{:S(2)}) copy-start(f32[4,128,256]{2,1,0:T(8,128)} %get-tuple-element.70) | copy-start | bytes 1572868
  59.8 11.2 %copy-start.16 = (f32[4,128,256]{2,1,0:T(8,128)S(1)}, f32[4,128,256]{2,1,0:T(8,128)}, u32[]{:S(2)}) copy-start(f32[4,128,256]{2,1,0:T(8,128)} %get-tuple-element.71) | copy-start | bytes 1572868
  71.8 1.0 copy-start.23
  93.7 4.7 copy-start.9
  101.3 3.3 copy-start.5
  109.3 11.8 %copy-start.25 = (bf16[256,1024]{1,0:T(8,128)(2,1)S(1)}, bf16[256,1024]{1,0:T(8,128)(2,1)}, u32[]{:S(2)}) copy-start(bf16[256,1024]{1,0:T(8,128)(2,1)} %param.12) | copy-start | bytes 1572868
  121.1 10.8 %copy-start.20 = (bf16[4,128,2,128]{1,3,2,0:T(8,128)(2,1)}, bf16[4,128,2,128]{1,3,2,0:T(8,128)(2,1)S(1)}, u32[]{:S(2)}) copy-start(bf16[4,128,2,128]{1,3,2,0:T(8,128)(2,1)S(1)} %copy.190) | copy-start | bytes 786436
  133.9 18.5 %collective-permute-start.3 = (bf16[128,1024]{1,0:T(8,128)(2,1)}, bf16[128,1024]{1,0:T(8,128)(2,1)}, u32[]{:S(2)}, u32[]{:S(2)}) collective-permute-start(bf16[128,1024]{1,0:T(8,128)(2,1)} %bitcast.1), channel_id=1, source_target_pairs={{0,1},{1,0},{2,3},{3,2},{4,5},{5,4},{6,7},{7,6},{8,9},{9,8},{10,11... | collective-permute-start | bytes 786440 | tf_op jit(solution)/shard_map/ppermute | solution.py:792
  157.5 3.6 copy-start.19
  169.9 3.7 copy-start.28
  169.9 3.7 copy-start.29
  188.4 11.6 %copy-start.26 = (bf16[256,1024]{1,0:T(8,128)(2,1)S(1)}, bf16[256,1024]{1,0:T(8,128)(2,1)}, u32[]{:S(2)}) copy-start(bf16[256,1024]{1,0:T(8,128)(2,1)} %param.12) | copy-start | bytes 1572868
  190.4 10.8 %copy-start.11 = (bf16[4,128,1024]{2,1,0:T(8,128)(2,1)S(1)}, bf16[4,128,1024]{2,1,0:T(8,128)(2,1)}, u32[]{:S(2)}) copy-start(bf16[4,128,1024]{2,1,0:T(8,128)(2,1)} %convolution_convert_fusion.2) | copy-start | bytes 3145732
  200.0 4.1 copy-start.18
  202.1 80.6 %collective-permute-start.8 = (bf16[128,1024]{1,0:T(8,128)(2,1)}, bf16[128,1024]{1,0:T(8,128)(2,1)}, u32[]{:S(2)}, u32[]{:S(2)}) collective-permute-start(bf16[128,1024]{1,0:T(8,128)(2,1)} %get-tuple-element.76), channel_id=1, source_target_pairs={{0,3},{1,2},{2,1},{3,0},{4,7},{5,6},{6,5},{7,4},{8,11},{9,10},{10,... | collective-permute-start | bytes 786440 | tf_op jit(solution)/shard_map/ppermute | solution.py:792
  203.1 80.2 %collective-permute-start.7 = (bf16[128,1024]{1,0:T(8,128)(2,1)}, bf16[128,1024]{1,0:T(8,128)(2,1)}, u32[]{:S(2)}, u32[]{:S(2)}) collective-permute-start(bf16[128,1024]{1,0:T(8,128)(2,1)} %get-tuple-element.77), channel_id=1, source_target_pairs={{0,2},{1,3},{2,0},{3,1},{4,6},{5,7},{6,4},{7,5},{8,10},{9,11},{10,... | collective-permute-start | bytes 786440 | tf_op jit(solution)/shard_map/ppermute | solution.py:792
  204.1 80.7 %collective-permute-start.6 = (bf16[128,1024]{1,0:T(8,128)(2,1)}, bf16[128,1024]{1,0:T(8,128)(2,1)}, u32[]{:S(2)}, u32[]{:S(2)}) collective-permute-start(bf16[128,1024]{1,0:T(8,128)(2,1)} %get-tuple-element.75), channel_id=1, source_target_pairs={{0,1},{1,0},{2,3},{3,2},{4,5},{5,4},{6,7},{7,6},{8,9},{9,8},{10,11... | collective-permute-start | bytes 786440 | tf_op jit(solution)/shard_map/ppermute | solution.py:792
  204.4 7.3 %copy-start.7 = (bf16[82,8,8,128]{3,2,0,1:T(8,128)(2,1)}, bf16[82,8,8,128]{3,2,0,1:T(8,128)(2,1)S(1)}, u32[]{:S(2)}) copy-start(bf16[82,8,8,128]{3,2,0,1:T(8,128)(2,1)S(1)} %copy.264) | copy-start | bytes 4030468
  205.4 68.0 %collective-permute-start.9 = (bf16[4,656,128]{2,1,0:T(8,128)(2,1)}, bf16[4,656,128]{2,1,0:T(8,128)(2,1)}, u32[]{:S(2)}, u32[]{:S(2)}) collective-permute-start(bf16[4,656,128]{2,1,0:T(8,128)(2,1)} %dynamic-slice_bitcast_fusion), channel_id=1, source_target_pairs={{0,4},{4,0},{8,12},{12,8},{16,20},{20,16},{24,28},{28,24},{1,5},{5... | collective-permute-start | bytes 2015240 | tf_op jit(solution)/shard_map/ppermute | solution.py:991
  213.8 1.6 copy-start.3
  216.6 3.1 copy-start.30
  219.4 36.9 %copy-start.10 = (pred[1024,1024]{0,1:T(8,128)(4,1)S(1)}, pred[1024,1024]{0,1:T(8,128)(4,1)}, u32[]{:S(2)}) copy-start(pred[1024,1024]{0,1:T(8,128)(4,1)} %broadcast_compare_fusion) | copy-start | bytes 3145732
  219.4 56.0 %collective-permute-start.13 = (bf16[4,128,1312]{1,2,0:T(8,128)(2,1)}, bf16[4,128,1312]{1,2,0:T(8,128)(2,1)}, u32[]{:S(2)}, u32[]{:S(2)}) collective-permute-start(bf16[4,128,1312]{1,2,0:T(8,128)(2,1)} %bitcast.314), channel_id=1, source_target_pairs={{0,4},{4,0},{8,12},{12,8},{16,20},{20,16},{24,28},{28,24},{1,5},{5... | collective-permute-start | bytes 4030472 | tf_op jit(solution)/shard_map/ppermute | solution.py:991
  256.2 6.3 %copy-start.27 = (f32[2,1024,64]{1,2,0:T(8,128)S(1)}, f32[2,1024,64]{1,2,0:T(8,128)}, u32[]{:S(2)}) copy-start(f32[2,1024,64]{1,2,0:T(8,128)} %get-tuple-element.111) | copy-start | bytes 1572868
  256.2 6.4 %copy-start.14 = (bf16[1024,3,2,64]{0,3,2,1:T(8,128)(2,1)S(1)}, bf16[1024,3,2,64]{0,3,2,1:T(8,128)(2,1)}, u32[]{:S(2)}) copy-start(bf16[1024,3,2,64]{0,3,2,1:T(8,128)(2,1)} %reshape.376) | copy-start | bytes 2359300
  268.2 1.4 copy-start.13
  270.5 1.0 copy-start.24
  271.7 1.2 copy-start.21
  271.8 1.6 copy-start.8
  274.8 15.9 %collective-permute-start.12 = (bf16[656,128]{1,0:T(8,128)(2,1)S(1)}, bf16[656,128]{1,0:T(8,128)(2,1)}, u32[]{:S(2)}, u32[]{:S(2)}) collective-permute-start(bf16[656,128]{1,0:T(8,128)(2,1)S(1)} %get-tuple-element.81), channel_id=1, source_target_pairs={{0,24},{4,28},{8,16},{12,20},{16,8},{20,12},{24,0},{28,4},{1,25},{... | collective-permute-start | bytes 503816 | tf_op jit(solution)/shard_map/ppermute | solution.py:1002
  275.4 31.0 %collective-permute-start.11 = (bf16[656,128]{1,0:T(8,128)(2,1)S(1)}, bf16[656,128]{1,0:T(8,128)(2,1)}, u32[]{:S(2)}, u32[]{:S(2)}) collective-permute-start(bf16[656,128]{1,0:T(8,128)(2,1)S(1)} %get-tuple-element.82), channel_id=1, source_target_pairs={{0,16},{4,20},{8,24},{12,28},{16,0},{20,4},{24,8},{28,12},{1,17},{... | collective-permute-start | bytes 503816 | tf_op jit(solution)/shard_map/ppermute | solution.py:1002
  282.8 23.7 %collective-permute-start.10 = (bf16[656,128]{1,0:T(8,128)(2,1)S(1)}, bf16[656,128]{1,0:T(8,128)(2,1)S(1)}, u32[]{:S(2)}, u32[]{:S(2)}) collective-permute-start(bf16[656,128]{1,0:T(8,128)(2,1)S(1)} %get-tuple-element.80), channel_id=1, source_target_pairs={{0,8},{4,12},{8,0},{12,4},{16,24},{20,28},{24,16},{28,20},{1,9},{5... | collective-permute-start | bytes 503816 | tf_op jit(solution)/shard_map/ppermute | solution.py:1002
  283.3 32.7 %collective-permute-start.16 = (bf16[128,1312]{1,0:T(8,128)(2,1)S(1)}, bf16[128,1312]{1,0:T(8,128)(2,1)S(1)}, u32[]{:S(2)}, u32[]{:S(2)}) collective-permute-start(bf16[128,1312]{1,0:T(8,128)(2,1)S(1)} %get-tuple-element.73), channel_id=1, source_target_pairs={{0,24},{4,28},{8,16},{12,20},{16,8},{20,12},{24,0},{28,4},{1,25},{... | collective-permute-start | bytes 1007624 | tf_op jit(solution)/shard_map/ppermute | solution.py:1002
  284.9 35.8 %collective-permute-start.15 = (bf16[128,1312]{1,0:T(8,128)(2,1)S(1)}, bf16[128,1312]{1,0:T(8,128)(2,1)S(1)}, u32[]{:S(2)}, u32[]{:S(2)}) collective-permute-start(bf16[128,1312]{1,0:T(8,128)(2,1)S(1)} %get-tuple-element.74), channel_id=1, source_target_pairs={{0,16},{4,20},{8,24},{12,28},{16,0},{20,4},{24,8},{28,12},{1,17},{... | collective-permute-start | bytes 1007624 | tf_op jit(solution)/shard_map/ppermute | solution.py:1002
  290.7 30.0 %collective-permute-start.14 = (bf16[128,1312]{1,0:T(8,128)(2,1)S(1)}, bf16[128,1312]{1,0:T(8,128)(2,1)S(1)}, u32[]{:S(2)}, u32[]{:S(2)}) collective-permute-start(bf16[128,1312]{1,0:T(8,128)(2,1)S(1)} %get-tuple-element.72), channel_id=1, source_target_pairs={{0,8},{4,12},{8,0},{12,4},{16,24},{20,28},{24,16},{28,20},{1,9},{5... | collective-permute-start | bytes 1007624 | tf_op jit(solution)/shard_map/ppermute | solution.py:1002
  292.8 28.1 %copy-start.12 = (bf16[48,8,8,128]{3,2,1,0:T(8,128)(2,1)S(1)}, bf16[48,8,8,128]{3,2,1,0:T(8,128)(2,1)}, u32[]{:S(2)}) copy-start(bf16[48,8,8,128]{3,2,1,0:T(8,128)(2,1)} %copy.253) | copy-start | bytes 2359300
  345.6 1.4 copy-start.32
  348.0 10.9 %copy-start.22 = (bf16[1024,4,128]{2,0,1:T(8,128)(2,1)S(1)}, bf16[1024,4,128]{2,0,1:T(8,128)(2,1)}, u32[]{:S(2)}) copy-start(bf16[1024,4,128]{2,0,1:T(8,128)(2,1)} %copy.222) | copy-start | bytes 3145732
  360.0 123.3 %copy-start.15 = (f32[128,1024]{1,0:T(8,128)S(1)}, f32[128,1024]{1,0:T(8,128)}, u32[]{:S(2)}) copy-start(f32[128,1024]{1,0:T(8,128)} %get-tuple-element.55) | copy-start | bytes 1572868
  484.3 1.8 copy-start.2
  486.2 5.3 %copy-start.1 = (bf16[656,1024]{1,0:T(8,128)(2,1)S(1)}, bf16[656,1024]{1,0:T(8,128)(2,1)}, u32[]{:S(2)}) copy-start(bf16[656,1024]{1,0:T(8,128)(2,1)} %param.14) | copy-start | bytes 4030468

commit v4 on v3

--- a/solution.py
+++ b/solution.py
@@ -932,25 +932,6 @@
     grad_hidden = jnp.concatenate([grad_inner, grad_gate], -1).astype(low)
     normed_back = dot("stf,cf->stc", grad_hidden, in_cols).astype(low)
     normed_back = normed_back.reshape(parts, row_count, parts, part_d)[:, :, relative]
-    grad_normed_mlp = square_sum(normed_back.reshape(normed_mlp.shape), 9)
-    grad_gain_mlp = jnp.sum(grad_normed_mlp * norm_two, 0)
-    grad_mixed = cot.astype(wide) + norm_back(grad_normed_mlp, gain_two, norm_two, factor_two)
-    grad_branch = gather(grad_mixed.astype(low), 10)
-    grad_attended = dot("stf,cf->stc", grad_branch, w_out).astype(low)
-    grad_out = (
-        grad_attended.reshape(parts, row_count, seq_split, pairs * HEAD)
-        .transpose(0, 2, 1, 3)
-        .reshape(ctx_size, row_count, pairs * HEAD)
-    )
-    grad_heads = swap_ctx(grad_out, 11).reshape(length, pairs, HEAD).transpose(1, 0, 2)
-
-    output_parts = dot("stf,fn->stn", product, w_down).astype(low)
-    output_parts, grad_branch = lax.optimization_barrier((output_parts, grad_branch))
-    output_parts = permute_group(
-        lambda peer: lax.dynamic_index_in_dim(output_parts, peer, 0, False), parts
-    )
-    output = (mixed + sum(part.astype(wide) for part in output_parts)).astype(low)
-
     def rows_of(grad, width):
         return (
             grad.reshape(parts, ctx_size, part_d // ctx_size, width)
@@ -962,6 +943,53 @@
     def columns_of(grad):
         rows = grad.shape[0]
         return grad.reshape(rows, ctx_size, D // ctx_size).transpose(1, 0, 2).astype(low)
+
+    depth = ctx_size // 2
+    place_z, side = ctx_index // 2, ctx_index % 2
+
+    def by_side(grad):
+        split = grad.reshape((depth, 2) + grad.shape[1:])
+        return [lax.dynamic_index_in_dim(split, at, 1, False) for at in (side, 1 - side)]
+
+    def sum_sides(kept, sent):
+        came = lax.ppermute(sent, "ctx", [(i, i ^ 1) for i in range(ctx_size)])
+        return (kept.astype(wide) + came.astype(wide)).astype(low)
+
+    def sum_depth(grad):
+        summed = lax.dynamic_index_in_dim(grad, place_z, 0, False).astype(wide)
+        for step in range(1, depth):
+            summed = summed + lax.ppermute(
+                lax.dynamic_index_in_dim(grad, place_z ^ step, 0, False),
+                "ctx",
+                [(i, i ^ (2 * step)) for i in range(ctx_size)],
+            ).astype(wide)
+        return summed.astype(low)
+
+    down_kept, down_sent = by_side(columns_of(dot("stf,stn->fn", product, all_cot)))
+    in_kept, in_sent = by_side(rows_of(dot("stc,stf->cf", normed_mlp, grad_hidden), 2 * part_ff))
+    down_sent, in_sent, normed_back = lax.optimization_barrier((down_sent, in_sent, normed_back))
+    down_grad = sum_sides(down_kept, down_sent)
+    in_grad = sum_sides(in_kept, in_sent)
+    grad_normed_mlp = square_sum(normed_back.reshape(normed_mlp.shape), 9)
+    grad_gain_mlp = jnp.sum(grad_normed_mlp * norm_two, 0)
+    grad_mixed = cot.astype(wide) + norm_back(grad_normed_mlp, gain_two, norm_two, factor_two)
+    down_grad, branch_low = lax.optimization_barrier((down_grad, grad_mixed.astype(low)))
+    down_grad = sum_depth(down_grad)
+    grad_branch = gather(branch_low, 10)
+    grad_attended = dot("stf,cf->stc", grad_branch, w_out).astype(low)
+    grad_out = (
+        grad_attended.reshape(parts, row_count, seq_split, pairs * HEAD)
+        .transpose(0, 2, 1, 3)
+        .reshape(ctx_size, row_count, pairs * HEAD)
+    )
+    grad_heads = swap_ctx(grad_out, 11).reshape(length, pairs, HEAD).transpose(1, 0, 2)
+
+    output_parts = dot("stf,fn->stn", product, w_down).astype(low)
+    output_parts, grad_branch = lax.optimization_barrier((output_parts, grad_branch))
+    output_parts = permute_group(
+        lambda peer: lax.dynamic_index_in_dim(output_parts, peer, 0, False), parts
+    )
+    output = (mixed + sum(part.astype(wide) for part in output_parts)).astype(low)
 
     def place(grads, pieces):
         specs, shapes = [], []
@@ -983,34 +1011,8 @@
             compiler_params=pltpu.CompilerParams(vmem_limit_bytes=32 * 1024 * 1024),
         )(*grads)
 
-    depth = ctx_size // 2
-    place_z, side = ctx_index // 2, ctx_index % 2
-
-    def sum_sides(grad):
-        split = grad.reshape((depth, 2) + grad.shape[1:])
-        came = lax.ppermute(
-            lax.dynamic_index_in_dim(split, 1 - side, 1, False),
-            "ctx",
-            [(i, i ^ 1) for i in range(ctx_size)],
-        )
-        kept = lax.dynamic_index_in_dim(split, side, 1, False)
-        return (kept.astype(wide) + came.astype(wide)).astype(low)
-
-    def sum_depth(grad):
-        summed = lax.dynamic_index_in_dim(grad, place_z, 0, False).astype(wide)
-        for step in range(1, depth):
-            summed = summed + lax.ppermute(
-                lax.dynamic_index_in_dim(grad, place_z ^ step, 0, False),
-                "ctx",
-                [(i, i ^ (2 * step)) for i in range(ctx_size)],
-            ).astype(wide)
-        return summed.astype(low)
-
-    down_grad = sum_sides(columns_of(dot("stf,stn->fn", product, all_cot)))
-    in_grad = sum_sides(rows_of(dot("stc,stf->cf", normed_mlp, grad_hidden), 2 * part_ff))
-    down_grad = sum_depth(down_grad)
+    in_grad, down_grad, grad_heads = lax.optimization_barrier((in_grad, down_grad, grad_heads))
     in_grad = sum_depth(in_grad)
-
     row_dot = jnp.sum(grad_heads.astype(wide) * attended, -1, keepdims=True)
     weights_f = jnp.where(same, jnp.exp(scores - log_total), 0.0)
     grad_weights = dot("hqd,hkd->hqk", grad_heads, values)
@@ -1028,7 +1030,7 @@
         ]
     ).astype(low)
     grads = grads.transpose(2, 0, 1, 3).reshape(ctx_size, row_count, 3 * pairs * HEAD)
-    down_grad, in_grad, grads = lax.optimization_barrier((down_grad, in_grad, grads))
+    in_grad, grads = lax.optimization_barrier((in_grad, grads))
     grads = swap_ctx(grads, 15)
     grad_projected = (
         grads.reshape(parts, seq_split, row_count, 3, pairs * HEAD)

time: 502 us -> 497 us (0.990)
  waiting for transfers between devices: 30.3 us -> 50.4 us
  Pallas kernels: 302 us -> 283 us
  matrix products: 45.9 us -> 40.7 us
    pallas_call x6, Pallas kernels: 123 us -> 99.8 us  [exchange(): pl.pallas_call(functools.partial(exchange_kernel, size, group, spreads),...]
    ppermute x2, waiting for transfers between devices: 0.01 us -> 12.9 us  [sum_sides(): came = lax.ppermute(sent, 'ctx', [(i, i ^ 1) for i in range(ctx_size)])]
    ppermute x6, waiting for transfers between devices: 30.3 us -> 37.5 us  [sum_depth(): lax.ppermute(lax.dynamic_index_in_dim(grad, place_z ^ step, 0, False), 'c...]
    dot_general x18, matrix products: 45.9 us -> 40.7 us  [dot(): return jnp.einsum(equation, left, right, preferred_element_type=jnp.float32)]
    unnamed x73 -> x81, local copies, waits for them, and re-layouts: 12.1 us -> 10.1 us
  transfers between devices with their start and end apart: 17 -> 17, of which waited for: 4 -> 6; matrix products, arithmetic and copies ran while one was open for 19% -> 13% of each run, Pallas kernels for 19% -> 17%
where the time goes in v4:
time: 497 us; the launch traced here: 487 us
  Pallas kernels  283 us (57%)
  local copies, waits for them, and re-layouts  66 us (13%)
  waiting for transfers between devices  50.4 us (10%)
  matrix products  40.7 us (8%)
  other arithmetic  30.1 us (6%)
  starting transfers between devices  14.8 us (3%)
    pallas_call x1, Pallas kernels, reduce_over_ctx(): pl.pallas_call(functools.partial(reduce_kernel, turns, ready, size, count...  123 us
    pallas_call x6, Pallas kernels, exchange(): pl.pallas_call(functools.partial(exchange_kernel, size, group, spreads),...  99.8 us
    dot_general x18, matrix products, dot(): return jnp.einsum(equation, left, right, preferred_element_type=jnp.float32)  40.7 us
    ppermute x6, waiting for transfers between devices, sum_depth(): lax.ppermute(lax.dynamic_index_in_dim(grad, place_z ^ step, 0, False), 'c...  37.5 us
    pallas_call x3, Pallas kernels, square_sum(): pl.pallas_call(square_sum_kernel, out_shape=jax.ShapeDtypeStruct(terms.sh...  31.1 us
    pallas_call x2, Pallas kernels, square_gather(): pl.pallas_call(square_gather_kernel, out_shape=jax.ShapeDtypeStruct((4,)...  24.3 us
    ppermute x2, waiting for transfers between devices, sum_sides(): came = lax.ppermute(sent, 'ctx', [(i, i ^ 1) for i in range(ctx_size)])  12.9 us
    unnamed x81, local copies, waits for them, and re-layouts  10.1 us
  transfers between devices with their start and end apart: 17, of which 6 were waited for; matrix products, arithmetic and copies ran while one was open for 13% of the time, Pallas kernels for 17%

profile of v4, /device:TPU:8, one launch (start us, length us, event | category | flops | bytes accessed | tf_op | source)
XLA Modules:
  0.0 487.3 jit_solution(6801719808661288676)
XLA Ops:
  0.6 2.7 copy.177
  3.3 1.5 copy.178
  4.9 1.6 copy.179.refs_2_
  7.1 30.7 %shard_map.152 = (f32[4,5,128]{2,1,0:T(8,128)}, bf16[4,128,1024]{2,1,0:T(8,128)(2,1)}, bf16[4,256,768]{2,1,0:T(8,128)(2,1)}) custom-call(f32[5,128]{1,0:T(8,128)} %maximum_bitcast_fusion.5.refs_0_, bf16[128,1024]{1,0:T(8,128)(2,1)} %bitcast.287, bf16[4,256,768]{2,1,0:T(8,128)(2,1)} %copy.179.refs_2_), custom_call_target="tpu_custom_call" | custom-call | tf_op jit(solution)/shard_map/pallas_call | solution.py:417
  39.4 1.5 collective-permute-start.4
  40.9 4.5 copy.194
  45.3 2.7 constant_dynamic-slice_fusion.8
  51.2 1.3 collective-permute-start.2
  56.0 1.4 fusion.42
  57.3 1.2 copy.237
  60.5 7.1 %shard_map.153 = s32[8,4,128]{2,1,0:T(4,128)} custom-call(s32[4,128]{1,0:T(4,128)} %slice_convert_fusion.1.refs_0_), custom_call_target="tpu_custom_call" | custom-call | tf_op jit(solution)/shard_map/pallas_call | solution.py:417
  72.9 20.0 %shard_map.154 = bf16[8,128,384]{2,1,0:T(8,128)(2,1)} custom-call(bf16[8,128,384]{2,1,0:T(8,128)(2,1)} %copy.186.refs_0_), custom_call_target="tpu_custom_call" | custom-call | tf_op jit(solution)/shard_map/pallas_call | solution.py:417
  92.9 1.6 copy.187
  96.3 1.9 fusion.3
  98.3 2.3 fusion
  101.5 3.7 fusion.65
  106.2 9.9 %shard_map.155 = bf16[8,128,128]{2,1,0:T(8,128)(2,1)} custom-call(bf16[8,128,128]{2,1,0:T(8,128)(2,1)} %copy.189.refs_0_), custom_call_target="tpu_custom_call" | custom-call | tf_op jit(solution)/shard_map/pallas_call | solution.py:417
  117.8 10.3 %shard_map.156 = f32[128,1024]{1,0:T(8,128)S(1)} custom-call(bf16[4,128,1024]{2,1,0:T(8,128)(2,1)S(1)} %convolution_convert_fusion.3.src), custom_call_target="tpu_custom_call" | custom-call | tf_op jit(solution)/shard_map/pallas_call | solution.py:529
  130.2 15.5 %shard_map.157 = bf16[4,128,1024]{2,1,0:T(8,128)(2,1)S(1)} custom-call(bf16[128,1024]{1,0:T(8,128)(2,1)S(1)} %multiply_convert_fusion.3.src), custom_call_target="tpu_custom_call" | custom-call | tf_op jit(solution)/shard_map/pallas_call | solution.py:479
  146.9 2.8 gather_fusion
  149.7 2.3 copy.193
  151.9 2.3 copy.222
  154.2 2.3 pad_maximum_fusion.1
  156.5 2.8 gather_fusion.1
  159.4 3.6 fusion.38
  162.9 4.5 add_convert_fusion
  168.6 3.7 bitcast_convert_fusion
  172.3 3.3 convolution_convert_fusion.1
  176.7 1.8 gather_fusion.2
  178.6 4.5 copy.205
  183.1 2.1 copy.206
  185.2 1.6 copy-done.2
  188.0 2.5 copy.207
  190.5 2.3 fusion.16
  193.2 10.3 %shard_map.158 = f32[128,1024]{1,0:T(8,128)S(1)} custom-call(bf16[4,128,1024]{2,1,0:T(8,128)(2,1)S(1)} %bitcast.281), custom_call_target="tpu_custom_call" | custom-call | tf_op jit(solution)/shard_map/pallas_call | solution.py:529
  203.8 1.8 collective-permute-start.6
  205.9 2.0 fusion.94
  209.0 12.9 %collective-permute-done.6 = bf16[4,656,128]{2,1,0:T(8,128)(2,1)S(1)} collective-permute-done((bf16[4,656,128]{2,1,0:T(8,128)(2,1)S(1)}, bf16[4,656,128]{2,1,0:T(8,128)(2,1)S(1)}, u32[]{:S(2)}, u32[]{:S(2)}) %collective-permute-start.6) | collective-permute-done | bytes 671776 | tf_op jit(solution)/shard_map/ppermute | solution.py:955
  222.1 8.8 %shard_map.159 = bf16[4,128,1024]{2,1,0:T(8,128)(2,1)S(1)} custom-call(bf16[128,1024]{1,0:T(8,128)(2,1)S(1)} %get-tuple-element.43.src), custom_call_target="tpu_custom_call" | custom-call | tf_op jit(solution)/shard_map/pallas_call | solution.py:479
  233.6 1.5 collective-permute-start.13
  237.0 2.1 collective-permute-done.11
  239.2 1.4 collective-permute-start.8
  240.6 4.9 %collective-permute-done.12 = bf16[656,128]{1,0:T(8,128)(2,1)S(1)} collective-permute-done((bf16[656,128]{1,0:T(8,128)(2,1)S(1)}, bf16[656,128]{1,0:T(8,128)(2,1)S(1)}, u32[]{:S(2)}, u32[]{:S(2)}) %collective-permute-start.12) | collective-permute-done | bytes 167968 | tf_op jit(solution)/shard_map/ppermute | solution.py:961
  246.2 12.7 %shard_map.160 = bf16[8,128,128]{2,1,0:T(8,128)(2,1)} custom-call(bf16[8,128,128]{2,1,0:T(8,128)(2,1)} %bitcast.321), custom_call_target="tpu_custom_call" | custom-call | tf_op jit(solution)/shard_map/pallas_call | solution.py:417
  260.2 1.3 fusion.72.refs_0_
  261.5 2.1 fusion.73
  263.6 2.6 copy.211
  266.2 2.3 fusion.10
  268.6 6.6 %fusion.33 = bf16[1,2,1024,64]{2,3,1,0:T(8,128)(2,1)S(1)} fusion(bf16[2,1024,64]{1,2,0:T(8,128)(2,1)S(1)} %bitcast.316, f32[2,1024,1024]{1,2,0:T(8,128)} %copy-done.4, f32[2,1024]{1,0:T(2,128)S(1)} %log_add_fusion, pred[1024,1024]{0,1:T(8,128)(4,1)} %copy-done.6), kind=kOutput, calls=%fused_computation.66 | convolution fusion | flops 279052288 | bytes 9969664 | tf_op jit(solution)/shard_map/hqk,hqd->hkd/dot_general | solution.py:813
  275.2 3.4 multiply_convert_fusion
  278.7 1.4 fusion.79
  281.2 1.7 collective-permute-start.15
  282.9 1.8 collective-permute-start.16
  286.1 10.1 %collective-permute-done.14 = bf16[128,1312]{1,0:T(8,128)(2,1)S(1)} collective-permute-done((bf16[128,1312]{1,0:T(8,128)(2,1)S(1)}, bf16[128,1312]{1,0:T(8,128)(2,1)S(1)}, u32[]{:S(2)}, u32[]{:S(2)}) %collective-permute-start.14) | collective-permute-done | bytes 335904 | tf_op jit(solution)/shard_map/ppermute | solution.py:961
  296.2 10.8 %collective-permute-done.15 = bf16[128,1312]{1,0:T(8,128)(2,1)S(1)} collective-permute-done((bf16[128,1312]{1,0:T(8,128)(2,1)S(1)}, bf16[128,1312]{1,0:T(8,128)(2,1)S(1)}, u32[]{:S(2)}, u32[]{:S(2)}) %collective-permute-start.15) | collective-permute-done | bytes 335904 | tf_op jit(solution)/shard_map/ppermute | solution.py:961
  307.0 9.5 %collective-permute-done.16 = bf16[128,1312]{1,0:T(8,128)(2,1)S(1)} collective-permute-done((bf16[128,1312]{1,0:T(8,128)(2,1)S(1)}, bf16[128,1312]{1,0:T(8,128)(2,1)S(1)}, u32[]{:S(2)}, u32[]{:S(2)}) %collective-permute-start.16) | collective-permute-done | bytes 335904 | tf_op jit(solution)/shard_map/ppermute | solution.py:961
  316.8 2.4 copy.217.refs_0_
  319.2 19.4 %shard_map.161 = bf16[8,128,384]{2,1,0:T(8,128)(2,1)} custom-call(bf16[8,128,384]{2,1,0:T(8,128)(2,1)} %copy.217.refs_0_), custom_call_target="tpu_custom_call" | custom-call | tf_op jit(solution)/shard_map/pallas_call | solution.py:417
  338.6 2.3 copy.218
  340.9 1.3 copy.219
  343.6 10.5 %shard_map.162 = f32[128,1024]{1,0:T(8,128)S(1)} custom-call(bf16[4,128,1024]{2,1,0:T(8,128)(2,1)S(1)} %convolution_convert_fusion.src), custom_call_target="tpu_custom_call" | custom-call | tf_op jit(solution)/shard_map/pallas_call | solution.py:529
  355.5 122.6 %shard_map.163 = (bf16[8,656,128]{2,1,0:T(8,128)(2,1)S(1)}, bf16[8,128,1312]{2,1,0:T(8,128)(2,1)}, bf16[8,256,128]{2,1,0:T(8,128)(2,1)S(1)}, bf16[8,128,768]{2,1,0:T(8,128)(2,1)S(1)}, f32[2,256]{1,0:T(2,128)S(1)}) custom-call(bf16[656,128]{1,0:T(8,128)(2,1)S(1)} %fusion.72.refs_0_, bf16[128,1312]{1,0:T(8,128)(2,1)S(1)} %fusion.41.refs_1_, ...), custom_call_target="tpu_custom_call" | custom-call | tf_op jit(solution)/shard_map/pallas_call | solution.py:764
  479.8 1.8 copy-done.1
  481.6 5.3 %shard_map.164 = (f32[256,3072]{1,0:T(8,128)}, f32[256,1024]{1,0:T(8,128)}, f32[256,5248]{1,0:T(8,128)}, f32[656,1024]{1,0:T(8,128)}) custom-call(bf16[8,128,768]{2,1,0:T(8,128)(2,1)S(1)} %get-tuple-element.53.refs_0_, bf16[8,256,128]{2,1,0:T(8,128)(2,1)S(1)} %get-tuple-element.54.refs_1_, bf16[8,128,1312]{2,1,0:T(8,128)(2,1)S(1)} %copy-done.1, ...), custom_call_target="tpu_custom_call" | custom-call | tf_op jit(solution)/shard_map/pallas_call | solution.py:1005
  (186 shorter events, 43.7 us)
Async XLA Ops:
  0.6 162.3 %copy-start = (bf16[656,1024]{1,0:T(8,128)(2,1)S(1)}, bf16[656,1024]{1,0:T(8,128)(2,1)}, u32[]{:S(2)}) copy-start(bf16[656,1024]{1,0:T(8,128)(2,1)} %param.14) | copy-start | bytes 4030468
  4.8 1.6 copy-start.32
  4.9 1.6 copy-start.33
  4.9 1.6 copy-start.34
  38.6 91.5 %collective-permute-start.3 = (bf16[128,1024]{1,0:T(8,128)(2,1)}, bf16[128,1024]{1,0:T(8,128)(2,1)}, u32[]{:S(2)}, u32[]{:S(2)}) collective-permute-start(bf16[128,1024]{1,0:T(8,128)(2,1)} %bitcast.1), channel_id=1, source_target_pairs={{0,1},{1,0},{2,3},{3,2},{4,5},{5,4},{6,7},{7,6},{8,9},{9,8},{10,11... | collective-permute-start | bytes 786440 | tf_op jit(solution)/shard_map/ppermute | solution.py:792
  39.4 114.8 %collective-permute-start.4 = (bf16[128,1024]{1,0:T(8,128)(2,1)}, bf16[128,1024]{1,0:T(8,128)(2,1)}, u32[]{:S(2)}, u32[]{:S(2)}) collective-permute-start(bf16[128,1024]{1,0:T(8,128)(2,1)} %bitcast.1), channel_id=1, source_target_pairs={{0,2},{1,3},{2,0},{3,1},{4,6},{5,7},{6,4},{7,5},{8,10},{9,11},{10,... | collective-permute-start | bytes 786440 | tf_op jit(solution)/shard_map/ppermute | solution.py:792
  48.9 4.3 copy-start.3
  48.9 110.4 %collective-permute-start = (bf16[256,1312]{0,1:T(8,128)(2,1)}, bf16[256,1312]{0,1:T(8,128)(2,1)}, u32[]{:S(2)}, u32[]{:S(2)}) collective-permute-start(bf16[256,1312]{0,1:T(8,128)(2,1)} %pad_maximum_fusion.5), channel_id=1, source_target_pairs={{0,1},{1,0},{2,3},{3,2},{4,5},{5,4},{6,7},{7,6},{8,9},{9,8},{10,11... | collective-permute-start | bytes 2015240 | tf_op jit(solution)/shard_map/ppermute | solution.py:792
  49.8 109.5 %collective-permute-start.1 = (bf16[256,1312]{0,1:T(8,128)(2,1)}, bf16[256,1312]{0,1:T(8,128)(2,1)}, u32[]{:S(2)}, u32[]{:S(2)}) collective-permute-start(bf16[256,1312]{0,1:T(8,128)(2,1)} %pad_maximum_fusion.6), channel_id=1, source_target_pairs={{0,2},{1,3},{2,0},{3,1},{4,6},{5,7},{6,4},{7,5},{8,10},{9,11},{10,... | collective-permute-start | bytes 2015240 | tf_op jit(solution)/shard_map/ppermute | solution.py:792
  50.4 3.5 copy-start.30
  51.2 108.1 %collective-permute-start.2 = (bf16[256,1312]{0,1:T(8,128)(2,1)}, bf16[256,1312]{0,1:T(8,128)(2,1)}, u32[]{:S(2)}, u32[]{:S(2)}) collective-permute-start(bf16[256,1312]{0,1:T(8,128)(2,1)} %pad_maximum_fusion.7), channel_id=1, source_target_pairs={{0,3},{1,2},{2,1},{3,0},{4,7},{5,6},{6,5},{7,4},{8,11},{9,10},{10,... | collective-permute-start | bytes 2015240 | tf_op jit(solution)/shard_map/ppermute | solution.py:792
  54.9 1.0 copy-start.5
  59.6 9.8 %copy-start.21 = (f32[1,4,128,4,32]{2,4,3,1,0:T(8,128)S(1)}, f32[1,4,128,4,32]{2,4,3,1,0:T(8,128)}, u32[]{:S(2)}) copy-start(f32[1,4,128,4,32]{2,4,3,1,0:T(8,128)} %get-tuple-element.101) | copy-start | bytes 786436
  59.6 9.8 %copy-start.22 = (f32[1,4,128,4,32]{2,4,3,1,0:T(8,128)S(1)}, f32[1,4,128,4,32]{2,4,3,1,0:T(8,128)}, u32[]{:S(2)}) copy-start(f32[1,4,128,4,32]{2,4,3,1,0:T(8,128)} %get-tuple-element.102) | copy-start | bytes 786436
  70.7 1.0 copy-start.19
  94.9 5.7 %copy-start.12 = (bf16[1024,3,2,64]{0,3,2,1:T(8,128)(2,1)}, bf16[1024,3,2,64]{0,3,2,1:T(8,128)(2,1)S(1)}, u32[]{:S(2)}) copy-start(bf16[1024,3,2,64]{0,3,2,1:T(8,128)(2,1)S(1)} %reshape.376) | copy-start | bytes 2359300
  96.3 4.2 copy-start.6
  98.2 3.3 copy-start.4
  105.3 12.0 %copy-start.23 = (bf16[256,1024]{1,0:T(8,128)(2,1)S(1)}, bf16[256,1024]{1,0:T(8,128)(2,1)}, u32[]{:S(2)}) copy-start(bf16[256,1024]{1,0:T(8,128)(2,1)} %param.12) | copy-start | bytes 1572868
  117.3 10.8 %copy-start.16 = (bf16[4,128,2,128]{1,3,2,0:T(8,128)(2,1)}, bf16[4,128,2,128]{1,3,2,0:T(8,128)(2,1)S(1)}, u32[]{:S(2)}) copy-start(bf16[4,128,2,128]{1,3,2,0:T(8,128)(2,1)S(1)} %copy.190) | copy-start | bytes 786436
  130.1 24.1 %collective-permute-start.5 = (bf16[128,1024]{1,0:T(8,128)(2,1)}, bf16[128,1024]{1,0:T(8,128)(2,1)}, u32[]{:S(2)}, u32[]{:S(2)}) collective-permute-start(bf16[128,1024]{1,0:T(8,128)(2,1)} %bitcast.1), channel_id=1, source_target_pairs={{0,3},{1,2},{2,1},{3,0},{4,7},{5,6},{6,5},{7,4},{8,11},{9,10},{10,... | collective-permute-start | bytes 786440 | tf_op jit(solution)/shard_map/ppermute | solution.py:792
  159.3 3.6 copy-start.15
  168.6 3.7 copy-start.26
  168.6 3.7 copy-start.27
  185.2 1.6 copy-start.2
  203.6 4.4 copy-start.9
  203.8 18.0 %collective-permute-start.6 = (bf16[4,656,128]{2,1,0:T(8,128)(2,1)S(1)}, bf16[4,656,128]{2,1,0:T(8,128)(2,1)S(1)}, u32[]{:S(2)}, u32[]{:S(2)}) collective-permute-start(bf16[4,656,128]{2,1,0:T(8,128)(2,1)S(1)} %dynamic-slice_bitcast_fusion), channel_id=1, source_target_pairs={{0,4},{4,0},{8,12},{12,8},{16,20},{20,16},{24,28},{28,24},{1,5},{5... | collective-permute-start | bytes 2015240 | tf_op jit(solution)/shard_map/ppermute | solution.py:955
  205.7 57.9 %collective-permute-start.10 = (bf16[4,128,1312]{1,2,0:T(8,128)(2,1)}, bf16[4,128,1312]{1,2,0:T(8,128)(2,1)}, u32[]{:S(2)}, u32[]{:S(2)}) collective-permute-start(bf16[4,128,1312]{1,2,0:T(8,128)(2,1)} %bitcast.57), channel_id=1, source_target_pairs={{0,4},{4,0},{8,12},{12,8},{16,20},{20,16},{24,28},{28,24},{1,5},{5... | collective-permute-start | bytes 4030472 | tf_op jit(solution)/shard_map/ppermute | solution.py:955
  208.9 26.2 %copy-start.8 = (bf16[4,128,1024]{2,1,0:T(8,128)(2,1)}, bf16[4,128,1024]{2,1,0:T(8,128)(2,1)S(1)}, u32[]{:S(2)}) copy-start(bf16[4,128,1024]{2,1,0:T(8,128)(2,1)S(1)} %convolution_convert_fusion.2) | copy-start | bytes 3145732
  222.1 14.0 %copy-start.10 = (bf16[4,656,128]{2,1,0:T(8,128)(2,1)}, bf16[4,656,128]{2,1,0:T(8,128)(2,1)S(1)}, u32[]{:S(2)}) copy-start(bf16[4,656,128]{2,1,0:T(8,128)(2,1)S(1)} %fusion.18) | copy-start | bytes 2015236
  230.9 5.2 %copy-start.24 = (bf16[256,1024]{1,0:T(8,128)(2,1)S(1)}, bf16[256,1024]{1,0:T(8,128)(2,1)}, u32[]{:S(2)}) copy-start(bf16[256,1024]{1,0:T(8,128)(2,1)} %param.12) | copy-start | bytes 1572868
  231.6 7.5 %collective-permute-start.11 = (bf16[656,128]{1,0:T(8,128)(2,1)S(1)}, bf16[656,128]{1,0:T(8,128)(2,1)S(1)}, u32[]{:S(2)}, u32[]{:S(2)}) collective-permute-start(bf16[656,128]{1,0:T(8,128)(2,1)S(1)} %get-tuple-element.94), channel_id=1, source_target_pairs={{0,8},{4,12},{8,0},{12,4},{16,24},{20,28},{24,16},{28,20},{1,9},{5... | collective-permute-start | bytes 503816 | tf_op jit(solution)/shard_map/ppermute | solution.py:961
  232.4 13.0 %collective-permute-start.12 = (bf16[656,128]{1,0:T(8,128)(2,1)S(1)}, bf16[656,128]{1,0:T(8,128)(2,1)S(1)}, u32[]{:S(2)}, u32[]{:S(2)}) collective-permute-start(bf16[656,128]{1,0:T(8,128)(2,1)S(1)} %get-tuple-element.96), channel_id=1, source_target_pairs={{0,16},{4,20},{8,24},{12,28},{16,0},{20,4},{24,8},{28,12},{1,17},{... | collective-permute-start | bytes 503816 | tf_op jit(solution)/shard_map/ppermute | solution.py:961
  233.6 2.9 copy-start.17
  233.6 26.6 %collective-permute-start.13 = (bf16[656,128]{1,0:T(8,128)(2,1)}, bf16[656,128]{1,0:T(8,128)(2,1)}, u32[]{:S(2)}, u32[]{:S(2)}) collective-permute-start(bf16[656,128]{1,0:T(8,128)(2,1)} %get-tuple-element.95), channel_id=1, source_target_pairs={{0,24},{4,28},{8,16},{12,20},{16,8},{20,12},{24,0},{28,4},{1,25},{... | collective-permute-start | bytes 503816 | tf_op jit(solution)/shard_map/ppermute | solution.py:961
  236.0 25.5 %collective-permute-start.7 = (bf16[128,1024]{1,0:T(8,128)(2,1)}, bf16[128,1024]{1,0:T(8,128)(2,1)}, u32[]{:S(2)}, u32[]{:S(2)}) collective-permute-start(bf16[128,1024]{1,0:T(8,128)(2,1)} %get-tuple-element.89), channel_id=1, source_target_pairs={{0,1},{1,0},{2,3},{3,2},{4,5},{5,4},{6,7},{7,6},{8,9},{9,8},{10,11... | collective-permute-start | bytes 786440 | tf_op jit(solution)/shard_map/ppermute | solution.py:792
  239.2 7.1 %copy-start.28 = (bf16[656,128]{1,0:T(8,128)(2,1)}, bf16[656,128]{1,0:T(8,128)(2,1)S(1)}, u32[]{:S(2)}) copy-start(bf16[656,128]{1,0:T(8,128)(2,1)S(1)} %collective-permute-done.11) | copy-start | bytes 503812
  239.2 22.4 %collective-permute-start.8 = (bf16[128,1024]{1,0:T(8,128)(2,1)}, bf16[128,1024]{1,0:T(8,128)(2,1)}, u32[]{:S(2)}, u32[]{:S(2)}) collective-permute-start(bf16[128,1024]{1,0:T(8,128)(2,1)} %get-tuple-element.91), channel_id=1, source_target_pairs={{0,2},{1,3},{2,0},{3,1},{4,6},{5,7},{6,4},{7,5},{8,10},{9,11},{10,... | collective-permute-start | bytes 786440 | tf_op jit(solution)/shard_map/ppermute | solution.py:792
  245.5 0.8 copy-start.29
  245.5 16.1 %collective-permute-start.9 = (bf16[128,1024]{1,0:T(8,128)(2,1)}, bf16[128,1024]{1,0:T(8,128)(2,1)}, u32[]{:S(2)}, u32[]{:S(2)}) collective-permute-start(bf16[128,1024]{1,0:T(8,128)(2,1)} %get-tuple-element.90), channel_id=1, source_target_pairs={{0,3},{1,2},{2,1},{3,0},{4,7},{5,6},{6,5},{7,4},{8,11},{9,10},{10,... | collective-permute-start | bytes 786440 | tf_op jit(solution)/shard_map/ppermute | solution.py:792
  263.6 4.9 copy-start.25
  266.2 9.0 %slice-start = ((s8[8388608]{0:T(1024)(128)(4,1)}), s8[4194304]{0:T(1024)(128)(4,1)S(1)}, s32[]{:S(2)}) async-start(s8[8388608]{0:T(1024)(128)(4,1)} %bitcast.285), calls=%async_computation | async-start | bytes 8388608
  268.6 6.6 %slice-start.1 = ((s8[8388608]{0:T(1024)(128)(4,1)}), s8[4194304]{0:T(1024)(128)(4,1)S(1)}, s32[]{:S(2)}) async-start(s8[8388608]{0:T(1024)(128)(4,1)} %bitcast.285), calls=%async_computation.1 | async-start | bytes 8388608
  268.6 6.6 %copy-start.7 = (pred[1024,1024]{0,1:T(8,128)(4,1)S(1)}, pred[1024,1024]{0,1:T(8,128)(4,1)}, u32[]{:S(2)}) copy-start(pred[1024,1024]{0,1:T(8,128)(4,1)} %copy-done.6) | copy-start | bytes 3145732
  268.6 6.6 %copy-start.13 = (bf16[1024,3,2,64]{0,3,2,1:T(8,128)(2,1)S(1)}, bf16[1024,3,2,64]{0,3,2,1:T(8,128)(2,1)}, u32[]{:S(2)}) copy-start(bf16[1024,3,2,64]{0,3,2,1:T(8,128)(2,1)} %copy-done.12) | copy-start | bytes 2359300
  278.7 1.4 copy-start.11
  281.0 3.7 copy-start.20
  281.2 15.1 %collective-permute-start.14 = (bf16[128,1312]{1,0:T(8,128)(2,1)S(1)}, bf16[128,1312]{1,0:T(8,128)(2,1)S(1)}, u32[]{:S(2)}, u32[]{:S(2)}) collective-permute-start(bf16[128,1312]{1,0:T(8,128)(2,1)S(1)} %get-tuple-element.86), channel_id=1, source_target_pairs={{0,8},{4,12},{8,0},{12,4},{16,24},{20,28},{24,16},{28,20},{1,9},{5... | collective-permute-start | bytes 1007624 | tf_op jit(solution)/shard_map/ppermute | solution.py:961
  281.2 25.8 %collective-permute-start.15 = (bf16[128,1312]{1,0:T(8,128)(2,1)S(1)}, bf16[128,1312]{1,0:T(8,128)(2,1)S(1)}, u32[]{:S(2)}, u32[]{:S(2)}) collective-permute-start(bf16[128,1312]{1,0:T(8,128)(2,1)S(1)} %get-tuple-element.88), channel_id=1, source_target_pairs={{0,16},{4,20},{8,24},{12,28},{16,0},{20,4},{24,8},{28,12},{1,17},{... | collective-permute-start | bytes 1007624 | tf_op jit(solution)/shard_map/ppermute | solution.py:961
  282.9 33.6 %collective-permute-start.16 = (bf16[128,1312]{1,0:T(8,128)(2,1)S(1)}, bf16[128,1312]{1,0:T(8,128)(2,1)S(1)}, u32[]{:S(2)}, u32[]{:S(2)}) collective-permute-start(bf16[128,1312]{1,0:T(8,128)(2,1)S(1)} %get-tuple-element.87), channel_id=1, source_target_pairs={{0,24},{4,28},{8,16},{12,20},{16,8},{20,12},{24,0},{28,4},{1,25},{... | collective-permute-start | bytes 1007624 | tf_op jit(solution)/shard_map/ppermute | solution.py:961
  340.9 1.6 copy-start.31
  343.5 10.5 %copy-start.18 = (bf16[1024,4,128]{2,0,1:T(8,128)(2,1)S(1)}, bf16[1024,4,128]{2,0,1:T(8,128)(2,1)}, u32[]{:S(2)}) copy-start(bf16[1024,4,128]{2,0,1:T(8,128)(2,1)} %copy.222) | copy-start | bytes 3145732
  355.2 123.5 %copy-start.14 = (f32[128,1024]{1,0:T(8,128)S(1)}, f32[128,1024]{1,0:T(8,128)}, u32[]{:S(2)}) copy-start(f32[128,1024]{1,0:T(8,128)} %get-tuple-element.69) | copy-start | bytes 1572868
  479.8 1.8 copy-start.1
